TPU v7x, 32 devices: a whole 2x2x4 slice. The times are simulated.
32 devices in a mesh: groups: 2 (over x), wide: 16 (over z, y, core).
Axes of the slice: x: 2, y: 2, z: 4, core: 2. Of those that a mesh axis runs over, the one named last changes fastest.
Arguments:
- tile_values: bfloat16 [256, 512, 512], P(('groups', 'wide')), parts along dimension 0, may hold values from -1.5 to 1.5
- tile_cols: int32 [32, 8], P(('groups', 'wide')), parts along dimension 0, may hold values from 0 to 15, as said below
- tile_counts: int32 [32], P(('groups', 'wide')), parts along dimension 0, may hold values from 2 to 8, as said below
Outputs:
- product_band: bfloat16 [32, 10, 512, 512], P(('groups', 'wide')), parts along dimension 0
There are 2 independent parts, one for each index of `groups`. A program takes and returns all parts, laid end to end along the dimension named above; each array names one. Nothing has to cross between parts.
Inputs may be any that keep to these rules, and one draw needn't show every extreme that they name: `tile_cols`: in every tile row i, slot 0 holds column i and slot 1 holds column (i + 1) mod 16; the columns of one row are distinct and lie within 4 tiles of i, counted around the loop of 16 tile columns. `tile_counts`: some tile row holds 8 tiles, some holds 2.
All inputs are finite; a program needn't handle non-finite values.
Results may differ from a plain program's by a relative error of at most 0.001.
Values may be sent and summed in bfloat16 or wider, within the bound.
No kernel may reach another device: no remote copies, remote signals or barrier semaphores. Data moves between devices by JAX's collectives and lax.ppermute only.
A program may use at most 128 MiB of HBM per device.

v0:
```python
import jax
import jax.numpy as jnp
from jax import lax
from jax.sharding import PartitionSpec as P

W = 4


def passed_along(value, axis, by):
    size = lax.axis_size(axis)
    return lax.ppermute(value, axis, [(i, (i + by) % size) for i in range(size)])


def live_tiles(values, counts):
    slots = values.shape[0]
    live = jnp.arange(slots, dtype=jnp.int32) < counts[0]
    return jnp.where(live[:, None, None], values, jnp.zeros((), values.dtype))


def tile_products(left, right):
    return jnp.einsum("ij,sjk->sik", left, right, preferred_element_type=jnp.float32)


def place_tiles(targets, products, width):
    positions = jnp.arange(width, dtype=jnp.int32)
    selector = (targets[None, :] == positions[:, None]).astype(jnp.float32)
    return jnp.einsum("ks,sij->kij", selector, products, precision=lax.Precision.HIGHEST)


def per_device(tile_values, tile_cols, tile_counts):
    total = lax.axis_size("wide")
    here = lax.axis_index("wide")
    width = 2 * W + 2
    masked = live_tiles(tile_values, tile_counts)
    first = tile_products(masked[0], masked)
    band = place_tiles((tile_cols[0] - here + W) % total, first, width)
    recv_values, recv_cols, recv_counts = passed_along(
        (tile_values, tile_cols, tile_counts), "wide", -1
    )
    recv_masked = live_tiles(recv_values, recv_counts)
    second = tile_products(masked[1], recv_masked)
    band = band + place_tiles((recv_cols[0] - here + W) % total, second, width)
    return band.astype(jnp.bfloat16)[None]


def solution(mesh):
    placed = (P(("groups", "wide"), None, None), P(("groups", "wide"), None), P(("groups", "wide")))
    return jax.shard_map(
        per_device,
        mesh=mesh,
        in_specs=placed,
        out_specs=P(("groups", "wide"), None, None, None),
        check_vma=False,
    )
```

profile of v0, /device:TPU:0, one launch (start us, length us, event | category | flops | bytes accessed | tf_op | source)
XLA Modules:
  0.0 88.8 jit_solution(3229662737136548513)
XLA Ops:
  0.0 5.4 %collective-permute-start.2 = (bf16[8,512,512]{2,1,0:T(8,128)(2,1)}, bf16[8,512,512]{2,1,0:T(8,128)(2,1)}, u32[]{:S(2)}, u32[]{:S(2)}) collective-permute-start(bf16[8,512,512]{2,1,0:T(8,128)(2,1)} %param.3), channel_id=1, source_target_pairs={{0,15},{1,0},{2,1},{3,2},{4,3},{5,4},{6,5},{7,6},{8,7},{9,8},{10,9... | collective-permute-start | bytes 12582920 | tf_op jit(solution)/shard_map/ppermute | solution.py:11
  5.4 0.7 collective-permute-start
  6.1 0.0 collective-permute-start.1
  6.9 2.5 %broadcast_select_fusion = bf16[8,512,512]{2,1,0:T(8,128)(2,1)S(1)} fusion(bf16[8,512,512]{2,1,0:T(8,128)(2,1)} %param.3, pred[8]{0:T(512)(128)(4,1)S(1)} %iota_compare_fusion.3), kind=kLoop, calls=%fused_computation.8 | loop fusion | flops 2097152 | bytes 8388616 | tf_op jit(solution)/shard_map/jit(_where)/select_n | solution.py:17
  9.4 0.0 copy-start
  9.4 2.0 %copy-done = bf16[8,512,512]{2,1,0:T(8,128)(2,1)} copy-done((bf16[8,512,512]{2,1,0:T(8,128)(2,1)}, bf16[8,512,512]{2,1,0:T(8,128)(2,1)S(1)}, u32[]{:S(2)}) %copy-start) | copy-done | bytes 4194328
  11.4 5.6 %fusion.10 = f32[8,512,512]{2,1,0:T(8,128)} fusion(bf16[8,512,512]{2,1,0:T(8,128)(2,1)S(1)} %broadcast_select_fusion), kind=kOutput, calls=%fused_computation.12 | convolution fusion | flops 2147483648 | bytes 13107200 | tf_op jit(solution)/shard_map/ij,sjk->sik/dot_general | solution.py:21
  17.0 0.0 copy-start.1
  17.0 10.4 %copy.5 = f32[8,512,512]{1,0,2:T(8,128)} copy(f32[8,512,512]{2,1,0:T(8,128)} %fusion.10) | data formatting | bytes 16777216 | tf_op jit(solution)/shard_map/ij,sjk->sik/dot_general | solution.py:21
  27.5 0.0 copy-done.1
  27.5 12.8 %fusion.1 = f32[10,512,512]{2,0,1:T(8,128)} fusion(f32[8,512,512]{1,0,2:T(8,128)} %copy.5, s32[8]{0:T(128)S(1)} %fusion.17), kind=kOutput, calls=%fused_computation.2 | convolution fusion | flops 251658320 | bytes 18874400 | tf_op jit(solution)/shard_map/ks,sij->kij/dot_general | solution.py:27
  40.3 11.5 %collective-permute-done.1 = s32[1]{0:T(128)} collective-permute-done((s32[1]{0:T(128)}, s32[1]{0:T(128)}, u32[]{:S(2)}, u32[]{:S(2)}) %collective-permute-start.1) | collective-permute-done | bytes 36 | tf_op jit(solution)/shard_map/ppermute | solution.py:11
  51.8 0.6 iota_compare_fusion.2
  52.4 0.0 collective-permute-done
  52.4 0.0 collective-permute-done.2
  52.5 8.4 %fusion.6 = f32[8,512,512]{2,1,0:T(8,128)} fusion(bf16[8,512,512]{2,1,0:T(8,128)(2,1)} %collective-permute-done.2, pred[8]{0:T(512)(128)(4,1)S(1)} %iota_compare_fusion.2, bf16[8,512,512]{2,1,0:T(8,128)(2,1)} %copy-done), kind=kOutput, calls=%fused_computation.5 | convolution fusion | flops 2149580800 | bytes 13107208 | tf_op jit(solution)/shard_map/ij,sjk->sik/dot_general | solution.py:21
  60.9 10.4 %copy.6 = f32[8,512,512]{1,0,2:T(8,128)} copy(f32[8,512,512]{2,1,0:T(8,128)} %fusion.6) | data formatting | bytes 16777216 | tf_op jit(solution)/shard_map/ij,sjk->sik/dot_general | solution.py:21
  71.3 12.2 %fusion.3 = bf16[1,10,512,512]{3,1,2,0:T(8,128)(2,1)S(1)} fusion(f32[10,512,512]{2,0,1:T(8,128)} %fusion.1, f32[8,512,512]{1,0,2:T(8,128)} %copy.6, s32[8]{0:T(128)S(1)} %fusion.18), kind=kOutput, calls=%fused_computation.4 | convolution fusion | flops 256901200 | bytes 24117280 | tf_op jit(solution)/shard_map/ks,sij->kij/dot_general | solution.py:27
  83.4 5.4 %copy.4 = bf16[1,10,512,512]{3,2,1,0:T(8,128)(2,1)} copy(bf16[1,10,512,512]{3,1,2,0:T(8,128)(2,1)S(1)} %fusion.3) | data formatting | bytes 10485760 | tf_op jit(solution)/shard_map/broadcast_in_dim | solution.py:43
  (3 shorter events, 0.0 us)
Async XLA Ops:
  0.0 52.4 %collective-permute-start.2 = (bf16[8,512,512]{2,1,0:T(8,128)(2,1)}, bf16[8,512,512]{2,1,0:T(8,128)(2,1)}, u32[]{:S(2)}, u32[]{:S(2)}) collective-permute-start(bf16[8,512,512]{2,1,0:T(8,128)(2,1)} %param.3), channel_id=1, source_target_pairs={{0,15},{1,0},{2,1},{3,2},{4,3},{5,4},{6,5},{7,6},{8,7},{9,8},{10,9... | collective-permute-start | bytes 12582920 | tf_op jit(solution)/shard_map/ppermute | solution.py:11
  5.4 47.0 %collective-permute-start = (s32[1,8]{1,0:T(1,128)}, s32[1,8]{1,0:T(1,128)S(1)}, u32[]{:S(2)}, u32[]{:S(2)}) collective-permute-start(s32[1,8]{1,0:T(1,128)} %param.4), channel_id=1, source_target_pairs={{0,15},{1,0},{2,1},{3,2},{4,3},{5,4},{6,5},{7,6},{8,7},{9,8},{10,9... | collective-permute-start | bytes 104 | tf_op jit(solution)/shard_map/ppermute | solution.py:11
  6.1 45.7 %collective-permute-start.1 = (s32[1]{0:T(128)}, s32[1]{0:T(128)}, u32[]{:S(2)}, u32[]{:S(2)}) collective-permute-start(s32[1]{0:T(128)} %param.5), channel_id=1, source_target_pairs={{0,15},{1,0},{2,1},{3,2},{4,3},{5,4},{6,5},{7,6},{8,7},{9,8},{10,9... | collective-permute-start | bytes 20 | tf_op jit(solution)/shard_map/ppermute | solution.py:11
  9.4 2.0 %copy-start = (bf16[8,512,512]{2,1,0:T(8,128)(2,1)}, bf16[8,512,512]{2,1,0:T(8,128)(2,1)S(1)}, u32[]{:S(2)}) copy-start(bf16[8,512,512]{2,1,0:T(8,128)(2,1)S(1)} %broadcast_select_fusion) | copy-start | bytes 12582916
  17.0 10.5 %copy-start.1 = (s32[1,8]{1,0:T(1,128)S(1)}, s32[1,8]{1,0:T(1,128)}, u32[]{:S(2)}) copy-start(s32[1,8]{1,0:T(1,128)} %param.4) | copy-start | bytes 100
where the time goes:
time: 89.4 us; the launch traced here: 88.8 us
  matrix products  39 us (44%)
  local copies, waits for them, and re-layouts  28.2 us (32%)
  waiting for transfers between devices  11.5 us (13%)
  starting transfers between devices  6.15 us (7%)
  other arithmetic  3.18 us (4%)
    dot_general x2, matrix products, place_tiles(): jnp.einsum('ks,sij->kij', selector, products, precision=lax.Precision.HIG...  25 us
    dot_general x2, local copies, waits for them, and re-layouts, tile_products(): jnp.einsum('ij,sjk->sik', left, right, preferred_element_type=jnp.float32)  20.8 us
    dot_general x2, matrix products, tile_products(): jnp.einsum('ij,sjk->sik', left, right, preferred_element_type=jnp.float32)  14 us
    ppermute x3, waiting for transfers between devices, passed_along(): lax.ppermute(value, axis, [(i, (i + by) % size) for i in range(size)])  11.5 us
    ppermute x3, starting transfers between devices, passed_along(): lax.ppermute(value, axis, [(i, (i + by) % size) for i in range(size)])  6.15 us
    broadcast_in_dim x1, local copies, waits for them, and re-layouts, per_device(): return band.astype(jnp.bfloat16)[None]  5.38 us
    select_n x1, other arithmetic, live_tiles(): return jnp.where(live[:, None, None], values, jnp.zeros((), values.dtype))  2.53 us
    unnamed x4, local copies, waits for them, and re-layouts  2.01 us
  transfers between devices with their start and end apart: 3, of which 1 were waited for; matrix products, arithmetic and copies ran while one was open for 36% of the time, Pallas kernels for 0%

commit v1 on v0

v1 whole, which is shorter than its diff:
```python
import functools

import jax
import jax.numpy as jnp
from jax import lax
from jax.experimental import pallas as pl
from jax.experimental.pallas import tpu as pltpu
from jax.sharding import PartitionSpec as P

W = 4
WIDTH = 2 * W + 2
META_ROWS = 16
HEAD = ((0, 1),)
LATER = ((1, 3), (3, 5), (5, 7), (7, 8))
ANY = pl.BlockSpec(memory_space=pl.ANY)
HBM = pl.BlockSpec(memory_space=pltpu.HBM)
SMEM = pl.BlockSpec(memory_space=pltpu.SMEM)
VMEM = pl.BlockSpec(memory_space=pltpu.VMEM)


def find(cols_ref, counts_ref, col):
    found = jnp.int32(-1)
    for s in range(cols_ref.shape[1]):
        found = jnp.where((cols_ref[0, s] == col) & (s < counts_ref[0]), s, found)
    return found


def dot(a, b):
    return jnp.dot(a, b, preferred_element_type=jnp.float32)


def finish(own, f, right, out_v, t):
    @pl.when(f >= 0)
    def _():
        acc = dot(own[0], own[f])
        if right is not None:
            acc = acc + dot(own[1], right())
        out_v[t] = acc.astype(out_v.dtype)

    @pl.when(f < 0)
    def _():
        if right is not None:
            out_v[t] = dot(own[1], right()).astype(out_v.dtype)
        else:
            out_v[t] = jnp.zeros(out_v.shape[1:], out_v.dtype)


def early_kernel(total, cols, counts, next_cols, next_counts, own, head, out, out_v, sems):
    here = cols[0, 0]

    def job(k):
        col = lax.rem(here + k - W + total, total)
        return find(cols, counts, col), find(next_cols, next_counts, col)

    def out_copy(k):
        return pltpu.make_async_copy(out_v.at[k], out.at[0, k], sems.at[k])

    @pl.loop(0, WIDTH)
    def _(k):
        f, s = job(k)

        @pl.when(s < 1)
        def _():
            @pl.when(s < 0)
            def _():
                finish(own, f, None, out_v, k)

            @pl.when(s == 0)
            def _():
                finish(own, f, lambda: head[: own.shape[1]], out_v, k)

            out_copy(k).start()

    @pl.loop(0, WIDTH)
    def _(k):
        _, s = job(k)

        @pl.when(s < 1)
        def _():
            out_copy(k).wait()


def chunk_kernel(first_slot, jobs, total, cols, counts, next_cols, next_counts, own, chunk, band, out, out_v, sems):
    here = cols[0, 0]
    rows = own.shape[1]

    def job(t):
        slot = first_slot + t
        col = next_cols[0, slot]
        return slot < next_counts[0], lax.rem(col - here + W + total, total), col

    def out_copy(t, k):
        return pltpu.make_async_copy(out_v.at[t], out.at[0, k], sems.at[t])

    @pl.loop(0, jobs)
    def _(t):
        active, k, col = job(t)

        @pl.when(active)
        def _():
            finish(own, find(cols, counts, col), lambda: chunk[pl.ds(pl.multiple_of(t * rows, rows), rows)], out_v, t)
            out_copy(t, k).start()

    @pl.loop(0, jobs)
    def _(t):
        active, k, _ = job(t)

        @pl.when(active)
        def _():
            out_copy(t, k).wait()


def call(kernel, jobs, operands, specs, aliases):
    own = operands[4]
    b = own.shape[1:]
    tile_bytes = b[0] * b[1] * 2
    return pl.pallas_call(
        kernel,
        out_shape=jax.ShapeDtypeStruct((1, WIDTH) + b, own.dtype),
        in_specs=specs,
        out_specs=ANY,
        input_output_aliases=aliases,
        scratch_shapes=[pltpu.VMEM((jobs,) + b, own.dtype), pltpu.SemaphoreType.DMA((jobs,))],
        compiler_params=pltpu.CompilerParams(vmem_limit_bytes=32 * 2**20),
        cost_estimate=pl.CostEstimate(
            flops=jobs * 4 * b[0] * b[0] * b[1],
            bytes_accessed=jobs * tile_bytes,
            transcendentals=0,
        ),
    )(*operands)


def pack_kernel(ranges, noted, *refs):
    cols, counts, own = refs[:3]
    parts, sems = refs[-1 - len(ranges) : -1], refs[-1]
    rows, lanes = own.shape[1:]
    copies = []
    for (a, b), part in zip(ranges, parts):
        for s in range(a, b):
            copies.append(pltpu.make_async_copy(own.at[s], part.at[pl.ds((s - a) * rows, rows)], sems.at[s]))
    for copy in copies:
        copy.start()
    if noted:
        lane = lax.broadcasted_iota(jnp.int32, (META_ROWS, lanes), 1)
        note = jnp.zeros((META_ROWS, lanes), jnp.int32)
        slots = cols.shape[1]
        for s in range(slots):
            note = jnp.where(lane == s, cols[0, s], note)
        note = jnp.where(lane == slots, counts[0], note)
        start = (ranges[0][1] - ranges[0][0]) * rows
        parts[0][pl.ds(start, META_ROWS)] = note.astype(jnp.float32).astype(parts[0].dtype)
    for copy in copies:
        copy.wait()


def pack(ranges, noted, cols, counts, own, *after):
    slots, rows, lanes = own.shape
    sizes = [(b - a) * rows for a, b in ranges]
    if noted:
        sizes[0] += META_ROWS
    return pl.pallas_call(
        functools.partial(pack_kernel, ranges, noted),
        out_shape=[jax.ShapeDtypeStruct((size, lanes), own.dtype) for size in sizes],
        in_specs=[SMEM] * 2 + [HBM] + [ANY] * len(after),
        out_specs=[VMEM] * len(sizes),
        scratch_shapes=[pltpu.SemaphoreType.DMA((slots,))],
        compiler_params=pltpu.CompilerParams(vmem_limit_bytes=32 * 2**20),
        cost_estimate=pl.CostEstimate(flops=0, bytes_accessed=8 * sum(sizes) * lanes, transcendentals=0),
    )(cols, counts, pltpu.with_memory_space_constraint(own, pltpu.HBM), *after)


def per_device(tile_values, tile_cols, tile_counts):
    total = lax.axis_size("wide")
    slots, rows, _ = tile_values.shape
    pairs = [(i, (i - 1) % total) for i in range(total)]
    send = lambda value: lax.ppermute(value, "wide", pairs)

    (first,) = pack(HEAD, True, tile_cols, tile_counts, tile_values)
    head = send(first)
    chunks = [send(part) for part in pack(LATER, False, tile_cols, tile_counts, tile_values, first)]

    got = head[rows, : slots + 1].astype(jnp.int32)
    meta = (tile_cols, tile_counts, got[None, :slots], got[slots:])
    band = call(
        functools.partial(early_kernel, total), WIDTH,
        (*meta, tile_values, head), [SMEM] * 4 + [VMEM] * 2, {},
    )
    for (a, b), chunk in zip(LATER, chunks):
        band = call(
            functools.partial(chunk_kernel, a, b - a, total), b - a,
            (*meta, tile_values, chunk, band), [SMEM] * 4 + [VMEM] * 2 + [ANY], {6: 0},
        )
    return band


def solution(mesh):
    placed = (P(("groups", "wide"), None, None), P(("groups", "wide"), None), P(("groups", "wide")))
    return jax.shard_map(
        per_device,
        mesh=mesh,
        in_specs=placed,
        out_specs=P(("groups", "wide"), None, None, None),
        check_vma=False,
    )
```

time: 89.4 us -> 56.5 us (0.63)
  matrix products: 39 us -> 0 us
  local copies, waits for them, and re-layouts: 28.2 us -> 1.39 us
  waiting for transfers between devices: 11.5 us -> 31.6 us
  Pallas kernels: 0 us -> 14.5 us
  other arithmetic: 3.18 us -> 0.01 us
  starting transfers between devices: 6.15 us -> 7.69 us
    dot_general x4 -> x0, matrix products: 39 us -> none  [the longest x2 25 us: place_tiles(): jnp.einsum('ks,sij->kij', selector, products, precision=lax.Precision.HIG...]
    dot_general x2 -> x0, local copies, waits for them, and re-layouts: 20.8 us -> none  [tile_products(): jnp.einsum('ij,sjk->sik', left, right, preferred_element_type=jnp.float32)]
    ppermute x3 -> x5, waiting for transfers between devices: 11.5 us -> 31.6 us  [per_device(): send = lambda value: lax.ppermute(value, 'wide', pairs)]
    pallas_call x0 -> x7, Pallas kernels: none -> 14.5 us  [the longest x5 10.3 us: call(): pl.pallas_call(kernel, out_shape=jax.ShapeDtypeStruct((1, WIDTH) + b, own...]
    broadcast_in_dim x1 -> x0, local copies, waits for them, and re-layouts: 5.38 us -> none  [per_device(): return band.astype(jnp.bfloat16)[None]]
    select_n x1 -> x0, other arithmetic: 2.53 us -> none  [live_tiles(): return jnp.where(live[:, None, None], values, jnp.zeros((), values.dtype))]
    ppermute x3 -> x5, starting transfers between devices: 6.15 us -> 7.69 us  [per_device(): send = lambda value: lax.ppermute(value, 'wide', pairs)]
    unnamed x4, local copies, waits for them, and re-layouts: 2.01 us -> 0.81 us
  transfers between devices with their start and end apart: 3 -> 5, of which waited for: 1 -> 5; matrix products, arithmetic and copies ran while one was open for 36% -> 1% of each run, Pallas kernels for 0% -> 21%
where the time goes in v1:
time: 56.5 us; the launch traced here: 56.1 us
  waiting for transfers between devices  31.6 us (56%)
  Pallas kernels  14.5 us (26%)
  starting transfers between devices  7.69 us (14%)
  local copies, waits for them, and re-layouts  1.39 us (2%)
  between operations  0.87 us (2%)
    ppermute x5, waiting for transfers between devices, per_device(): send = lambda value: lax.ppermute(value, 'wide', pairs)  31.6 us
    pallas_call x5, Pallas kernels, call(): pl.pallas_call(kernel, out_shape=jax.ShapeDtypeStruct((1, WIDTH) + b, own...  10.3 us
    ppermute x5, starting transfers between devices, per_device(): send = lambda value: lax.ppermute(value, 'wide', pairs)  7.69 us
    pallas_call x2, Pallas kernels, pack(): pl.pallas_call(functools.partial(pack_kernel, ranges, noted), out_shape=[...  4.25 us
  transfers between devices with their start and end apart: 5, of which 5 were waited for; matrix products, arithmetic and copies ran while one was open for 1% of the time, Pallas kernels for 21%

profile of v1, /device:TPU:0, one launch (start us, length us, event | category | flops | bytes accessed | tf_op | source)
XLA Modules:
  0.0 56.1 jit_solution(5718573740150329037)
XLA Ops:
  0.0 0.0 copy-start
  0.8 0.0 copy-start.1
  0.8 0.8 %copy-done.1 = s32[1,8]{1,0:T(1,128)S(1)} copy-done((s32[1,8]{1,0:T(1,128)S(1)}, s32[1,8]{1,0:T(1,128)}, u32[]{:S(2)}) %copy-start.1) | copy-done | bytes 56
  1.6 1.7 %shard_map.37.refs_3_ = bf16[528,512]{1,0:T(8,128)(2,1)S(1)} custom-call(s32[1,8]{1,0:T(1,128)S(1)} %copy-done.1, s32[1]{0:T(128)S(6)} %copy.12.refs_1_.counts, bf16[8,512,512]{2,1,0:T(8,128)(2,1)} %own.9), custom_call_target="tpu_custom_call" | custom-call | bytes 2162688 | tf_op jit(solution)/shard_map/pallas_call | solution.py:161
  3.3 5.5 %collective-permute-start = (bf16[528,512]{1,0:T(8,128)(2,1)S(1)}, bf16[528,512]{1,0:T(8,128)(2,1)S(1)}, u32[]{:S(2)}, u32[]{:S(2)}) collective-permute-start(bf16[528,512]{1,0:T(8,128)(2,1)S(1)} %shard_map.37.refs_3_), channel_id=1, source_target_pairs={{0,15},{1,0},{2,1},{3,2},{4,3},{5,4},{6,5},{7,6},{8,7},{9,8},{10,9... | collective-permute-start | bytes 1622024 | tf_op jit(solution)/shard_map/ppermute | solution.py:176
  8.8 2.6 %shard_map.38 = (bf16[1024,512]{1,0:T(8,128)(2,1)S(1)}, bf16[1024,512]{1,0:T(8,128)(2,1)S(1)}, bf16[1024,512]{1,0:T(8,128)(2,1)S(1)}, bf16[512,512]{1,0:T(8,128)(2,1)S(1)}) custom-call(s32[1,8]{1,0:T(1,128)S(1)} %copy-done.1, s32[1]{0:T(128)S(6)} %copy.12.refs_1_.counts, bf16[8,512,512]{2,1,0:T(8,128)(2,1)} %own.9, bf16[528,512]{1,0:T(8,128)(2,1)S(1)} %shard_map.37.refs_3_), custom_call_target="tpu_custom_call" | custom-call | bytes 14680064 | tf_op jit(solution)/shard_map/pallas_call | solution.py:161
  11.4 0.7 %collective-permute-start.4 = (bf16[1024,512]{1,0:T(8,128)(2,1)S(1)}, bf16[1024,512]{1,0:T(8,128)(2,1)S(1)}, u32[]{:S(2)}, u32[]{:S(2)}) collective-permute-start(bf16[1024,512]{1,0:T(8,128)(2,1)S(1)} %get-tuple-element.12), channel_id=1, source_target_pairs={{0,15},{1,0},{2,1},{3,2},{4,3},{5,4},{6,5},{7,6},{8,7},{9,8},{10,9... | collective-permute-start | bytes 3145736 | tf_op jit(solution)/shard_map/ppermute | solution.py:176
  12.1 0.1 collective-permute-start.3
  12.2 0.6 collective-permute-start.2
  12.7 0.8 %collective-permute-start.1 = (bf16[512,512]{1,0:T(8,128)(2,1)S(1)}, bf16[512,512]{1,0:T(8,128)(2,1)S(1)}, u32[]{:S(2)}, u32[]{:S(2)}) collective-permute-start(bf16[512,512]{1,0:T(8,128)(2,1)S(1)} %get-tuple-element.9), channel_id=1, source_target_pairs={{0,15},{1,0},{2,1},{3,2},{4,3},{5,4},{6,5},{7,6},{8,7},{9,8},{10,9... | collective-permute-start | bytes 1572872 | tf_op jit(solution)/shard_map/ppermute | solution.py:176
  13.6 2.1 %collective-permute-done.head = bf16[528,512]{1,0:T(8,128)(2,1)S(1)} collective-permute-done((bf16[528,512]{1,0:T(8,128)(2,1)S(1)}, bf16[528,512]{1,0:T(8,128)(2,1)S(1)}, u32[]{:S(2)}, u32[]{:S(2)}) %collective-permute-start) | collective-permute-done | bytes 540704 | tf_op jit(solution)/shard_map/ppermute | solution.py:176
  15.7 0.6 %slice.15 = s32[1,1]{1,0:T(1,128)} slice(s32[1,9]{1,0:T(1,128)S(1)} %slice_convert_fusion), slice={[0:1], [8:9]} | slice | bytes 8 | tf_op jit(solution)/shard_map/slice | solution.py:183
  16.2 0.0 copy-done
  16.2 4.5 %shard_map.39.band = bf16[1,10,512,512]{3,2,1,0:T(8,128)(2,1)} custom-call(s32[1,8]{1,0:T(1,128)S(1)} %copy-done.1, s32[1]{0:T(128)S(6)} %copy.12.refs_1_.counts, s32[1,8]{1,0:T(1,128)S(1)} %bitcast.2, s32[1]{0:T(128)} %bitcast.next_counts, bf16[8,512,512]{2,1,0:T(8,128)(2,1)S(1)} %copy-done, bf16[528,512]{1,0:T(8,128)(2,1)S(1)} %collective-permute-done.head), custom_call_target="tpu_custom_call" | custom-call | flops 5368709120 | bytes 5242880 | tf_op jit(solution)/shard_map/pallas_call | solution.py:117
  20.7 6.2 %collective-permute-done.4.chunk = bf16[1024,512]{1,0:T(8,128)(2,1)S(1)} collective-permute-done((bf16[1024,512]{1,0:T(8,128)(2,1)S(1)}, bf16[1024,512]{1,0:T(8,128)(2,1)S(1)}, u32[]{:S(2)}, u32[]{:S(2)}) %collective-permute-start.4) | collective-permute-done | bytes 1048608 | tf_op jit(solution)/shard_map/ppermute | solution.py:176
  26.9 2.4 %shard_map.40.band = bf16[1,10,512,512]{3,2,1,0:T(8,128)(2,1)} custom-call(s32[1,8]{1,0:T(1,128)S(1)} %copy-done.1, s32[1]{0:T(128)S(6)} %copy.12.refs_1_.counts, s32[1,8]{1,0:T(1,128)S(1)} %bitcast.3, s32[1]{0:T(128)} %bitcast.next_counts, bf16[8,512,512]{2,1,0:T(8,128)(2,1)S(1)} %copy-done, ...), custom_call_target="tpu_custom_call", output_to_operand_aliasing={{}: (6, {})} | custom-call | flops 1073741824 | bytes 1048576 | tf_op jit(solution)/shard_map/pallas_call | solution.py:117
  29.3 8.8 %collective-permute-done.3.chunk = bf16[1024,512]{1,0:T(8,128)(2,1)S(1)} collective-permute-done((bf16[1024,512]{1,0:T(8,128)(2,1)S(1)}, bf16[1024,512]{1,0:T(8,128)(2,1)S(1)}, u32[]{:S(2)}, u32[]{:S(2)}) %collective-permute-start.3) | collective-permute-done | bytes 1048608 | tf_op jit(solution)/shard_map/ppermute | solution.py:176
  38.1 1.2 %shard_map.41.band = bf16[1,10,512,512]{3,2,1,0:T(8,128)(2,1)} custom-call(s32[1,8]{1,0:T(1,128)S(1)} %copy-done.1, s32[1]{0:T(128)S(6)} %copy.12.refs_1_.counts, s32[1,8]{1,0:T(1,128)S(1)} %bitcast.4, s32[1]{0:T(128)} %bitcast.next_counts, bf16[8,512,512]{2,1,0:T(8,128)(2,1)S(1)} %copy-done, ...), custom_call_target="tpu_custom_call", output_to_operand_aliasing={{}: (6, {})} | custom-call | flops 1073741824 | bytes 1048576 | tf_op jit(solution)/shard_map/pallas_call | solution.py:117
  39.3 10.1 %collective-permute-done.2.chunk = bf16[1024,512]{1,0:T(8,128)(2,1)S(1)} collective-permute-done((bf16[1024,512]{1,0:T(8,128)(2,1)S(1)}, bf16[1024,512]{1,0:T(8,128)(2,1)S(1)}, u32[]{:S(2)}, u32[]{:S(2)}) %collective-permute-start.2) | collective-permute-done | bytes 1048608 | tf_op jit(solution)/shard_map/ppermute | solution.py:176
  49.4 1.2 %shard_map.42.band = bf16[1,10,512,512]{3,2,1,0:T(8,128)(2,1)} custom-call(s32[1,8]{1,0:T(1,128)S(1)} %copy-done.1, s32[1]{0:T(128)S(6)} %copy.12.refs_1_.counts, s32[1,8]{1,0:T(1,128)S(1)} %bitcast.5, s32[1]{0:T(128)} %bitcast.next_counts, bf16[8,512,512]{2,1,0:T(8,128)(2,1)S(1)} %copy-done, ...), custom_call_target="tpu_custom_call", output_to_operand_aliasing={{}: (6, {})} | custom-call | flops 1073741824 | bytes 1048576 | tf_op jit(solution)/shard_map/pallas_call | solution.py:117
  50.5 4.4 %collective-permute-done.1.chunk = bf16[512,512]{1,0:T(8,128)(2,1)S(1)} collective-permute-done((bf16[512,512]{1,0:T(8,128)(2,1)S(1)}, bf16[512,512]{1,0:T(8,128)(2,1)S(1)}, u32[]{:S(2)}, u32[]{:S(2)}) %collective-permute-start.1) | collective-permute-done | bytes 524320 | tf_op jit(solution)/shard_map/ppermute | solution.py:176
  55.0 1.1 %shard_map.43 = bf16[1,10,512,512]{3,2,1,0:T(8,128)(2,1)} custom-call(s32[1,8]{1,0:T(1,128)S(1)} %copy-done.1, s32[1]{0:T(128)S(6)} %copy.12.refs_1_.counts, s32[1,8]{1,0:T(1,128)S(1)} %bitcast.6, s32[1]{0:T(128)} %bitcast.next_counts, bf16[8,512,512]{2,1,0:T(8,128)(2,1)S(1)} %copy-done, ...), custom_call_target="tpu_custom_call", output_to_operand_aliasing={{}: (6, {})} | custom-call | flops 536870912 | bytes 524288 | tf_op jit(solution)/shard_map/pallas_call | solution.py:117
  (1 shorter events, 0.0 us)
Async XLA Ops:
  0.0 16.2 %copy-start = (bf16[8,512,512]{2,1,0:T(8,128)(2,1)S(1)}, bf16[8,512,512]{2,1,0:T(8,128)(2,1)}, u32[]{:S(2)}) copy-start(bf16[8,512,512]{2,1,0:T(8,128)(2,1)} %own.9) | copy-start | bytes 12582916
  0.8 0.8 %copy-start.1 = (s32[1,8]{1,0:T(1,128)S(1)}, s32[1,8]{1,0:T(1,128)}, u32[]{:S(2)}) copy-start(s32[1,8]{1,0:T(1,128)} %cols.9) | copy-start | bytes 100
  3.3 12.4 %collective-permute-start = (bf16[528,512]{1,0:T(8,128)(2,1)S(1)}, bf16[528,512]{1,0:T(8,128)(2,1)S(1)}, u32[]{:S(2)}, u32[]{:S(2)}) collective-permute-start(bf16[528,512]{1,0:T(8,128)(2,1)S(1)} %shard_map.37.refs_3_), channel_id=1, source_target_pairs={{0,15},{1,0},{2,1},{3,2},{4,3},{5,4},{6,5},{7,6},{8,7},{9,8},{10,9... | collective-permute-start | bytes 1622024 | tf_op jit(solution)/shard_map/ppermute | solution.py:176
  11.4 15.5 %collective-permute-start.4 = (bf16[1024,512]{1,0:T(8,128)(2,1)S(1)}, bf16[1024,512]{1,0:T(8,128)(2,1)S(1)}, u32[]{:S(2)}, u32[]{:S(2)}) collective-permute-start(bf16[1024,512]{1,0:T(8,128)(2,1)S(1)} %get-tuple-element.12), channel_id=1, source_target_pairs={{0,15},{1,0},{2,1},{3,2},{4,3},{5,4},{6,5},{7,6},{8,7},{9,8},{10,9... | collective-permute-start | bytes 3145736 | tf_op jit(solution)/shard_map/ppermute | solution.py:176
  12.1 26.0 %collective-permute-start.3 = (bf16[1024,512]{1,0:T(8,128)(2,1)S(1)}, bf16[1024,512]{1,0:T(8,128)(2,1)S(1)}, u32[]{:S(2)}, u32[]{:S(2)}) collective-permute-start(bf16[1024,512]{1,0:T(8,128)(2,1)S(1)} %get-tuple-element.11), channel_id=1, source_target_pairs={{0,15},{1,0},{2,1},{3,2},{4,3},{5,4},{6,5},{7,6},{8,7},{9,8},{10,9... | collective-permute-start | bytes 3145736 | tf_op jit(solution)/shard_map/ppermute | solution.py:176
  12.2 37.2 %collective-permute-start.2 = (bf16[1024,512]{1,0:T(8,128)(2,1)S(1)}, bf16[1024,512]{1,0:T(8,128)(2,1)S(1)}, u32[]{:S(2)}, u32[]{:S(2)}) collective-permute-start(bf16[1024,512]{1,0:T(8,128)(2,1)S(1)} %get-tuple-element.10), channel_id=1, source_target_pairs={{0,15},{1,0},{2,1},{3,2},{4,3},{5,4},{6,5},{7,6},{8,7},{9,8},{10,9... | collective-permute-start | bytes 3145736 | tf_op jit(solution)/shard_map/ppermute | solution.py:176
  12.7 42.2 %collective-permute-start.1 = (bf16[512,512]{1,0:T(8,128)(2,1)S(1)}, bf16[512,512]{1,0:T(8,128)(2,1)S(1)}, u32[]{:S(2)}, u32[]{:S(2)}) collective-permute-start(bf16[512,512]{1,0:T(8,128)(2,1)S(1)} %get-tuple-element.9), channel_id=1, source_target_pairs={{0,15},{1,0},{2,1},{3,2},{4,3},{5,4},{6,5},{7,6},{8,7},{9,8},{10,9... | collective-permute-start | bytes 1572872 | tf_op jit(solution)/shard_map/ppermute | solution.py:176

commit v2 on v1

v2 whole, which is shorter than its diff:
```python
import functools

import jax
import jax.numpy as jnp
from jax import lax
from jax.experimental import pallas as pl
from jax.experimental.pallas import tpu as pltpu
from jax.sharding import PartitionSpec as P

W = 4
WIDTH = 2 * W + 2
META_ROWS = 16
LAST = 7
LATER = ((1, 2), (2, 5), (5, LAST), (LAST, LAST + 1))
ANY = pl.BlockSpec(memory_space=pl.ANY)
HBM = pl.BlockSpec(memory_space=pltpu.HBM)
SMEM = pl.BlockSpec(memory_space=pltpu.SMEM)
VMEM = pl.BlockSpec(memory_space=pltpu.VMEM)


def find(cols_ref, counts_ref, col):
    found = jnp.int32(-1)
    for s in range(cols_ref.shape[1]):
        found = jnp.where((cols_ref[0, s] == col) & (s < counts_ref[0]), s, found)
    return found


def dot(a, b):
    return jnp.dot(a, b, preferred_element_type=jnp.float32)


def head_kernel(own, head, out, out_v, sem):
    out_v[...] = (dot(own[0], own[1]) + dot(own[1], head[...])).astype(out_v.dtype)
    copy = pltpu.make_async_copy(out_v, out.at[0, W + 1], sem)
    copy.start()
    copy.wait()


def early_kernel(total, cols, counts, next_cols, next_counts, own, band, out, table, out_v, sems):
    here = cols[0, 0]
    for s in range(next_cols.shape[1]):
        col = next_cols[0, s]
        table[0, s] = jnp.where(s < next_counts[0], lax.rem(col - here + W + total, total), -1)
        table[1, s] = find(cols, counts, col)
    table[0, next_cols.shape[1]] = lax.rem(here, 2)

    def job(k):
        col = lax.rem(here + k - W + total, total)
        return find(cols, counts, col), find(next_cols, next_counts, col) < 0

    def out_copy(k):
        return pltpu.make_async_copy(out_v.at[k], out.at[0, k], sems.at[k])

    @pl.loop(0, WIDTH)
    def _(k):
        f, active = job(k)

        @pl.when(active)
        def _():
            @pl.when(f >= 0)
            def _():
                out_v[k] = dot(own[0], own[f]).astype(out_v.dtype)

            @pl.when(f < 0)
            def _():
                out_v[k] = jnp.zeros(out_v.shape[1:], out_v.dtype)

            out_copy(k).start()

    @pl.loop(0, WIDTH)
    def _(k):
        _, active = job(k)

        @pl.when(active)
        def _():
            out_copy(k).wait()


def finish(table, own, right, slot, out_v, t):
    f = table[1, slot]

    @pl.when(f >= 0)
    def _():
        out_v[t] = (dot(own[0], own[f]) + dot(own[1], right())).astype(out_v.dtype)

    @pl.when(f < 0)
    def _():
        out_v[t] = dot(own[1], right()).astype(out_v.dtype)


def chunk_kernel(first_slot, jobs, table, own, chunk, band, out, out_v, sems):
    rows = own.shape[1]

    def out_copy(t):
        return pltpu.make_async_copy(out_v.at[t], out.at[0, table[0, first_slot + t]], sems.at[t])

    @pl.loop(0, jobs)
    def _(t):
        @pl.when(table[0, first_slot + t] >= 0)
        def _():
            finish(table, own, lambda: chunk[pl.ds(pl.multiple_of(t * rows, rows), rows)], first_slot + t, out_v, t)
            out_copy(t).start()

    @pl.loop(0, jobs)
    def _(t):
        @pl.when(table[0, first_slot + t] >= 0)
        def _():
            out_copy(t).wait()


def late_kernel(first_slot, jobs, table, own, chunk, near, band, out, base, out_v, sems):
    chunk_kernel(first_slot, jobs, table, own, chunk, band, out, out_v, sems)

    @pl.when(table[0, LAST] >= 0)
    def _():
        even = table[0, LAST + 1] == 0

        @pl.when(even)
        def _():
            finish(table, own, lambda: near[...], LAST, out_v, jobs)
            copy = pltpu.make_async_copy(out_v.at[jobs], out.at[0, table[0, LAST]], sems.at[jobs])
            copy.start()
            copy.wait()

        f = table[1, LAST]

        @pl.when(jnp.logical_not(even) & (f >= 0))
        def _():
            base[...] = dot(own[0], own[f])

        @pl.when(jnp.logical_not(even) & (f < 0))
        def _():
            base[...] = jnp.zeros(base.shape, base.dtype)


def last_kernel(table, own, chunk, base, band, out, out_v, sem):
    @pl.when((table[0, LAST] >= 0) & (table[0, LAST + 1] == 1))
    def _():
        out_v[...] = (base[...] + dot(own[1], chunk[...])).astype(out_v.dtype)
        copy = pltpu.make_async_copy(out_v, out.at[0, table[0, LAST]], sem)
        copy.start()
        copy.wait()


def pack_kernel(ranges, noted, *refs):
    cols, counts, own, _ = refs[:4]
    parts, sems = refs[4:-1], refs[-1]
    rows, lanes = own.shape[1:]
    copies = []
    for (a, b), part in zip(ranges, parts):
        for s in range(a, b):
            copies.append(pltpu.make_async_copy(own.at[s], part.at[pl.ds((s - a) * rows, rows)], sems.at[s]))
    for copy in copies:
        copy.start()
    if noted:
        lane = lax.broadcasted_iota(jnp.int32, (META_ROWS, lanes), 1)
        note = jnp.zeros((META_ROWS, lanes), jnp.int32)
        slots = cols.shape[1]
        for s in range(slots):
            note = jnp.where(lane == s, cols[0, s], note)
        note = jnp.where(lane == slots, counts[0], note)
        start = (ranges[0][1] - ranges[0][0]) * rows
        parts[0][pl.ds(start, META_ROWS)] = note.astype(jnp.float32).astype(parts[0].dtype)
    for copy in copies:
        copy.wait()


def params():
    return pltpu.CompilerParams(vmem_limit_bytes=20 * 2**20)


def pack(ranges, noted, cols, counts, own, after):
    slots, rows, lanes = own.shape
    sizes = [(b - a) * rows for a, b in ranges]
    if noted:
        sizes[0] += META_ROWS
    return pl.pallas_call(
        functools.partial(pack_kernel, ranges, noted),
        out_shape=[jax.ShapeDtypeStruct((size, lanes), own.dtype) for size in sizes],
        in_specs=[SMEM] * 2 + [HBM, ANY],
        out_specs=[VMEM] * len(sizes),
        scratch_shapes=[pltpu.SemaphoreType.DMA((slots,))],
        compiler_params=params(),
        cost_estimate=pl.CostEstimate(flops=0, bytes_accessed=8 * sum(sizes) * lanes, transcendentals=0),
    )(cols, counts, pltpu.with_memory_space_constraint(own, pltpu.HBM), after)


def call(kernel, weight, operands, spaces, scratch, extra=(), extra_specs=(), own=None):
    b = own.shape[1:]
    band = jax.ShapeDtypeStruct((1, WIDTH) + b, own.dtype)
    last = len(operands) - 1
    alone = operands[last].shape != band.shape
    return pl.pallas_call(
        kernel,
        out_shape=[band, *extra],
        in_specs=spaces,
        out_specs=[ANY, *extra_specs],
        input_output_aliases={} if alone else {last: 0},
        scratch_shapes=scratch,
        compiler_params=params(),
        cost_estimate=pl.CostEstimate(
            flops=weight * 4 * b[0] * b[0] * b[1], bytes_accessed=weight * b[0] * b[1] * 2, transcendentals=0
        ),
    )(*operands)


def per_device(tile_values, tile_cols, tile_counts):
    total = lax.axis_size("wide")
    own = tile_values
    slots, rows, lanes = own.shape
    pairs = [(i, (i - 1) % total) for i in range(total)]
    send = lambda value, some=pairs: lax.ppermute(value, "wide", some)
    tile = lambda *n: pltpu.VMEM(n + (rows, lanes), own.dtype)
    sems = lambda *n: pltpu.SemaphoreType.DMA(n)

    first = own[0]
    head = send(first)
    parts = [first]
    for ranges, after in ((LATER[:1], first), (LATER[1:3], None), (LATER[3:], head)):
        after = parts[-1] if after is None else after
        parts += pack(ranges, after is first, tile_cols, tile_counts, own, after)
    parts = parts[1:]
    chunks = [send(part) for part in parts[:-1]]
    near = send(parts[-1], pairs[1::2])
    far = send(parts[-1], pairs[0::2])

    (band,) = call(head_kernel, 12, (own, head), [VMEM] * 2, [tile(), sems()], own=own)
    got = chunks[0][(LATER[0][1] - LATER[0][0]) * rows, : slots + 1].astype(jnp.int32)
    band, table = call(
        functools.partial(early_kernel, total), 3 * WIDTH,
        (tile_cols, tile_counts, got[None, :slots], got[slots:], own, band),
        [SMEM] * 4 + [VMEM, ANY], [tile(WIDTH), sems(WIDTH)],
        [jax.ShapeDtypeStruct((2, slots + 1), jnp.int32)], [SMEM], own=own,
    )
    for (a, b), chunk in zip(LATER[:2], chunks[:2]):
        (band,) = call(
            functools.partial(chunk_kernel, a, b - a), b - a,
            (table, own, chunk, band), [SMEM] + [VMEM] * 2 + [ANY], [tile(b - a), sems(b - a)], own=own,
        )
    a, b = LATER[2]
    band, base = call(
        functools.partial(late_kernel, a, b - a), b - a + 1,
        (table, own, chunks[2], near, band), [SMEM] + [VMEM] * 3 + [ANY], [tile(b - a + 1), sems(b - a + 1)],
        [jax.ShapeDtypeStruct((rows, lanes), jnp.float32)], [VMEM], own=own,
    )
    (band,) = call(
        last_kernel, 1, (table, own, far, base, band), [SMEM] + [VMEM] * 3 + [ANY], [tile(), sems()], own=own,
    )
    return band


def solution(mesh):
    placed = (P(("groups", "wide"), None, None), P(("groups", "wide"), None), P(("groups", "wide")))
    return jax.shard_map(
        per_device,
        mesh=mesh,
        in_specs=placed,
        out_specs=P(("groups", "wide"), None, None, None),
        check_vma=False,
    )
```

time: 56.5 us -> 53.9 us (0.954)
  waiting for transfers between devices: 31.6 us -> 19.1 us
  starting transfers between devices: 7.69 us -> 14.8 us
  Pallas kernels: 14.5 us -> 16.3 us
  local copies, waits for them, and re-layouts: 1.39 us -> 2.34 us
    ppermute x5 -> x6, waiting for transfers between devices: 31.6 us -> 19.1 us  [per_device(): send = lambda value, some=pairs: lax.ppermute(value, 'wide', some)]
    ppermute x5 -> x6, starting transfers between devices: 7.69 us -> 14.8 us  [per_device(): send = lambda value, some=pairs: lax.ppermute(value, 'wide', some)]
    pallas_call x2 -> x3, Pallas kernels: 4.25 us -> 5.59 us  [pack(): pl.pallas_call(functools.partial(pack_kernel, ranges, noted), out_shape=[...]
    squeeze x0 -> x1, local copies, waits for them, and re-layouts: none -> 1.08 us  [per_device(): first = own[0]]
    pallas_call x5 -> x6, Pallas kernels: 10.3 us -> 10.7 us  [call(): pl.pallas_call(kernel, out_shape=[band, *extra], in_specs=spaces, out_spe...]
  transfers between devices with their start and end apart: 5 -> 6, of which waited for: 5 -> 3; matrix products, arithmetic and copies ran while one was open for 1% -> 1% of each run, Pallas kernels for 21% -> 30%
where the time goes in v2:
time: 53.9 us; the launch traced here: 53.3 us
  waiting for transfers between devices  19.1 us (35%)
  Pallas kernels  16.3 us (30%)
  starting transfers between devices  14.8 us (27%)
  local copies, waits for them, and re-layouts  2.34 us (4%)
  between operations  0.78 us (1%)
    ppermute x6, waiting for transfers between devices, per_device(): send = lambda value, some=pairs: lax.ppermute(value, 'wide', some)  19.1 us
    ppermute x6, starting transfers between devices, per_device(): send = lambda value, some=pairs: lax.ppermute(value, 'wide', some)  14.8 us
    pallas_call x6, Pallas kernels, call(): pl.pallas_call(kernel, out_shape=[band, *extra], in_specs=spaces, out_spe...  10.7 us
    pallas_call x3, Pallas kernels, pack(): pl.pallas_call(functools.partial(pack_kernel, ranges, noted), out_shape=[...  5.59 us
  transfers between devices with their start and end apart: 6, of which 3 were waited for; matrix products, arithmetic and copies ran while one was open for 1% of the time, Pallas kernels for 30%

profile of v2, /device:TPU:0, one launch (start us, length us, event | category | flops | bytes accessed | tf_op | source)
XLA Modules:
  0.0 53.3 jit_solution(13452520699344587359)
XLA Ops:
  0.0 1.1 %slice_bitcast_fusion.refs_3_ = bf16[512,512]{1,0:T(8,128)(2,1)S(1)} fusion(bf16[8,512,512]{2,1,0:T(8,128)(2,1)} %own.11), kind=kLoop, calls=%fused_computation | loop fusion | bytes 1048576 | tf_op jit(solution)/shard_map/squeeze | solution.py:216
  1.1 5.5 %collective-permute-start.1 = (bf16[512,512]{1,0:T(8,128)(2,1)S(1)}, bf16[512,512]{1,0:T(8,128)(2,1)S(1)}, u32[]{:S(2)}, u32[]{:S(2)}) collective-permute-start(bf16[512,512]{1,0:T(8,128)(2,1)S(1)} %slice_bitcast_fusion.refs_3_), channel_id=1, source_target_pairs={{0,15},{1,0},{2,1},{3,2},{4,3},{5,4},{6,5},{7,6},{8,7},{9,8},{10,9... | collective-permute-start | bytes 1572872 | tf_op jit(solution)/shard_map/ppermute | solution.py:212
  7.2 0.0 copy-start.1
  7.2 0.6 %copy-done.1 = s32[1,8]{1,0:T(1,128)S(1)} copy-done((s32[1,8]{1,0:T(1,128)S(1)}, s32[1,8]{1,0:T(1,128)}, u32[]{:S(2)}) %copy-start.1) | copy-done | bytes 56
  7.9 1.7 %shard_map.37.refs_3_ = bf16[528,512]{1,0:T(8,128)(2,1)S(1)} custom-call(s32[1,8]{1,0:T(1,128)S(1)} %copy-done.1, s32[1]{0:T(128)S(6)} %copy.14.refs_1_.counts, bf16[8,512,512]{2,1,0:T(8,128)(2,1)} %own.11, bf16[512,512]{1,0:T(8,128)(2,1)S(1)} %slice_bitcast_fusion.refs_3_), custom_call_target="tpu_custom_call" | custom-call | bytes 2162688 | tf_op jit(solution)/shard_map/pallas_call | solution.py:177
  9.5 0.0 copy-start
  9.6 0.7 %collective-permute-start = (bf16[528,512]{1,0:T(8,128)(2,1)S(1)}, bf16[528,512]{1,0:T(8,128)(2,1)S(1)}, u32[]{:S(2)}, u32[]{:S(2)}) collective-permute-start(bf16[528,512]{1,0:T(8,128)(2,1)S(1)} %shard_map.37.refs_3_), channel_id=1, source_target_pairs={{0,15},{1,0},{2,1},{3,2},{4,3},{5,4},{6,5},{7,6},{8,7},{9,8},{10,9... | collective-permute-start | bytes 1622024 | tf_op jit(solution)/shard_map/ppermute | solution.py:212
  10.3 2.3 %shard_map.41 = (bf16[1536,512]{1,0:T(8,128)(2,1)S(1)}, bf16[1024,512]{1,0:T(8,128)(2,1)S(1)}) custom-call(s32[1,8]{1,0:T(1,128)S(1)} %copy-done.1, s32[1]{0:T(128)S(6)} %copy.14.refs_1_.counts, bf16[8,512,512]{2,1,0:T(8,128)(2,1)} %own.11, bf16[528,512]{1,0:T(8,128)(2,1)S(1)} %shard_map.37.refs_3_), custom_call_target="tpu_custom_call" | custom-call | bytes 10485760 | tf_op jit(solution)/shard_map/pallas_call | solution.py:177
  12.6 0.4 collective-permute-start.5
  12.9 0.4 collective-permute-start.3
  13.3 0.0 collective-permute-done.1.head.refs_3_
  13.3 1.7 %shard_map.40 = bf16[512,512]{1,0:T(8,128)(2,1)S(1)} custom-call(s32[1,8]{1,0:T(1,128)S(1)} %copy-done.1, s32[1]{0:T(128)S(6)} %copy.14.refs_1_.counts, bf16[8,512,512]{2,1,0:T(8,128)(2,1)} %own.11, bf16[512,512]{1,0:T(8,128)(2,1)S(1)} %collective-permute-done.1.head.refs_3_), custom_call_target="tpu_custom_call" | custom-call | bytes 2097152 | tf_op jit(solution)/shard_map/pallas_call | solution.py:177
  15.0 1.3 %collective-permute-start.4 = (bf16[512,512]{1,0:T(8,128)(2,1)S(1)}, bf16[512,512]{1,0:T(8,128)(2,1)S(1)}, u32[]{:S(2)}, u32[]{:S(2)}) collective-permute-start(bf16[512,512]{1,0:T(8,128)(2,1)S(1)} %shard_map.40), channel_id=1, source_target_pairs={{1,0},{3,2},{5,4},{7,6},{9,8},{11,10},{13,12},{15,14},{17,16},{19,... | collective-permute-start | bytes 1572872 | tf_op jit(solution)/shard_map/ppermute | solution.py:212
  16.3 6.5 %collective-permute-start.2 = (bf16[512,512]{1,0:T(8,128)(2,1)S(1)}, bf16[512,512]{1,0:T(8,128)(2,1)S(1)}, u32[]{:S(2)}, u32[]{:S(2)}) collective-permute-start(bf16[512,512]{1,0:T(8,128)(2,1)S(1)} %shard_map.40), channel_id=1, source_target_pairs={{0,15},{2,1},{4,3},{6,5},{8,7},{10,9},{12,11},{14,13},{16,31},{18,... | collective-permute-start | bytes 1572872 | tf_op jit(solution)/shard_map/ppermute | solution.py:212
  22.8 0.0 copy-done
  22.8 1.5 %shard_map.38.band = bf16[1,10,512,512]{3,2,1,0:T(8,128)(2,1)} custom-call(bf16[8,512,512]{2,1,0:T(8,128)(2,1)S(1)} %copy-done, bf16[512,512]{1,0:T(8,128)(2,1)S(1)} %collective-permute-done.1.head.refs_3_), custom_call_target="tpu_custom_call" | custom-call | flops 6442450944 | bytes 6291456 | tf_op jit(solution)/shard_map/pallas_call | solution.py:193
  24.3 0.0 collective-permute-done.chunk
  24.4 0.6 %slice.19 = s32[1,1]{1,0:T(1,128)} slice(s32[1,9]{1,0:T(1,128)S(1)} %slice_convert_fusion), slice={[0:1], [8:9]} | slice | bytes 8 | tf_op jit(solution)/shard_map/slice | solution.py:231
  25.0 3.7 %shard_map.39 = (bf16[1,10,512,512]{3,2,1,0:T(8,128)(2,1)}, s32[2,9]{1,0:T(2,128)S(1)}) custom-call(s32[1,8]{1,0:T(1,128)S(1)} %copy-done.1, s32[1]{0:T(128)S(6)} %copy.14.refs_1_.counts, s32[1,8]{1,0:T(1,128)S(1)} %bitcast.4, s32[1]{0:T(128)} %bitcast.1.next_counts, bf16[8,512,512]{2,1,0:T(8,128)(2,1)S(1)} %copy-done, ...), custom_call_target="tpu_custom_call", output_to_operand_aliasing={{0}: (5, {})} | custom-call | flops 16106127360 | bytes 15728640 | tf_op jit(solution)/shard_map/pallas_call | solution.py:193
  28.7 1.8 %shard_map.42.band = bf16[1,10,512,512]{3,2,1,0:T(8,128)(2,1)} custom-call(s32[2,9]{1,0:T(2,128)S(1)} %get-tuple-element.11.table, bf16[8,512,512]{2,1,0:T(8,128)(2,1)S(1)} %copy-done, bf16[528,512]{1,0:T(8,128)(2,1)S(1)} %collective-permute-done.chunk, bf16[1,10,512,512]{3,2,1,0:T(8,128)(2,1)} %get-tuple-element.14.band), custom_call_target="tpu_custom_call", output_to_operand_aliasing={{}: (3, {})} | custom-call | flops 536870912 | bytes 524288 | tf_op jit(solution)/shard_map/pallas_call | solution.py:193
  30.5 5.4 %collective-permute-done.5.chunk = bf16[1536,512]{1,0:T(8,128)(2,1)S(1)} collective-permute-done((bf16[1536,512]{1,0:T(8,128)(2,1)S(1)}, bf16[1536,512]{1,0:T(8,128)(2,1)S(1)}, u32[]{:S(2)}, u32[]{:S(2)}) %collective-permute-start.5) | collective-permute-done | bytes 1572896 | tf_op jit(solution)/shard_map/ppermute | solution.py:212
  35.9 2.5 %shard_map.43.band = bf16[1,10,512,512]{3,2,1,0:T(8,128)(2,1)} custom-call(s32[2,9]{1,0:T(2,128)S(1)} %get-tuple-element.11.table, bf16[8,512,512]{2,1,0:T(8,128)(2,1)S(1)} %copy-done, bf16[1536,512]{1,0:T(8,128)(2,1)S(1)} %collective-permute-done.5.chunk, bf16[1,10,512,512]{3,2,1,0:T(8,128)(2,1)} %shard_map.42.band), custom_call_target="tpu_custom_call", output_to_operand_aliasing={{}: (3, {})} | custom-call | flops 1610612736 | bytes 1572864 | tf_op jit(solution)/shard_map/pallas_call | solution.py:193
  38.5 8.7 %collective-permute-done.3.chunk = bf16[1024,512]{1,0:T(8,128)(2,1)S(1)} collective-permute-done((bf16[1024,512]{1,0:T(8,128)(2,1)S(1)}, bf16[1024,512]{1,0:T(8,128)(2,1)S(1)}, u32[]{:S(2)}, u32[]{:S(2)}) %collective-permute-start.3) | collective-permute-done | bytes 1048608 | tf_op jit(solution)/shard_map/ppermute | solution.py:212
  47.2 0.0 collective-permute-done.4.near
  47.2 0.6 %shard_map.44 = (bf16[1,10,512,512]{3,2,1,0:T(8,128)(2,1)}, f32[512,512]{1,0:T(8,128)S(1)}) custom-call(s32[2,9]{1,0:T(2,128)S(1)} %get-tuple-element.11.table, bf16[8,512,512]{2,1,0:T(8,128)(2,1)S(1)} %copy-done, bf16[1024,512]{1,0:T(8,128)(2,1)S(1)} %collective-permute-done.3.chunk, ...), custom_call_target="tpu_custom_call", output_to_operand_aliasing={{0}: (4, {})} | custom-call | flops 1610612736 | bytes 1572864 | tf_op jit(solution)/shard_map/pallas_call | solution.py:193
  47.8 5.0 %collective-permute-done.2.chunk = bf16[512,512]{1,0:T(8,128)(2,1)S(1)} collective-permute-done((bf16[512,512]{1,0:T(8,128)(2,1)S(1)}, bf16[512,512]{1,0:T(8,128)(2,1)S(1)}, u32[]{:S(2)}, u32[]{:S(2)}) %collective-permute-start.2) | collective-permute-done | bytes 524320 | tf_op jit(solution)/shard_map/ppermute | solution.py:212
  52.8 0.6 %shard_map.45 = bf16[1,10,512,512]{3,2,1,0:T(8,128)(2,1)} custom-call(s32[2,9]{1,0:T(2,128)S(1)} %get-tuple-element.11.table, bf16[8,512,512]{2,1,0:T(8,128)(2,1)S(1)} %copy-done, bf16[512,512]{1,0:T(8,128)(2,1)S(1)} %collective-permute-done.2.chunk, f32[512,512]{1,0:T(8,128)S(1)} %get-tuple-element.15.base, ...), custom_call_target="tpu_custom_call", output_to_operand_aliasing={{}: (4, {})} | custom-call | flops 536870912 | bytes 524288 | tf_op jit(solution)/shard_map/pallas_call | solution.py:193
  (1 shorter events, 0.0 us)
Async XLA Ops:
  1.1 12.2 %collective-permute-start.1 = (bf16[512,512]{1,0:T(8,128)(2,1)S(1)}, bf16[512,512]{1,0:T(8,128)(2,1)S(1)}, u32[]{:S(2)}, u32[]{:S(2)}) collective-permute-start(bf16[512,512]{1,0:T(8,128)(2,1)S(1)} %slice_bitcast_fusion.refs_3_), channel_id=1, source_target_pairs={{0,15},{1,0},{2,1},{3,2},{4,3},{5,4},{6,5},{7,6},{8,7},{9,8},{10,9... | collective-permute-start | bytes 1572872 | tf_op jit(solution)/shard_map/ppermute | solution.py:212
  7.2 0.7 %copy-start.1 = (s32[1,8]{1,0:T(1,128)S(1)}, s32[1,8]{1,0:T(1,128)}, u32[]{:S(2)}) copy-start(s32[1,8]{1,0:T(1,128)} %refs_0_.5) | copy-start | bytes 100
  9.5 13.3 %copy-start = (bf16[8,512,512]{2,1,0:T(8,128)(2,1)S(1)}, bf16[8,512,512]{2,1,0:T(8,128)(2,1)}, u32[]{:S(2)}) copy-start(bf16[8,512,512]{2,1,0:T(8,128)(2,1)} %own.11) | copy-start | bytes 12582916
  9.6 14.8 %collective-permute-start = (bf16[528,512]{1,0:T(8,128)(2,1)S(1)}, bf16[528,512]{1,0:T(8,128)(2,1)S(1)}, u32[]{:S(2)}, u32[]{:S(2)}) collective-permute-start(bf16[528,512]{1,0:T(8,128)(2,1)S(1)} %shard_map.37.refs_3_), channel_id=1, source_target_pairs={{0,15},{1,0},{2,1},{3,2},{4,3},{5,4},{6,5},{7,6},{8,7},{9,8},{10,9... | collective-permute-start | bytes 1622024 | tf_op jit(solution)/shard_map/ppermute | solution.py:212
  12.6 23.3 %collective-permute-start.5 = (bf16[1536,512]{1,0:T(8,128)(2,1)S(1)}, bf16[1536,512]{1,0:T(8,128)(2,1)S(1)}, u32[]{:S(2)}, u32[]{:S(2)}) collective-permute-start(bf16[1536,512]{1,0:T(8,128)(2,1)S(1)} %get-tuple-element.13), channel_id=1, source_target_pairs={{0,15},{1,0},{2,1},{3,2},{4,3},{5,4},{6,5},{7,6},{8,7},{9,8},{10,9... | collective-permute-start | bytes 4718600 | tf_op jit(solution)/shard_map/ppermute | solution.py:212
  12.9 34.2 %collective-permute-start.3 = (bf16[1024,512]{1,0:T(8,128)(2,1)S(1)}, bf16[1024,512]{1,0:T(8,128)(2,1)S(1)}, u32[]{:S(2)}, u32[]{:S(2)}) collective-permute-start(bf16[1024,512]{1,0:T(8,128)(2,1)S(1)} %get-tuple-element.12), channel_id=1, source_target_pairs={{0,15},{1,0},{2,1},{3,2},{4,3},{5,4},{6,5},{7,6},{8,7},{9,8},{10,9... | collective-permute-start | bytes 3145736 | tf_op jit(solution)/shard_map/ppermute | solution.py:212
  15.0 32.2 %collective-permute-start.4 = (bf16[512,512]{1,0:T(8,128)(2,1)S(1)}, bf16[512,512]{1,0:T(8,128)(2,1)S(1)}, u32[]{:S(2)}, u32[]{:S(2)}) collective-permute-start(bf16[512,512]{1,0:T(8,128)(2,1)S(1)} %shard_map.40), channel_id=1, source_target_pairs={{1,0},{3,2},{5,4},{7,6},{9,8},{11,10},{13,12},{15,14},{17,16},{19,... | collective-permute-start | bytes 1572872 | tf_op jit(solution)/shard_map/ppermute | solution.py:212
  16.3 36.5 %collective-permute-start.2 = (bf16[512,512]{1,0:T(8,128)(2,1)S(1)}, bf16[512,512]{1,0:T(8,128)(2,1)S(1)}, u32[]{:S(2)}, u32[]{:S(2)}) collective-permute-start(bf16[512,512]{1,0:T(8,128)(2,1)S(1)} %shard_map.40), channel_id=1, source_target_pairs={{0,15},{2,1},{4,3},{6,5},{8,7},{10,9},{12,11},{14,13},{16,31},{18,... | collective-permute-start | bytes 1572872 | tf_op jit(solution)/shard_map/ppermute | solution.py:212

commit v3 on v2

--- a/solution.py
+++ b/solution.py
@@ -11,7 +11,7 @@
 WIDTH = 2 * W + 2
 META_ROWS = 16
 LAST = 7
-LATER = ((1, 2), (2, 5), (5, LAST), (LAST, LAST + 1))
+MIDDLE = ((1, 2), (2, 4), (4, 6))
 ANY = pl.BlockSpec(memory_space=pl.ANY)
 HBM = pl.BlockSpec(memory_space=pltpu.HBM)
 SMEM = pl.BlockSpec(memory_space=pltpu.SMEM)
@@ -110,46 +110,47 @@
 
 def late_kernel(first_slot, jobs, table, own, chunk, near, band, out, base, out_v, sems):
     chunk_kernel(first_slot, jobs, table, own, chunk, band, out, out_v, sems)
+    rows = own.shape[1]
+    upper = near.shape[0]
 
     @pl.when(table[0, LAST] >= 0)
     def _():
-        even = table[0, LAST + 1] == 0
-
-        @pl.when(even)
-        def _():
-            finish(table, own, lambda: near[...], LAST, out_v, jobs)
+        f = table[1, LAST]
+        base[...] = dot(own[1, :, upper:], chunk[jobs * rows :])
+
+        @pl.when(f >= 0)
+        def _():
+            base[...] += dot(own[0], own[f])
+
+        @pl.when(table[0, LAST + 1] == 0)
+        def _():
+            out_v[jobs] = (base[...] + dot(own[1, :, :upper], near[...])).astype(out_v.dtype)
             copy = pltpu.make_async_copy(out_v.at[jobs], out.at[0, table[0, LAST]], sems.at[jobs])
             copy.start()
             copy.wait()
 
-        f = table[1, LAST]
-
-        @pl.when(jnp.logical_not(even) & (f >= 0))
-        def _():
-            base[...] = dot(own[0], own[f])
-
-        @pl.when(jnp.logical_not(even) & (f < 0))
-        def _():
-            base[...] = jnp.zeros(base.shape, base.dtype)
-
 
 def last_kernel(table, own, chunk, base, band, out, out_v, sem):
     @pl.when((table[0, LAST] >= 0) & (table[0, LAST + 1] == 1))
     def _():
-        out_v[...] = (base[...] + dot(own[1], chunk[...])).astype(out_v.dtype)
+        out_v[...] = (base[...] + dot(own[1, :, : chunk.shape[0]], chunk[...])).astype(out_v.dtype)
         copy = pltpu.make_async_copy(out_v, out.at[0, table[0, LAST]], sem)
         copy.start()
         copy.wait()
 
 
-def pack_kernel(ranges, noted, *refs):
+def pack_kernel(pieces, noted, *refs):
     cols, counts, own, _ = refs[:4]
-    parts, sems = refs[4:-1], refs[-1]
-    rows, lanes = own.shape[1:]
+    parts, sem = refs[4:-1], refs[-1]
+    lanes = own.shape[2]
     copies = []
-    for (a, b), part in zip(ranges, parts):
-        for s in range(a, b):
-            copies.append(pltpu.make_async_copy(own.at[s], part.at[pl.ds((s - a) * rows, rows)], sems.at[s]))
+    ends = []
+    for of_part, part in zip(pieces, parts):
+        at = 0
+        for slot, row, rows in of_part:
+            copies.append(pltpu.make_async_copy(own.at[slot, pl.ds(row, rows)], part.at[pl.ds(at, rows)], sem.at[len(copies)]))
+            at += rows
+        ends.append(at)
     for copy in copies:
         copy.start()
     if noted:
@@ -159,8 +160,7 @@
         for s in range(slots):
             note = jnp.where(lane == s, cols[0, s], note)
         note = jnp.where(lane == slots, counts[0], note)
-        start = (ranges[0][1] - ranges[0][0]) * rows
-        parts[0][pl.ds(start, META_ROWS)] = note.astype(jnp.float32).astype(parts[0].dtype)
+        parts[0][pl.ds(ends[0], META_ROWS)] = note.astype(jnp.float32).astype(parts[0].dtype)
     for copy in copies:
         copy.wait()
 
@@ -169,17 +169,17 @@
     return pltpu.CompilerParams(vmem_limit_bytes=20 * 2**20)
 
 
-def pack(ranges, noted, cols, counts, own, after):
-    slots, rows, lanes = own.shape
-    sizes = [(b - a) * rows for a, b in ranges]
+def pack(pieces, noted, cols, counts, own, after):
+    lanes = own.shape[2]
+    sizes = [sum(rows for _, _, rows in of_part) for of_part in pieces]
     if noted:
         sizes[0] += META_ROWS
     return pl.pallas_call(
-        functools.partial(pack_kernel, ranges, noted),
+        functools.partial(pack_kernel, pieces, noted),
         out_shape=[jax.ShapeDtypeStruct((size, lanes), own.dtype) for size in sizes],
         in_specs=[SMEM] * 2 + [HBM, ANY],
         out_specs=[VMEM] * len(sizes),
-        scratch_shapes=[pltpu.SemaphoreType.DMA((slots,))],
+        scratch_shapes=[pltpu.SemaphoreType.DMA((sum(map(len, pieces)),))],
         compiler_params=params(),
         cost_estimate=pl.CostEstimate(flops=0, bytes_accessed=8 * sum(sizes) * lanes, transcendentals=0),
     )(cols, counts, pltpu.with_memory_space_constraint(own, pltpu.HBM), after)
@@ -213,38 +213,41 @@
     tile = lambda *n: pltpu.VMEM(n + (rows, lanes), own.dtype)
     sems = lambda *n: pltpu.SemaphoreType.DMA(n)
 
+    whole = lambda a, b: tuple((s, 0, rows) for s in range(a, b))
+    upper = rows // 2
+
     first = own[0]
     head = send(first)
-    parts = [first]
-    for ranges, after in ((LATER[:1], first), (LATER[1:3], None), (LATER[3:], head)):
-        after = parts[-1] if after is None else after
-        parts += pack(ranges, after is first, tile_cols, tile_counts, own, after)
-    parts = parts[1:]
-    chunks = [send(part) for part in parts[:-1]]
-    near = send(parts[-1], pairs[1::2])
-    far = send(parts[-1], pairs[0::2])
-
-    (band,) = call(head_kernel, 12, (own, head), [VMEM] * 2, [tile(), sems()], own=own)
-    got = chunks[0][(LATER[0][1] - LATER[0][0]) * rows, : slots + 1].astype(jnp.int32)
+    (one,) = pack([whole(1, 2)], True, tile_cols, tile_counts, own, first)
+    two, three, local = pack([whole(*MIDDLE[1]), whole(*MIDDLE[2]), whole(0, slots)], False, tile_cols, tile_counts, own, one)
+    (four,) = pack([whole(LAST - 1, LAST) + ((LAST, upper, rows - upper),)], False, tile_cols, tile_counts, own, head)
+    chunks = [send(part) for part in (one, two, three)]
+    (five,) = pack([((LAST, 0, upper),)], False, tile_cols, tile_counts, own, chunks[0])
+    late = send(four)
+    near = send(five, pairs[1::2])
+    far = send(five, pairs[0::2])
+    local = local.reshape(own.shape)
+
+    (band,) = call(head_kernel, 12, (local, head), [VMEM] * 2, [tile(), sems()], own=own)
+    got = chunks[0][rows, : slots + 1].astype(jnp.int32)
     band, table = call(
         functools.partial(early_kernel, total), 3 * WIDTH,
-        (tile_cols, tile_counts, got[None, :slots], got[slots:], own, band),
+        (tile_cols, tile_counts, got[None, :slots], got[slots:], local, band),
         [SMEM] * 4 + [VMEM, ANY], [tile(WIDTH), sems(WIDTH)],
         [jax.ShapeDtypeStruct((2, slots + 1), jnp.int32)], [SMEM], own=own,
     )
-    for (a, b), chunk in zip(LATER[:2], chunks[:2]):
+    for (a, b), chunk in zip(MIDDLE, chunks):
         (band,) = call(
             functools.partial(chunk_kernel, a, b - a), b - a,
-            (table, own, chunk, band), [SMEM] + [VMEM] * 2 + [ANY], [tile(b - a), sems(b - a)], own=own,
+            (table, local, chunk, band), [SMEM] + [VMEM] * 2 + [ANY], [tile(b - a), sems(b - a)], own=own,
         )
-    a, b = LATER[2]
     band, base = call(
-        functools.partial(late_kernel, a, b - a), b - a + 1,
-        (table, own, chunks[2], near, band), [SMEM] + [VMEM] * 3 + [ANY], [tile(b - a + 1), sems(b - a + 1)],
+        functools.partial(late_kernel, LAST - 1, 1), 2,
+        (table, local, late, near, band), [SMEM] + [VMEM] * 3 + [ANY], [tile(2), sems(2)],
         [jax.ShapeDtypeStruct((rows, lanes), jnp.float32)], [VMEM], own=own,
     )
     (band,) = call(
-        last_kernel, 1, (table, own, far, base, band), [SMEM] + [VMEM] * 3 + [ANY], [tile(), sems()], own=own,
+        last_kernel, 1, (table, local, far, base, band), [SMEM] + [VMEM] * 3 + [ANY], [tile(), sems()], own=own,
     )
     return band
 

time: 53.9 us -> 53.7 us (level)
  waiting for transfers between devices: 19.1 us -> 12.8 us
  Pallas kernels: 16.3 us -> 21.2 us
  starting transfers between devices: 14.8 us -> 16.2 us
    ppermute x6 -> x7, waiting for transfers between devices: 19.1 us -> 12.8 us  [per_device(): send = lambda value, some=pairs: lax.ppermute(value, 'wide', some)]
    pallas_call x3 -> x4, Pallas kernels: 5.59 us -> 8.27 us  [pack(): pl.pallas_call(functools.partial(pack_kernel, pieces, noted), out_shape=[...]
    pallas_call x6 -> x7, Pallas kernels: 10.7 us -> 12.9 us  [call(): pl.pallas_call(kernel, out_shape=[band, *extra], in_specs=spaces, out_spe...]
    ppermute x6 -> x7, starting transfers between devices: 14.8 us -> 16.2 us  [per_device(): send = lambda value, some=pairs: lax.ppermute(value, 'wide', some)]
  transfers between devices with their start and end apart: 6 -> 7, of which waited for: 3 -> 3; matrix products, arithmetic and copies ran while one was open for 1% -> 1% of each run, Pallas kernels for 30% -> 39%
where the time goes in v3:
time: 53.7 us; the launch traced here: 53.3 us
  Pallas kernels  21.2 us (39%)
  starting transfers between devices  16.2 us (30%)
  waiting for transfers between devices  12.8 us (24%)
  local copies, waits for them, and re-layouts  2.37 us (4%)
  between operations  0.8 us (1%)
    ppermute x7, starting transfers between devices, per_device(): send = lambda value, some=pairs: lax.ppermute(value, 'wide', some)  16.2 us
    pallas_call x7, Pallas kernels, call(): pl.pallas_call(kernel, out_shape=[band, *extra], in_specs=spaces, out_spe...  12.9 us
    ppermute x7, waiting for transfers between devices, per_device(): send = lambda value, some=pairs: lax.ppermute(value, 'wide', some)  12.8 us
    pallas_call x4, Pallas kernels, pack(): pl.pallas_call(functools.partial(pack_kernel, pieces, noted), out_shape=[...  8.27 us
    squeeze x1, local copies, waits for them, and re-layouts, per_device(): first = own[0]  1.08 us
  transfers between devices with their start and end apart: 7, of which 3 were waited for; matrix products, arithmetic and copies ran while one was open for 1% of the time, Pallas kernels for 39%

profile of v3, /device:TPU:0, one launch (start us, length us, event | category | flops | bytes accessed | tf_op | source)
XLA Modules:
  0.0 53.3 jit_solution(1436920987182284873)
XLA Ops:
  0.0 1.1 %slice_bitcast_fusion.refs_3_ = bf16[512,512]{1,0:T(8,128)(2,1)S(1)} fusion(bf16[8,512,512]{2,1,0:T(8,128)(2,1)} %refs_2_.7), kind=kLoop, calls=%fused_computation | loop fusion | bytes 1048576 | tf_op jit(solution)/shard_map/squeeze | solution.py:219
  1.1 5.5 %collective-permute-start.1 = (bf16[512,512]{1,0:T(8,128)(2,1)S(1)}, bf16[512,512]{1,0:T(8,128)(2,1)S(1)}, u32[]{:S(2)}, u32[]{:S(2)}) collective-permute-start(bf16[512,512]{1,0:T(8,128)(2,1)S(1)} %slice_bitcast_fusion.refs_3_), channel_id=1, source_target_pairs={{0,15},{1,0},{2,1},{3,2},{4,3},{5,4},{6,5},{7,6},{8,7},{9,8},{10,9... | collective-permute-start | bytes 1572872 | tf_op jit(solution)/shard_map/ppermute | solution.py:212
  7.2 0.0 copy-start
  7.2 0.6 %copy-done = s32[1,8]{1,0:T(1,128)S(1)} copy-done((s32[1,8]{1,0:T(1,128)S(1)}, s32[1,8]{1,0:T(1,128)}, u32[]{:S(2)}) %copy-start) | copy-done | bytes 56
  7.9 1.6 %shard_map.37.refs_3_ = bf16[528,512]{1,0:T(8,128)(2,1)S(1)} custom-call(s32[1,8]{1,0:T(1,128)S(1)} %copy-done, s32[1]{0:T(128)S(6)} %copy.16.refs_1_.counts, bf16[8,512,512]{2,1,0:T(8,128)(2,1)} %refs_2_.7, bf16[512,512]{1,0:T(8,128)(2,1)S(1)} %slice_bitcast_fusion.refs_3_), custom_call_target="tpu_custom_call" | custom-call | bytes 2162688 | tf_op jit(solution)/shard_map/pallas_call | solution.py:177
  9.5 0.7 %collective-permute-start = (bf16[528,512]{1,0:T(8,128)(2,1)S(1)}, bf16[528,512]{1,0:T(8,128)(2,1)S(1)}, u32[]{:S(2)}, u32[]{:S(2)}) collective-permute-start(bf16[528,512]{1,0:T(8,128)(2,1)S(1)} %shard_map.37.refs_3_), channel_id=1, source_target_pairs={{0,15},{1,0},{2,1},{3,2},{4,3},{5,4},{6,5},{7,6},{8,7},{9,8},{10,9... | collective-permute-start | bytes 1622024 | tf_op jit(solution)/shard_map/ppermute | solution.py:212
  10.2 3.5 %shard_map.38 = (bf16[1024,512]{1,0:T(8,128)(2,1)S(1)}, bf16[1024,512]{1,0:T(8,128)(2,1)S(1)}, bf16[4096,512]{1,0:T(8,128)(2,1)S(1)}) custom-call(s32[1,8]{1,0:T(1,128)S(1)} %copy-done, s32[1]{0:T(128)S(6)} %copy.16.refs_1_.counts, bf16[8,512,512]{2,1,0:T(8,128)(2,1)} %refs_2_.7, bf16[528,512]{1,0:T(8,128)(2,1)S(1)} %shard_map.37.refs_3_), custom_call_target="tpu_custom_call" | custom-call | bytes 25165824 | tf_op jit(solution)/shard_map/pallas_call | solution.py:177
  13.7 0.1 collective-permute-start.6
  13.8 0.6 %collective-permute-start.5 = (bf16[1024,512]{1,0:T(8,128)(2,1)S(1)}, bf16[1024,512]{1,0:T(8,128)(2,1)S(1)}, u32[]{:S(2)}, u32[]{:S(2)}) collective-permute-start(bf16[1024,512]{1,0:T(8,128)(2,1)S(1)} %get-tuple-element.14), channel_id=1, source_target_pairs={{0,15},{1,0},{2,1},{3,2},{4,3},{5,4},{6,5},{7,6},{8,7},{9,8},{10,9... | collective-permute-start | bytes 3145736 | tf_op jit(solution)/shard_map/ppermute | solution.py:212
  14.4 0.0 collective-permute-done.1.head.refs_3_
  14.4 1.7 %shard_map.42 = bf16[768,512]{1,0:T(8,128)(2,1)S(1)} custom-call(s32[1,8]{1,0:T(1,128)S(1)} %copy-done, s32[1]{0:T(128)S(6)} %copy.16.refs_1_.counts, bf16[8,512,512]{2,1,0:T(8,128)(2,1)} %refs_2_.7, bf16[512,512]{1,0:T(8,128)(2,1)S(1)} %collective-permute-done.1.head.refs_3_), custom_call_target="tpu_custom_call" | custom-call | bytes 3145728 | tf_op jit(solution)/shard_map/pallas_call | solution.py:177
  16.1 3.5 %collective-permute-start.3 = (bf16[768,512]{1,0:T(8,128)(2,1)S(1)}, bf16[768,512]{1,0:T(8,128)(2,1)S(1)}, u32[]{:S(2)}, u32[]{:S(2)}) collective-permute-start(bf16[768,512]{1,0:T(8,128)(2,1)S(1)} %shard_map.42), channel_id=1, source_target_pairs={{0,15},{1,0},{2,1},{3,2},{4,3},{5,4},{6,5},{7,6},{8,7},{9,8},{10,9... | collective-permute-start | bytes 2359304 | tf_op jit(solution)/shard_map/ppermute | solution.py:212
  19.6 0.0 copy-start.1
  19.6 1.5 %shard_map.39.band = bf16[1,10,512,512]{3,2,1,0:T(8,128)(2,1)} custom-call(bf16[8,512,512]{2,1,0:T(8,128)(2,1)S(1)} %bitcast.5, bf16[512,512]{1,0:T(8,128)(2,1)S(1)} %collective-permute-done.1.head.refs_3_), custom_call_target="tpu_custom_call" | custom-call | flops 6442450944 | bytes 6291456 | tf_op jit(solution)/shard_map/pallas_call | solution.py:193
  21.1 0.0 collective-permute-done.refs_3_.chunk
  21.1 1.5 %shard_map.41 = bf16[256,512]{1,0:T(8,128)(2,1)S(1)} custom-call(s32[1,8]{1,0:T(1,128)S(1)} %copy-done, s32[1]{0:T(128)S(6)} %copy.16.refs_1_.counts, bf16[8,512,512]{2,1,0:T(8,128)(2,1)} %refs_2_.7, bf16[528,512]{1,0:T(8,128)(2,1)S(1)} %collective-permute-done.refs_3_.chunk), custom_call_target="tpu_custom_call" | custom-call | bytes 1048576 | tf_op jit(solution)/shard_map/pallas_call | solution.py:177
  22.6 1.3 %collective-permute-start.4 = (bf16[256,512]{1,0:T(8,128)(2,1)S(1)}, bf16[256,512]{1,0:T(8,128)(2,1)S(1)}, u32[]{:S(2)}, u32[]{:S(2)}) collective-permute-start(bf16[256,512]{1,0:T(8,128)(2,1)S(1)} %shard_map.41), channel_id=1, source_target_pairs={{1,0},{3,2},{5,4},{7,6},{9,8},{11,10},{13,12},{15,14},{17,16},{19,... | collective-permute-start | bytes 786440 | tf_op jit(solution)/shard_map/ppermute | solution.py:212
  23.9 4.5 %collective-permute-start.2 = (bf16[256,512]{1,0:T(8,128)(2,1)S(1)}, bf16[256,512]{1,0:T(8,128)(2,1)S(1)}, u32[]{:S(2)}, u32[]{:S(2)}) collective-permute-start(bf16[256,512]{1,0:T(8,128)(2,1)S(1)} %shard_map.41), channel_id=1, source_target_pairs={{0,15},{2,1},{4,3},{6,5},{8,7},{10,9},{12,11},{14,13},{16,31},{18,... | collective-permute-start | bytes 786440 | tf_op jit(solution)/shard_map/ppermute | solution.py:212
  28.4 0.6 %slice.19 = s32[1,1]{1,0:T(1,128)} slice(s32[1,9]{1,0:T(1,128)S(1)} %slice_convert_fusion), slice={[0:1], [8:9]} | slice | bytes 8 | tf_op jit(solution)/shard_map/slice | solution.py:235
  29.1 0.0 copy-done.1
  29.1 4.1 %shard_map.40 = (bf16[1,10,512,512]{3,2,1,0:T(8,128)(2,1)}, s32[2,9]{1,0:T(2,128)S(1)}) custom-call(s32[1,8]{1,0:T(1,128)S(1)} %copy-done.1, s32[1]{0:T(128)S(6)} %copy.16.refs_1_.counts, s32[1,8]{1,0:T(1,128)S(1)} %bitcast.12, s32[1]{0:T(128)} %bitcast.1.next_counts, bf16[8,512,512]{2,1,0:T(8,128)(2,1)S(1)} %bitcast.6, ...), custom_call_target="tpu_custom_call", output_to_operand_aliasing={{0}: (5, {})} | custom-call | flops 16106127360 | bytes 15728640 | tf_op jit(solution)/shard_map/pallas_call | solution.py:193
  33.2 1.8 %shard_map.43.band = bf16[1,10,512,512]{3,2,1,0:T(8,128)(2,1)} custom-call(s32[2,9]{1,0:T(2,128)S(1)} %get-tuple-element.13.table, bf16[8,512,512]{2,1,0:T(8,128)(2,1)S(1)} %bitcast.7, bf16[528,512]{1,0:T(8,128)(2,1)S(1)} %collective-permute-done.refs_3_.chunk, bf16[1,10,512,512]{3,2,1,0:T(8,128)(2,1)} %get-tuple-element.16.band), custom_call_target="tpu_custom_call", output_to_operand_aliasing={{}: (3, {})} | custom-call | flops 536870912 | bytes 524288 | tf_op jit(solution)/shard_map/pallas_call | solution.py:193
  35.0 0.0 collective-permute-done.6.chunk
  35.0 2.3 %shard_map.44.band = bf16[1,10,512,512]{3,2,1,0:T(8,128)(2,1)} custom-call(s32[2,9]{1,0:T(2,128)S(1)} %get-tuple-element.13.table, bf16[8,512,512]{2,1,0:T(8,128)(2,1)S(1)} %bitcast.8, bf16[1024,512]{1,0:T(8,128)(2,1)S(1)} %collective-permute-done.6.chunk, bf16[1,10,512,512]{3,2,1,0:T(8,128)(2,1)} %shard_map.43.band), custom_call_target="tpu_custom_call", output_to_operand_aliasing={{}: (3, {})} | custom-call | flops 1073741824 | bytes 1048576 | tf_op jit(solution)/shard_map/pallas_call | solution.py:193
  37.3 4.3 %collective-permute-done.5.chunk = bf16[1024,512]{1,0:T(8,128)(2,1)S(1)} collective-permute-done((bf16[1024,512]{1,0:T(8,128)(2,1)S(1)}, bf16[1024,512]{1,0:T(8,128)(2,1)S(1)}, u32[]{:S(2)}, u32[]{:S(2)}) %collective-permute-start.5) | collective-permute-done | bytes 1048608 | tf_op jit(solution)/shard_map/ppermute | solution.py:212
  41.5 2.1 %shard_map.45.band = bf16[1,10,512,512]{3,2,1,0:T(8,128)(2,1)} custom-call(s32[2,9]{1,0:T(2,128)S(1)} %get-tuple-element.13.table, bf16[8,512,512]{2,1,0:T(8,128)(2,1)S(1)} %bitcast.9, bf16[1024,512]{1,0:T(8,128)(2,1)S(1)} %collective-permute-done.5.chunk, bf16[1,10,512,512]{3,2,1,0:T(8,128)(2,1)} %shard_map.44.band), custom_call_target="tpu_custom_call", output_to_operand_aliasing={{}: (3, {})} | custom-call | flops 1073741824 | bytes 1048576 | tf_op jit(solution)/shard_map/pallas_call | solution.py:193
  43.6 0.0 collective-permute-done.4.near
  43.6 6.3 %collective-permute-done.3.chunk = bf16[768,512]{1,0:T(8,128)(2,1)S(1)} collective-permute-done((bf16[768,512]{1,0:T(8,128)(2,1)S(1)}, bf16[768,512]{1,0:T(8,128)(2,1)S(1)}, u32[]{:S(2)}, u32[]{:S(2)}) %collective-permute-start.3) | collective-permute-done | bytes 786464 | tf_op jit(solution)/shard_map/ppermute | solution.py:212
  50.0 0.6 %shard_map.46 = (bf16[1,10,512,512]{3,2,1,0:T(8,128)(2,1)}, f32[512,512]{1,0:T(8,128)S(1)}) custom-call(s32[2,9]{1,0:T(2,128)S(1)} %get-tuple-element.13.table, bf16[8,512,512]{2,1,0:T(8,128)(2,1)S(1)} %bitcast.10, bf16[768,512]{1,0:T(8,128)(2,1)S(1)} %collective-permute-done.3.chunk, ...), custom_call_target="tpu_custom_call", output_to_operand_aliasing={{0}: (4, {})} | custom-call | flops 1073741824 | bytes 1048576 | tf_op jit(solution)/shard_map/pallas_call | solution.py:193
  50.6 2.2 %collective-permute-done.2.chunk = bf16[256,512]{1,0:T(8,128)(2,1)S(1)} collective-permute-done((bf16[256,512]{1,0:T(8,128)(2,1)S(1)}, bf16[256,512]{1,0:T(8,128)(2,1)S(1)}, u32[]{:S(2)}, u32[]{:S(2)}) %collective-permute-start.2) | collective-permute-done | bytes 262176 | tf_op jit(solution)/shard_map/ppermute | solution.py:212
  52.8 0.6 %shard_map.47 = bf16[1,10,512,512]{3,2,1,0:T(8,128)(2,1)} custom-call(s32[2,9]{1,0:T(2,128)S(1)} %get-tuple-element.13.table, bf16[8,512,512]{2,1,0:T(8,128)(2,1)S(1)} %bitcast.11, bf16[256,512]{1,0:T(8,128)(2,1)S(1)} %collective-permute-done.2.chunk, f32[512,512]{1,0:T(8,128)S(1)} %get-tuple-element.17.base, ...), custom_call_target="tpu_custom_call", output_to_operand_aliasing={{}: (4, {})} | custom-call | flops 536870912 | bytes 524288 | tf_op jit(solution)/shard_map/pallas_call | solution.py:193
  (1 shorter events, 0.0 us)
Async XLA Ops:
  1.1 13.3 %collective-permute-start.1 = (bf16[512,512]{1,0:T(8,128)(2,1)S(1)}, bf16[512,512]{1,0:T(8,128)(2,1)S(1)}, u32[]{:S(2)}, u32[]{:S(2)}) collective-permute-start(bf16[512,512]{1,0:T(8,128)(2,1)S(1)} %slice_bitcast_fusion.refs_3_), channel_id=1, source_target_pairs={{0,15},{1,0},{2,1},{3,2},{4,3},{5,4},{6,5},{7,6},{8,7},{9,8},{10,9... | collective-permute-start | bytes 1572872 | tf_op jit(solution)/shard_map/ppermute | solution.py:212
  7.2 0.7 %copy-start = (s32[1,8]{1,0:T(1,128)S(1)}, s32[1,8]{1,0:T(1,128)}, u32[]{:S(2)}) copy-start(s32[1,8]{1,0:T(1,128)} %refs_0_.7) | copy-start | bytes 100
  9.5 11.6 %collective-permute-start = (bf16[528,512]{1,0:T(8,128)(2,1)S(1)}, bf16[528,512]{1,0:T(8,128)(2,1)S(1)}, u32[]{:S(2)}, u32[]{:S(2)}) collective-permute-start(bf16[528,512]{1,0:T(8,128)(2,1)S(1)} %shard_map.37.refs_3_), channel_id=1, source_target_pairs={{0,15},{1,0},{2,1},{3,2},{4,3},{5,4},{6,5},{7,6},{8,7},{9,8},{10,9... | collective-permute-start | bytes 1622024 | tf_op jit(solution)/shard_map/ppermute | solution.py:212
  13.7 21.2 %collective-permute-start.6 = (bf16[1024,512]{1,0:T(8,128)(2,1)S(1)}, bf16[1024,512]{1,0:T(8,128)(2,1)S(1)}, u32[]{:S(2)}, u32[]{:S(2)}) collective-permute-start(bf16[1024,512]{1,0:T(8,128)(2,1)S(1)} %get-tuple-element.15), channel_id=1, source_target_pairs={{0,15},{1,0},{2,1},{3,2},{4,3},{5,4},{6,5},{7,6},{8,7},{9,8},{10,9... | collective-permute-start | bytes 3145736 | tf_op jit(solution)/shard_map/ppermute | solution.py:212
  13.8 27.7 %collective-permute-start.5 = (bf16[1024,512]{1,0:T(8,128)(2,1)S(1)}, bf16[1024,512]{1,0:T(8,128)(2,1)S(1)}, u32[]{:S(2)}, u32[]{:S(2)}) collective-permute-start(bf16[1024,512]{1,0:T(8,128)(2,1)S(1)} %get-tuple-element.14), channel_id=1, source_target_pairs={{0,15},{1,0},{2,1},{3,2},{4,3},{5,4},{6,5},{7,6},{8,7},{9,8},{10,9... | collective-permute-start | bytes 3145736 | tf_op jit(solution)/shard_map/ppermute | solution.py:212
  16.1 33.9 %collective-permute-start.3 = (bf16[768,512]{1,0:T(8,128)(2,1)S(1)}, bf16[768,512]{1,0:T(8,128)(2,1)S(1)}, u32[]{:S(2)}, u32[]{:S(2)}) collective-permute-start(bf16[768,512]{1,0:T(8,128)(2,1)S(1)} %shard_map.42), channel_id=1, source_target_pairs={{0,15},{1,0},{2,1},{3,2},{4,3},{5,4},{6,5},{7,6},{8,7},{9,8},{10,9... | collective-permute-start | bytes 2359304 | tf_op jit(solution)/shard_map/ppermute | solution.py:212
  19.6 9.5 %copy-start.1 = (s32[1,8]{1,0:T(1,128)S(1)}, s32[1,8]{1,0:T(1,128)}, u32[]{:S(2)}) copy-start(s32[1,8]{1,0:T(1,128)} %refs_0_.7) | copy-start | bytes 100
  22.6 21.0 %collective-permute-start.4 = (bf16[256,512]{1,0:T(8,128)(2,1)S(1)}, bf16[256,512]{1,0:T(8,128)(2,1)S(1)}, u32[]{:S(2)}, u32[]{:S(2)}) collective-permute-start(bf16[256,512]{1,0:T(8,128)(2,1)S(1)} %shard_map.41), channel_id=1, source_target_pairs={{1,0},{3,2},{5,4},{7,6},{9,8},{11,10},{13,12},{15,14},{17,16},{19,... | collective-permute-start | bytes 786440 | tf_op jit(solution)/shard_map/ppermute | solution.py:212
  23.9 28.8 %collective-permute-start.2 = (bf16[256,512]{1,0:T(8,128)(2,1)S(1)}, bf16[256,512]{1,0:T(8,128)(2,1)S(1)}, u32[]{:S(2)}, u32[]{:S(2)}) collective-permute-start(bf16[256,512]{1,0:T(8,128)(2,1)S(1)} %shard_map.41), channel_id=1, source_target_pairs={{0,15},{2,1},{4,3},{6,5},{8,7},{10,9},{12,11},{14,13},{16,31},{18,... | collective-permute-start | bytes 786440 | tf_op jit(solution)/shard_map/ppermute | solution.py:212

commit v4 on v3

--- a/solution.py
+++ b/solution.py
@@ -12,6 +12,7 @@
 META_ROWS = 16
 LAST = 7
 MIDDLE = ((1, 2), (2, 4), (4, 6))
+DETOUR = 80
 ANY = pl.BlockSpec(memory_space=pl.ANY)
 HBM = pl.BlockSpec(memory_space=pltpu.HBM)
 SMEM = pl.BlockSpec(memory_space=pltpu.SMEM)
@@ -36,8 +37,17 @@
     copy.wait()
 
 
-def early_kernel(total, cols, counts, next_cols, next_counts, own, band, out, table, out_v, sems):
+def early_kernel(total, cols, counts, next_cols, next_counts, own, direct, detour, band, out, table, rest, out_v, sems):
     here = cols[0, 0]
+
+    @pl.when(here == total - 1)
+    def _():
+        rest[...] = detour[...]
+
+    @pl.when(here < total - 1)
+    def _():
+        rest[...] = direct[...]
+
     for s in range(next_cols.shape[1]):
         col = next_cols[0, s]
         table[0, s] = jnp.where(s < next_counts[0], lax.rem(col - here + W + total, total), -1)
@@ -108,7 +118,7 @@
             out_copy(t).wait()
 
 
-def late_kernel(first_slot, jobs, table, own, chunk, near, band, out, base, out_v, sems):
+def late_kernel(first_slot, jobs, table, own, chunk, rest, near, band, out, base, low, out_v, sems):
     chunk_kernel(first_slot, jobs, table, own, chunk, band, out, out_v, sems)
     rows = own.shape[1]
     upper = near.shape[0]
@@ -116,7 +126,9 @@
     @pl.when(table[0, LAST] >= 0)
     def _():
         f = table[1, LAST]
-        base[...] = dot(own[1, :, upper:], chunk[jobs * rows :])
+        low[: low.shape[0] - DETOUR] = chunk[jobs * rows :]
+        low[low.shape[0] - DETOUR :] = rest[...]
+        base[...] = dot(own[1, :, upper:], low[...])
 
         @pl.when(f >= 0)
         def _():
@@ -218,9 +230,11 @@
 
     first = own[0]
     head = send(first)
-    (one,) = pack([whole(1, 2)], True, tile_cols, tile_counts, own, first)
+    one, end = pack([whole(1, 2), ((LAST, rows - DETOUR, DETOUR),)], True, tile_cols, tile_counts, own, first)
+    detour = send(send(end, [(0, 2)]), [(2, total - 1)])
+    direct = send(end, pairs[1:])
     two, three, local = pack([whole(*MIDDLE[1]), whole(*MIDDLE[2]), whole(0, slots)], False, tile_cols, tile_counts, own, one)
-    (four,) = pack([whole(LAST - 1, LAST) + ((LAST, upper, rows - upper),)], False, tile_cols, tile_counts, own, head)
+    (four,) = pack([whole(LAST - 1, LAST) + ((LAST, upper, rows - upper - DETOUR),)], False, tile_cols, tile_counts, own, head)
     chunks = [send(part) for part in (one, two, three)]
     (five,) = pack([((LAST, 0, upper),)], False, tile_cols, tile_counts, own, chunks[0])
     late = send(four)
@@ -230,11 +244,11 @@
 
     (band,) = call(head_kernel, 12, (local, head), [VMEM] * 2, [tile(), sems()], own=own)
     got = chunks[0][rows, : slots + 1].astype(jnp.int32)
-    band, table = call(
+    band, table, rest = call(
         functools.partial(early_kernel, total), 3 * WIDTH,
-        (tile_cols, tile_counts, got[None, :slots], got[slots:], local, band),
-        [SMEM] * 4 + [VMEM, ANY], [tile(WIDTH), sems(WIDTH)],
-        [jax.ShapeDtypeStruct((2, slots + 1), jnp.int32)], [SMEM], own=own,
+        (tile_cols, tile_counts, got[None, :slots], got[slots:], local, direct, detour, band),
+        [SMEM] * 4 + [VMEM] * 3 + [ANY], [tile(WIDTH), sems(WIDTH)],
+        [jax.ShapeDtypeStruct((2, slots + 1), jnp.int32), jax.ShapeDtypeStruct(end.shape, own.dtype)], [SMEM, VMEM], own=own,
     )
     for (a, b), chunk in zip(MIDDLE, chunks):
         (band,) = call(
@@ -243,7 +257,8 @@
         )
     band, base = call(
         functools.partial(late_kernel, LAST - 1, 1), 2,
-        (table, local, late, near, band), [SMEM] + [VMEM] * 3 + [ANY], [tile(2), sems(2)],
+        (table, local, late, rest, near, band), [SMEM] + [VMEM] * 4 + [ANY],
+        [pltpu.VMEM((rows - upper, lanes), own.dtype), tile(2), sems(2)],
         [jax.ShapeDtypeStruct((rows, lanes), jnp.float32)], [VMEM], own=own,
     )
     (band,) = call(

time: 53.7 us -> 68.5 us (1.28)
  the two profiles are of different devices: /device:TPU:0 before, /device:TPU:1 now
where the time goes in v4:
time: 68.5 us; the launch traced here: 68.4 us
  starting transfers between devices  38.1 us (56%)
  Pallas kernels  25.2 us (37%)
  local copies, waits for them, and re-layouts  2.39 us (3%)
  waiting for transfers between devices  1.75 us (3%)
  between operations  0.86 us (1%)
    ppermute x10, starting transfers between devices, per_device(): send = lambda value, some=pairs: lax.ppermute(value, 'wide', some)  38.1 us
    pallas_call x7, Pallas kernels, call(): pl.pallas_call(kernel, out_shape=[band, *extra], in_specs=spaces, out_spe...  17 us
    pallas_call x4, Pallas kernels, pack(): pl.pallas_call(functools.partial(pack_kernel, pieces, noted), out_shape=[...  8.26 us
    ppermute x10, waiting for transfers between devices, per_device(): send = lambda value, some=pairs: lax.ppermute(value, 'wide', some)  1.75 us
  transfers between devices with their start and end apart: 10, of which 1 were waited for; matrix products, arithmetic and copies ran while one was open for 1% of the time, Pallas kernels for 34%

profile of v4, /device:TPU:1, one launch (start us, length us, event | category | flops | bytes accessed | tf_op | source)
XLA Modules:
  0.0 68.4 jit_solution(10235615358676166873)
XLA Ops:
  0.0 0.0 copy-start.1
  0.0 1.1 %slice_bitcast_fusion.refs_3_ = bf16[512,512]{1,0:T(8,128)(2,1)S(1)} fusion(bf16[8,512,512]{2,1,0:T(8,128)(2,1)} %refs_2_.7), kind=kLoop, calls=%fused_computation | loop fusion | bytes 1048576 | tf_op jit(solution)/shard_map/squeeze | solution.py:231
  1.1 0.1 collective-permute-start.4
  1.9 0.0 copy-start
  1.9 0.6 copy-done
  2.5 1.6 %shard_map.37 = (bf16[528,512]{1,0:T(8,128)(2,1)S(1)}, bf16[80,512]{1,0:T(8,128)(2,1)S(1)}) custom-call(s32[1,8]{1,0:T(1,128)S(1)} %copy-done, s32[1]{0:T(128)S(6)} %copy.16.refs_1_.counts, bf16[8,512,512]{2,1,0:T(8,128)(2,1)} %refs_2_.7, bf16[512,512]{1,0:T(8,128)(2,1)S(1)} %slice_bitcast_fusion.refs_3_), custom_call_target="tpu_custom_call" | custom-call | bytes 2490368 | tf_op jit(solution)/shard_map/pallas_call | solution.py:189
  4.1 0.7 collective-permute-start.2
  4.8 8.0 %collective-permute-start.1 = (bf16[80,512]{1,0:T(8,128)(2,1)S(1)}, bf16[80,512]{1,0:T(8,128)(2,1)S(1)}, u32[]{:S(2)}, u32[]{:S(2)}) collective-permute-start(bf16[80,512]{1,0:T(8,128)(2,1)S(1)} %get-tuple-element.17), channel_id=1, source_target_pairs={{1,0},{2,1},{3,2},{4,3},{5,4},{6,5},{7,6},{8,7},{9,8},{10,9},{11,1... | collective-permute-start | bytes 245768 | tf_op jit(solution)/shard_map/ppermute | solution.py:224
  12.8 0.1 collective-permute-start
  12.9 3.5 %shard_map.38 = (bf16[1024,512]{1,0:T(8,128)(2,1)S(1)}, bf16[1024,512]{1,0:T(8,128)(2,1)S(1)}, bf16[4096,512]{1,0:T(8,128)(2,1)S(1)}) custom-call(s32[1,8]{1,0:T(1,128)S(1)} %copy-done, s32[1]{0:T(128)S(6)} %copy.16.refs_1_.counts, bf16[8,512,512]{2,1,0:T(8,128)(2,1)} %refs_2_.7, bf16[528,512]{1,0:T(8,128)(2,1)S(1)} %get-tuple-element.15.refs_3_), custom_call_target="tpu_custom_call" | custom-call | bytes 25165824 | tf_op jit(solution)/shard_map/pallas_call | solution.py:189
  16.4 0.1 collective-permute-start.9
  16.5 0.0 collective-permute-done.2
  16.5 25.3 %collective-permute-start.8 = (bf16[1024,512]{1,0:T(8,128)(2,1)S(1)}, bf16[1024,512]{1,0:T(8,128)(2,1)S(1)}, u32[]{:S(2)}, u32[]{:S(2)}) collective-permute-start(bf16[1024,512]{1,0:T(8,128)(2,1)S(1)} %get-tuple-element.20), channel_id=1, source_target_pairs={{0,15},{1,0},{2,1},{3,2},{4,3},{5,4},{6,5},{7,6},{8,7},{9,8},{10,9... | collective-permute-start | bytes 3145736 | tf_op jit(solution)/shard_map/ppermute | solution.py:224
  41.8 0.0 collective-permute-done.4.head.refs_3_
  41.8 0.7 collective-permute-start.3
  42.4 0.0 copy-done.1
  42.5 1.6 %shard_map.42 = bf16[688,512]{1,0:T(8,128)(2,1)S(1)} custom-call(s32[1,8]{1,0:T(1,128)S(1)} %copy-done.1, s32[1]{0:T(128)S(6)} %copy.16.refs_1_.counts, bf16[8,512,512]{2,1,0:T(8,128)(2,1)} %refs_2_.7, bf16[512,512]{1,0:T(8,128)(2,1)S(1)} %collective-permute-done.4.head.refs_3_), custom_call_target="tpu_custom_call" | custom-call | bytes 2818048 | tf_op jit(solution)/shard_map/pallas_call | solution.py:189
  44.1 1.5 %shard_map.39.band = bf16[1,10,512,512]{3,2,1,0:T(8,128)(2,1)} custom-call(bf16[8,512,512]{2,1,0:T(8,128)(2,1)S(1)} %bitcast.5, bf16[512,512]{1,0:T(8,128)(2,1)S(1)} %collective-permute-done.4.head.refs_3_), custom_call_target="tpu_custom_call" | custom-call | flops 6442450944 | bytes 6291456 | tf_op jit(solution)/shard_map/pallas_call | solution.py:205
  45.6 0.0 collective-permute-done.refs_3_.chunk
  45.6 0.1 collective-permute-start.6
  45.7 0.6 slice.19
  46.3 1.5 %shard_map.41 = bf16[256,512]{1,0:T(8,128)(2,1)S(1)} custom-call(s32[1,8]{1,0:T(1,128)S(1)} %copy-done.1, s32[1]{0:T(128)S(6)} %copy.16.refs_1_.counts, bf16[8,512,512]{2,1,0:T(8,128)(2,1)} %refs_2_.7, bf16[528,512]{1,0:T(8,128)(2,1)S(1)} %collective-permute-done.refs_3_.chunk), custom_call_target="tpu_custom_call" | custom-call | bytes 1048576 | tf_op jit(solution)/shard_map/pallas_call | solution.py:189
  47.9 0.0 collective-permute-done.1.direct
  47.9 1.9 %collective-permute-start.7 = (bf16[256,512]{1,0:T(8,128)(2,1)S(1)}, bf16[256,512]{1,0:T(8,128)(2,1)S(1)}, u32[]{:S(2)}, u32[]{:S(2)}) collective-permute-start(bf16[256,512]{1,0:T(8,128)(2,1)S(1)} %shard_map.41), channel_id=1, source_target_pairs={{1,0},{3,2},{5,4},{7,6},{9,8},{11,10},{13,12},{15,14},{17,16},{19,... | collective-permute-start | bytes 786440 | tf_op jit(solution)/shard_map/ppermute | solution.py:224
  49.8 0.0 collective-permute-done.3.detour
  49.8 1.3 %collective-permute-start.5 = (bf16[256,512]{1,0:T(8,128)(2,1)S(1)}, bf16[256,512]{1,0:T(8,128)(2,1)S(1)}, u32[]{:S(2)}, u32[]{:S(2)}) collective-permute-start(bf16[256,512]{1,0:T(8,128)(2,1)S(1)} %shard_map.41), channel_id=1, source_target_pairs={{0,15},{2,1},{4,3},{6,5},{8,7},{10,9},{12,11},{14,13},{16,31},{18,... | collective-permute-start | bytes 786440 | tf_op jit(solution)/shard_map/ppermute | solution.py:224
  51.1 3.6 %shard_map.40 = (bf16[1,10,512,512]{3,2,1,0:T(8,128)(2,1)}, s32[2,9]{1,0:T(2,128)S(1)}, bf16[80,512]{1,0:T(8,128)(2,1)S(1)}) custom-call(s32[1,8]{1,0:T(1,128)S(1)} %copy-done.1, s32[1]{0:T(128)S(6)} %copy.16.refs_1_.counts, s32[1,8]{1,0:T(1,128)S(1)} %bitcast.12, s32[1]{0:T(128)} %bitcast.1.next_counts, ...), custom_call_target="tpu_custom_call", output_to_operand_aliasing={{0}: (7, {})} | custom-call | flops 16106127360 | bytes 15728640 | tf_op jit(solution)/shard_map/pallas_call | solution.py:205
  54.7 2.1 %shard_map.43.band = bf16[1,10,512,512]{3,2,1,0:T(8,128)(2,1)} custom-call(s32[2,9]{1,0:T(2,128)S(1)} %get-tuple-element.18.table, bf16[8,512,512]{2,1,0:T(8,128)(2,1)S(1)} %bitcast.7, bf16[528,512]{1,0:T(8,128)(2,1)S(1)} %collective-permute-done.refs_3_.chunk, bf16[1,10,512,512]{3,2,1,0:T(8,128)(2,1)} %get-tuple-element.22.band), custom_call_target="tpu_custom_call", output_to_operand_aliasing={{}: (3, {})} | custom-call | flops 536870912 | bytes 524288 | tf_op jit(solution)/shard_map/pallas_call | solution.py:205
  56.8 0.0 collective-permute-done.9.chunk
  56.8 2.5 %shard_map.44.band = bf16[1,10,512,512]{3,2,1,0:T(8,128)(2,1)} custom-call(s32[2,9]{1,0:T(2,128)S(1)} %get-tuple-element.18.table, bf16[8,512,512]{2,1,0:T(8,128)(2,1)S(1)} %bitcast.8, bf16[1024,512]{1,0:T(8,128)(2,1)S(1)} %collective-permute-done.9.chunk, bf16[1,10,512,512]{3,2,1,0:T(8,128)(2,1)} %shard_map.43.band), custom_call_target="tpu_custom_call", output_to_operand_aliasing={{}: (3, {})} | custom-call | flops 1073741824 | bytes 1048576 | tf_op jit(solution)/shard_map/pallas_call | solution.py:205
  59.3 0.0 collective-permute-done.8.chunk
  59.3 2.8 %shard_map.45.band = bf16[1,10,512,512]{3,2,1,0:T(8,128)(2,1)} custom-call(s32[2,9]{1,0:T(2,128)S(1)} %get-tuple-element.18.table, bf16[8,512,512]{2,1,0:T(8,128)(2,1)S(1)} %bitcast.9, bf16[1024,512]{1,0:T(8,128)(2,1)S(1)} %collective-permute-done.8.chunk, bf16[1,10,512,512]{3,2,1,0:T(8,128)(2,1)} %shard_map.44.band), custom_call_target="tpu_custom_call", output_to_operand_aliasing={{}: (3, {})} | custom-call | flops 1073741824 | bytes 1048576 | tf_op jit(solution)/shard_map/pallas_call | solution.py:205
  62.2 0.0 collective-permute-done.7.near
  62.2 1.7 %collective-permute-done.6.chunk = bf16[688,512]{1,0:T(8,128)(2,1)S(1)} collective-permute-done((bf16[688,512]{1,0:T(8,128)(2,1)S(1)}, bf16[688,512]{1,0:T(8,128)(2,1)S(1)}, u32[]{:S(2)}, u32[]{:S(2)}) %collective-permute-start.6) | collective-permute-done | bytes 704544 | tf_op jit(solution)/shard_map/ppermute | solution.py:224
  63.9 2.8 %shard_map.46 = (bf16[1,10,512,512]{3,2,1,0:T(8,128)(2,1)}, f32[512,512]{1,0:T(8,128)S(1)}) custom-call(s32[2,9]{1,0:T(2,128)S(1)} %get-tuple-element.18.table, bf16[8,512,512]{2,1,0:T(8,128)(2,1)S(1)} %bitcast.10, bf16[688,512]{1,0:T(8,128)(2,1)S(1)} %collective-permute-done.6.chunk, ...), custom_call_target="tpu_custom_call", output_to_operand_aliasing={{0}: (5, {})} | custom-call | flops 1073741824 | bytes 1048576 | tf_op jit(solution)/shard_map/pallas_call | solution.py:205
  66.7 0.0 collective-permute-done.5.chunk
  66.7 1.6 %shard_map.47 = bf16[1,10,512,512]{3,2,1,0:T(8,128)(2,1)} custom-call(s32[2,9]{1,0:T(2,128)S(1)} %get-tuple-element.18.table, bf16[8,512,512]{2,1,0:T(8,128)(2,1)S(1)} %bitcast.11, bf16[256,512]{1,0:T(8,128)(2,1)S(1)} %collective-permute-done.5.chunk, f32[512,512]{1,0:T(8,128)S(1)} %get-tuple-element.23.base, ...), custom_call_target="tpu_custom_call", output_to_operand_aliasing={{}: (4, {})} | custom-call | flops 536870912 | bytes 524288 | tf_op jit(solution)/shard_map/pallas_call | solution.py:205
  (1 shorter events, 0.0 us)
Async XLA Ops:
  0.0 42.4 %copy-start.1 = (s32[1,8]{1,0:T(1,128)S(1)}, s32[1,8]{1,0:T(1,128)}, u32[]{:S(2)}) copy-start(s32[1,8]{1,0:T(1,128)} %refs_0_.7) | copy-start | bytes 100
  1.1 40.7 %collective-permute-start.4 = (bf16[512,512]{1,0:T(8,128)(2,1)S(1)}, bf16[512,512]{1,0:T(8,128)(2,1)S(1)}, u32[]{:S(2)}, u32[]{:S(2)}) collective-permute-start(bf16[512,512]{1,0:T(8,128)(2,1)S(1)} %slice_bitcast_fusion.refs_3_), channel_id=1, source_target_pairs={{0,15},{1,0},{2,1},{3,2},{4,3},{5,4},{6,5},{7,6},{8,7},{9,8},{10,9... | collective-permute-start | bytes 1572872 | tf_op jit(solution)/shard_map/ppermute | solution.py:224
  1.9 0.7 copy-start
  4.1 12.4 %collective-permute-start.2 = (bf16[80,512]{1,0:T(8,128)(2,1)S(1)}, bf16[80,512]{1,0:T(8,128)(2,1)S(1)}, u32[]{:S(2)}, u32[]{:S(2)}) collective-permute-start(bf16[80,512]{1,0:T(8,128)(2,1)S(1)} %get-tuple-element.17), channel_id=1, source_target_pairs={{0,2},{16,18}} | collective-permute-start | bytes 245768 | tf_op jit(solution)/shard_map/ppermute | solution.py:224
  4.8 43.1 %collective-permute-start.1 = (bf16[80,512]{1,0:T(8,128)(2,1)S(1)}, bf16[80,512]{1,0:T(8,128)(2,1)S(1)}, u32[]{:S(2)}, u32[]{:S(2)}) collective-permute-start(bf16[80,512]{1,0:T(8,128)(2,1)S(1)} %get-tuple-element.17), channel_id=1, source_target_pairs={{1,0},{2,1},{3,2},{4,3},{5,4},{6,5},{7,6},{8,7},{9,8},{10,9},{11,1... | collective-permute-start | bytes 245768 | tf_op jit(solution)/shard_map/ppermute | solution.py:224
  12.8 32.8 %collective-permute-start = (bf16[528,512]{1,0:T(8,128)(2,1)S(1)}, bf16[528,512]{1,0:T(8,128)(2,1)S(1)}, u32[]{:S(2)}, u32[]{:S(2)}) collective-permute-start(bf16[528,512]{1,0:T(8,128)(2,1)S(1)} %get-tuple-element.15.refs_3_), channel_id=1, source_target_pairs={{0,15},{1,0},{2,1},{3,2},{4,3},{5,4},{6,5},{7,6},{8,7},{9,8},{10,9... | collective-permute-start | bytes 1622024 | tf_op jit(solution)/shard_map/ppermute | solution.py:224
  16.4 40.4 %collective-permute-start.9 = (bf16[1024,512]{1,0:T(8,128)(2,1)S(1)}, bf16[1024,512]{1,0:T(8,128)(2,1)S(1)}, u32[]{:S(2)}, u32[]{:S(2)}) collective-permute-start(bf16[1024,512]{1,0:T(8,128)(2,1)S(1)} %get-tuple-element.21), channel_id=1, source_target_pairs={{0,15},{1,0},{2,1},{3,2},{4,3},{5,4},{6,5},{7,6},{8,7},{9,8},{10,9... | collective-permute-start | bytes 3145736 | tf_op jit(solution)/shard_map/ppermute | solution.py:224
  16.5 42.9 %collective-permute-start.8 = (bf16[1024,512]{1,0:T(8,128)(2,1)S(1)}, bf16[1024,512]{1,0:T(8,128)(2,1)S(1)}, u32[]{:S(2)}, u32[]{:S(2)}) collective-permute-start(bf16[1024,512]{1,0:T(8,128)(2,1)S(1)} %get-tuple-element.20), channel_id=1, source_target_pairs={{0,15},{1,0},{2,1},{3,2},{4,3},{5,4},{6,5},{7,6},{8,7},{9,8},{10,9... | collective-permute-start | bytes 3145736 | tf_op jit(solution)/shard_map/ppermute | solution.py:224
  41.8 8.0 %collective-permute-start.3 = (bf16[80,512]{1,0:T(8,128)(2,1)S(1)}, bf16[80,512]{1,0:T(8,128)(2,1)S(1)}, u32[]{:S(2)}, u32[]{:S(2)}) collective-permute-start(bf16[80,512]{1,0:T(8,128)(2,1)S(1)} %collective-permute-done.2), channel_id=1, source_target_pairs={{2,15},{18,31}} | collective-permute-start | bytes 245768 | tf_op jit(solution)/shard_map/ppermute | solution.py:224
  45.6 18.3 %collective-permute-start.6 = (bf16[688,512]{1,0:T(8,128)(2,1)S(1)}, bf16[688,512]{1,0:T(8,128)(2,1)S(1)}, u32[]{:S(2)}, u32[]{:S(2)}) collective-permute-start(bf16[688,512]{1,0:T(8,128)(2,1)S(1)} %shard_map.42), channel_id=1, source_target_pairs={{0,15},{1,0},{2,1},{3,2},{4,3},{5,4},{6,5},{7,6},{8,7},{9,8},{10,9... | collective-permute-start | bytes 2113544 | tf_op jit(solution)/shard_map/ppermute | solution.py:224
  47.9 14.3 %collective-permute-start.7 = (bf16[256,512]{1,0:T(8,128)(2,1)S(1)}, bf16[256,512]{1,0:T(8,128)(2,1)S(1)}, u32[]{:S(2)}, u32[]{:S(2)}) collective-permute-start(bf16[256,512]{1,0:T(8,128)(2,1)S(1)} %shard_map.41), channel_id=1, source_target_pairs={{1,0},{3,2},{5,4},{7,6},{9,8},{11,10},{13,12},{15,14},{17,16},{19,... | collective-permute-start | bytes 786440 | tf_op jit(solution)/shard_map/ppermute | solution.py:224
  49.8 16.9 %collective-permute-start.5 = (bf16[256,512]{1,0:T(8,128)(2,1)S(1)}, bf16[256,512]{1,0:T(8,128)(2,1)S(1)}, u32[]{:S(2)}, u32[]{:S(2)}) collective-permute-start(bf16[256,512]{1,0:T(8,128)(2,1)S(1)} %shard_map.41), channel_id=1, source_target_pairs={{0,15},{2,1},{4,3},{6,5},{8,7},{10,9},{12,11},{14,13},{16,31},{18,... | collective-permute-start | bytes 786440 | tf_op jit(solution)/shard_map/ppermute | solution.py:224

commit v5 on v3

--- a/solution.py
+++ b/solution.py
@@ -12,6 +12,8 @@
 META_ROWS = 16
 LAST = 7
 MIDDLE = ((1, 2), (2, 4), (4, 6))
+DETOUR = 80
+RELAY = 2
 ANY = pl.BlockSpec(memory_space=pl.ANY)
 HBM = pl.BlockSpec(memory_space=pltpu.HBM)
 SMEM = pl.BlockSpec(memory_space=pltpu.SMEM)
@@ -43,6 +45,7 @@
         table[0, s] = jnp.where(s < next_counts[0], lax.rem(col - here + W + total, total), -1)
         table[1, s] = find(cols, counts, col)
     table[0, next_cols.shape[1]] = lax.rem(here, 2)
+    table[1, next_cols.shape[1]] = here
 
     def job(k):
         col = lax.rem(here + k - W + total, total)
@@ -108,33 +111,79 @@
             out_copy(t).wait()
 
 
-def late_kernel(first_slot, jobs, table, own, chunk, near, band, out, base, out_v, sems):
+def rest_kernel(last_device, first_slot, jobs, table, own, chunk, direct, detour, band, out, rest, out_v, sems):
+    @pl.when(table[1, LAST + 1] == last_device)
+    def _():
+        rest[...] = detour[...]
+
+    @pl.when(table[1, LAST + 1] != last_device)
+    def _():
+        rest[...] = direct[...]
+
     chunk_kernel(first_slot, jobs, table, own, chunk, band, out, out_v, sems)
-    rows = own.shape[1]
-    upper = near.shape[0]
-
-    @pl.when(table[0, LAST] >= 0)
-    def _():
-        f = table[1, LAST]
-        base[...] = dot(own[1, :, upper:], chunk[jobs * rows :])
-
-        @pl.when(f >= 0)
-        def _():
-            base[...] += dot(own[0], own[f])
-
-        @pl.when(table[0, LAST + 1] == 0)
-        def _():
-            out_v[jobs] = (base[...] + dot(own[1, :, :upper], near[...])).astype(out_v.dtype)
-            copy = pltpu.make_async_copy(out_v.at[jobs], out.at[0, table[0, LAST]], sems.at[jobs])
-            copy.start()
-            copy.wait()
-
-
-def last_kernel(table, own, chunk, base, band, out, out_v, sem):
-    @pl.when((table[0, LAST] >= 0) & (table[0, LAST + 1] == 1))
-    def _():
-        out_v[...] = (base[...] + dot(own[1, :, : chunk.shape[0]], chunk[...])).astype(out_v.dtype)
-        copy = pltpu.make_async_copy(out_v, out.at[0, table[0, LAST]], sem)
+
+
+def base_kernel(first_slot, jobs, table, own, chunk, band, out, base, out_v, sems):
+    f = table[1, LAST]
+
+    @pl.when(f >= 0)
+    def _():
+        base[...] = dot(own[0], own[f])
+
+    @pl.when(f < 0)
+    def _():
+        base[...] = jnp.zeros(base.shape, base.dtype)
+
+    chunk_kernel(first_slot, jobs, table, own, chunk, band, out, out_v, sems)
+
+
+def late_kernel(table, own, chunk, rest, near, base, band, out, low, left_v, out_v, sems):
+    rows, half = left_v.shape
+    fold = low.shape[0]
+    k, k_last = table[0, LAST - 1], table[0, LAST]
+    even = table[0, LAST + 1] == 0
+
+    def tile(j):
+        return pltpu.make_async_copy(out_v.at[j], out.at[0, table[0, LAST - 1 + j]], sems.at[j])
+
+    left_copy = pltpu.make_async_copy(left_v, out.at[0, k_last, :, pl.ds(0, half)], sems.at[2])
+
+    @pl.when(k >= 0)
+    def _():
+        finish(table, own, lambda: chunk[:rows], LAST - 1, out_v, 0)
+        tile(0).start()
+
+    @pl.when((k_last >= 0) & jnp.logical_not(even))
+    def _():
+        low[: fold - DETOUR] = chunk[rows:]
+        low[fold - DETOUR :] = rest[...]
+        left = dot(own[1, :, :fold], low[:, :half]) + dot(own[1, :, fold:], low[:, half:])
+        left_v[...] = (base[:, :half] + left).astype(left_v.dtype)
+        left_copy.start()
+        left_copy.wait()
+
+    @pl.when((k_last >= 0) & even)
+    def _():
+        out_v[1] = (base[...] + dot(own[1], near[...])).astype(out_v.dtype)
+        tile(1).start()
+        tile(1).wait()
+
+    @pl.when(k >= 0)
+    def _():
+        tile(0).wait()
+
+
+def last_kernel(table, own, chunk, base, band, out, places, out_v, sems):
+    fetch = pltpu.make_async_copy(table, places, sems.at[0])
+    fetch.start()
+    half = chunk.shape[1]
+    out_v[...] = (base[:, half:] + dot(own[1], chunk[...])).astype(out_v.dtype)
+    fetch.wait()
+    k = places[0, LAST]
+
+    @pl.when((k >= 0) & (places[0, LAST + 1] == 1))
+    def _():
+        copy = pltpu.make_async_copy(out_v, out.at[0, k, :, pl.ds(half, half)], sems.at[1])
         copy.start()
         copy.wait()
 
@@ -142,25 +191,27 @@
 def pack_kernel(pieces, noted, *refs):
     cols, counts, own, _ = refs[:4]
     parts, sem = refs[4:-1], refs[-1]
-    lanes = own.shape[2]
     copies = []
-    ends = []
     for of_part, part in zip(pieces, parts):
-        at = 0
-        for slot, row, rows in of_part:
-            copies.append(pltpu.make_async_copy(own.at[slot, pl.ds(row, rows)], part.at[pl.ds(at, rows)], sem.at[len(copies)]))
-            at += rows
-        ends.append(at)
+        for slot, row, rows, lane, lanes, to_row, to_lane in of_part:
+            copies.append(
+                pltpu.make_async_copy(
+                    own.at[slot, pl.ds(row, rows), pl.ds(lane, lanes)],
+                    part.at[pl.ds(to_row, rows), pl.ds(to_lane, lanes)],
+                    sem.at[len(copies)],
+                )
+            )
     for copy in copies:
         copy.start()
     if noted:
+        size, lanes = parts[0].shape
         lane = lax.broadcasted_iota(jnp.int32, (META_ROWS, lanes), 1)
         note = jnp.zeros((META_ROWS, lanes), jnp.int32)
         slots = cols.shape[1]
         for s in range(slots):
             note = jnp.where(lane == s, cols[0, s], note)
         note = jnp.where(lane == slots, counts[0], note)
-        parts[0][pl.ds(ends[0], META_ROWS)] = note.astype(jnp.float32).astype(parts[0].dtype)
+        parts[0][pl.ds(size - META_ROWS, META_ROWS)] = note.astype(jnp.float32).astype(parts[0].dtype)
     for copy in copies:
         copy.wait()
 
@@ -170,18 +221,19 @@
 
 
 def pack(pieces, noted, cols, counts, own, after):
-    lanes = own.shape[2]
-    sizes = [sum(rows for _, _, rows in of_part) for of_part in pieces]
+    shapes = []
+    for of_part in pieces:
+        shapes.append((max(p[5] + p[2] for p in of_part), max(p[6] + p[4] for p in of_part)))
     if noted:
-        sizes[0] += META_ROWS
+        shapes[0] = (shapes[0][0] + META_ROWS, shapes[0][1])
     return pl.pallas_call(
         functools.partial(pack_kernel, pieces, noted),
-        out_shape=[jax.ShapeDtypeStruct((size, lanes), own.dtype) for size in sizes],
+        out_shape=[jax.ShapeDtypeStruct(shape, own.dtype) for shape in shapes],
         in_specs=[SMEM] * 2 + [HBM, ANY],
-        out_specs=[VMEM] * len(sizes),
+        out_specs=[VMEM] * len(shapes),
         scratch_shapes=[pltpu.SemaphoreType.DMA((sum(map(len, pieces)),))],
         compiler_params=params(),
-        cost_estimate=pl.CostEstimate(flops=0, bytes_accessed=8 * sum(sizes) * lanes, transcendentals=0),
+        cost_estimate=pl.CostEstimate(flops=0, bytes_accessed=8 * sum(a * b for a, b in shapes), transcendentals=0),
     )(cols, counts, pltpu.with_memory_space_constraint(own, pltpu.HBM), after)
 
 
@@ -213,18 +265,27 @@
     tile = lambda *n: pltpu.VMEM(n + (rows, lanes), own.dtype)
     sems = lambda *n: pltpu.SemaphoreType.DMA(n)
 
-    whole = lambda a, b: tuple((s, 0, rows) for s in range(a, b))
-    upper = rows // 2
+    half, fold = lanes // 2, rows // 2
+    whole = lambda a, b: tuple((s, 0, rows, 0, lanes, (s - a) * rows, 0) for s in range(a, b))
+    folded = lambda a, b, at: tuple((LAST, j * fold + a, b - a, 0, half, at, j * half) for j in range(2))
 
     first = own[0]
     head = send(first)
-    (one,) = pack([whole(1, 2)], True, tile_cols, tile_counts, own, first)
+    one, end = pack([whole(1, 2), folded(fold - DETOUR, fold, 0)], True, tile_cols, tile_counts, own, first)
     two, three, local = pack([whole(*MIDDLE[1]), whole(*MIDDLE[2]), whole(0, slots)], False, tile_cols, tile_counts, own, one)
-    (four,) = pack([whole(LAST - 1, LAST) + ((LAST, upper, rows - upper),)], False, tile_cols, tile_counts, own, head)
+    (four,) = pack([whole(LAST - 1, LAST) + folded(0, fold - DETOUR, rows)], False, tile_cols, tile_counts, own, head)
     chunks = [send(part) for part in (one, two, three)]
-    (five,) = pack([((LAST, 0, upper),)], False, tile_cols, tile_counts, own, chunks[0])
+    five, seven = pack([((LAST, 0, rows, half, half, 0, 0),), whole(LAST, LAST + 1)], False, tile_cols, tile_counts, own, chunks[0])
     late = send(four)
-    near = send(five, pairs[1::2])
+    groups = lax.axis_size("groups")
+    across = [(g * total, (g ^ 1 if groups % 2 == 0 else g) * total) for g in range(groups)]
+    both = lambda value, some: lax.ppermute(value, ("groups", "wide"), some)
+    direct = both(
+        end,
+        [(g + a, g + b) for g, _ in across for a, b in pairs[2::2]] + [(g, h + RELAY) for g, h in across],
+    )
+    detour = both(direct, [(h + RELAY, g + total - 1) for g, h in across])
+    near = send(seven, pairs[1::2])
     far = send(five, pairs[0::2])
     local = local.reshape(own.shape)
 
@@ -236,18 +297,31 @@
         [SMEM] * 4 + [VMEM, ANY], [tile(WIDTH), sems(WIDTH)],
         [jax.ShapeDtypeStruct((2, slots + 1), jnp.int32)], [SMEM], own=own,
     )
-    for (a, b), chunk in zip(MIDDLE, chunks):
-        (band,) = call(
-            functools.partial(chunk_kernel, a, b - a), b - a,
-            (table, local, chunk, band), [SMEM] + [VMEM] * 2 + [ANY], [tile(b - a), sems(b - a)], own=own,
-        )
+    a, b = MIDDLE[0]
+    (band,) = call(
+        functools.partial(chunk_kernel, a, b - a), b - a,
+        (table, local, chunks[0], band), [SMEM] + [VMEM] * 2 + [ANY], [tile(b - a), sems(b - a)], own=own,
+    )
+    a, b = MIDDLE[1]
+    band, rest = call(
+        functools.partial(rest_kernel, total - 1, a, b - a), b - a,
+        (table, local, chunks[1], direct, detour, band), [SMEM] + [VMEM] * 4 + [ANY], [tile(b - a), sems(b - a)],
+        [jax.ShapeDtypeStruct(end.shape, own.dtype)], [VMEM], own=own,
+    )
+    a, b = MIDDLE[2]
     band, base = call(
-        functools.partial(late_kernel, LAST - 1, 1), 2,
-        (table, local, late, near, band), [SMEM] + [VMEM] * 3 + [ANY], [tile(2), sems(2)],
+        functools.partial(base_kernel, a, b - a), b - a,
+        (table, local, chunks[2], band), [SMEM] + [VMEM] * 2 + [ANY], [tile(b - a), sems(b - a)],
         [jax.ShapeDtypeStruct((rows, lanes), jnp.float32)], [VMEM], own=own,
     )
+    side = pltpu.VMEM((rows, half), own.dtype)
     (band,) = call(
-        last_kernel, 1, (table, local, far, base, band), [SMEM] + [VMEM] * 3 + [ANY], [tile(), sems()], own=own,
+        late_kernel, 2, (table, local, late, rest, near, base, band), [SMEM] + [VMEM] * 5 + [ANY],
+        [pltpu.VMEM((fold, lanes), own.dtype), side, tile(2), sems(3)], own=own,
+    )
+    (band,) = call(
+        last_kernel, 1, (table, local, far, base, band), [VMEM] * 4 + [ANY],
+        [pltpu.SMEM(table.shape, table.dtype), side, sems(2)], own=own,
     )
     return band
 

time: 53.7 us -> 52.8 us (0.983)
  waiting for transfers between devices: 12.8 us -> 8.81 us
  starting transfers between devices: 16.2 us -> 18.2 us
  Pallas kernels: 21.2 us -> 22.3 us
    ppermute x7, waiting for transfers between devices: 12.8 us -> 8.81 us  [per_device(): send = lambda value, some=pairs: lax.ppermute(value, 'wide', some)]
    ppermute x0 -> x2, starting transfers between devices: none -> 1.95 us  [per_device(): both = lambda value, some: lax.ppermute(value, ('groups', 'wide'), some)]
    pallas_call x7, Pallas kernels: 12.9 us -> 13.8 us  [call(): pl.pallas_call(kernel, out_shape=[band, *extra], in_specs=spaces, out_spe...]
  transfers between devices with their start and end apart: 7 -> 9, of which waited for: 3 -> 3; matrix products, arithmetic and copies ran while one was open for 1% -> 1% of each run, Pallas kernels for 39% -> 41%
where the time goes in v5:
time: 52.8 us; the launch traced here: 52.5 us
  Pallas kernels  22.3 us (42%)
  starting transfers between devices  18.2 us (34%)
  waiting for transfers between devices  8.81 us (17%)
  local copies, waits for them, and re-layouts  2.35 us (4%)
  between operations  0.83 us (2%)
    ppermute x7, starting transfers between devices, per_device(): send = lambda value, some=pairs: lax.ppermute(value, 'wide', some)  16.3 us
    pallas_call x7, Pallas kernels, call(): pl.pallas_call(kernel, out_shape=[band, *extra], in_specs=spaces, out_spe...  13.8 us
    ppermute x7, waiting for transfers between devices, per_device(): send = lambda value, some=pairs: lax.ppermute(value, 'wide', some)  8.81 us
    pallas_call x4, Pallas kernels, pack(): pl.pallas_call(functools.partial(pack_kernel, pieces, noted), out_shape=[...  8.45 us
    ppermute x2, starting transfers between devices, per_device(): both = lambda value, some: lax.ppermute(value, ('groups', 'wide'), some)  1.95 us
    squeeze x1, local copies, waits for them, and re-layouts, per_device(): first = own[0]  1.09 us
  transfers between devices with their start and end apart: 9, of which 3 were waited for; matrix products, arithmetic and copies ran while one was open for 1% of the time, Pallas kernels for 41%

profile of v5, /device:TPU:0, one launch (start us, length us, event | category | flops | bytes accessed | tf_op | source)
XLA Modules:
  0.0 52.5 jit_solution(12625346161609821703)
XLA Ops:
  0.0 0.0 copy-start.1
  0.0 1.1 %slice_bitcast_fusion.refs_3_ = bf16[512,512]{1,0:T(8,128)(2,1)S(1)} fusion(bf16[8,512,512]{2,1,0:T(8,128)(2,1)} %refs_2_.7), kind=kLoop, calls=%fused_computation | loop fusion | bytes 1048576 | tf_op jit(solution)/shard_map/squeeze | solution.py:272
  1.1 5.5 %collective-permute-start.1 = (bf16[512,512]{1,0:T(8,128)(2,1)S(1)}, bf16[512,512]{1,0:T(8,128)(2,1)S(1)}, u32[]{:S(2)}, u32[]{:S(2)}) collective-permute-start(bf16[512,512]{1,0:T(8,128)(2,1)S(1)} %slice_bitcast_fusion.refs_3_), channel_id=1, source_target_pairs={{0,15},{1,0},{2,1},{3,2},{4,3},{5,4},{6,5},{7,6},{8,7},{9,8},{10,9... | collective-permute-start | bytes 1572872 | tf_op jit(solution)/shard_map/ppermute | solution.py:264
  7.2 0.0 copy-start
  7.3 0.6 %copy-done = s32[1,8]{1,0:T(1,128)S(1)} copy-done((s32[1,8]{1,0:T(1,128)S(1)}, s32[1,8]{1,0:T(1,128)}, u32[]{:S(2)}) %copy-start) | copy-done | bytes 56
  7.9 1.6 %shard_map.37 = (bf16[528,512]{1,0:T(8,128)(2,1)S(1)}, bf16[80,512]{1,0:T(8,128)(2,1)S(1)}) custom-call(s32[1,8]{1,0:T(1,128)S(1)} %copy-done, s32[1]{0:T(128)S(6)} %copy.16.refs_1_.counts, bf16[8,512,512]{2,1,0:T(8,128)(2,1)} %refs_2_.7, bf16[512,512]{1,0:T(8,128)(2,1)S(1)} %slice_bitcast_fusion.refs_3_), custom_call_target="tpu_custom_call" | custom-call | bytes 2490368 | tf_op jit(solution)/shard_map/pallas_call | solution.py:229
  9.5 1.3 %collective-permute-start.5 = (bf16[80,512]{1,0:T(8,128)(2,1)S(1)}, bf16[80,512]{1,0:T(8,128)(2,1)S(1)}, u32[]{:S(2)}, u32[]{:S(2)}) collective-permute-start(bf16[80,512]{1,0:T(8,128)(2,1)S(1)} %get-tuple-element.24), channel_id=1, source_target_pairs={{2,1},{4,3},{6,5},{8,7},{10,9},{12,11},{14,13},{18,17},{20,19},{22... | collective-permute-start | bytes 245768 | tf_op jit(solution)/shard_map/ppermute | solution.py:282
  10.8 0.1 collective-permute-start
  10.9 3.5 %shard_map.38 = (bf16[1024,512]{1,0:T(8,128)(2,1)S(1)}, bf16[1024,512]{1,0:T(8,128)(2,1)S(1)}, bf16[4096,512]{1,0:T(8,128)(2,1)S(1)}) custom-call(s32[1,8]{1,0:T(1,128)S(1)} %copy-done, s32[1]{0:T(128)S(6)} %copy.16.refs_1_.counts, bf16[8,512,512]{2,1,0:T(8,128)(2,1)} %refs_2_.7, bf16[528,512]{1,0:T(8,128)(2,1)S(1)} %get-tuple-element.18.refs_3_), custom_call_target="tpu_custom_call" | custom-call | bytes 25165824 | tf_op jit(solution)/shard_map/pallas_call | solution.py:229
  14.5 1.9 %collective-permute-start.4 = (bf16[1024,512]{1,0:T(8,128)(2,1)S(1)}, bf16[1024,512]{1,0:T(8,128)(2,1)S(1)}, u32[]{:S(2)}, u32[]{:S(2)}) collective-permute-start(bf16[1024,512]{1,0:T(8,128)(2,1)S(1)} %get-tuple-element.23), channel_id=1, source_target_pairs={{0,15},{1,0},{2,1},{3,2},{4,3},{5,4},{6,5},{7,6},{8,7},{9,8},{10,9... | collective-permute-start | bytes 3145736 | tf_op jit(solution)/shard_map/ppermute | solution.py:264
  16.4 0.1 collective-permute-start.3
  16.4 0.0 collective-permute-done.5.direct
  16.4 0.7 %collective-permute-start.6 = (bf16[80,512]{1,0:T(8,128)(2,1)S(1)}, bf16[80,512]{1,0:T(8,128)(2,1)S(1)}, u32[]{:S(2)}, u32[]{:S(2)}) collective-permute-start(bf16[80,512]{1,0:T(8,128)(2,1)S(1)} %collective-permute-done.5.direct), channel_id=1, source_target_pairs={{18,15},{2,31}} | collective-permute-start | bytes 245768 | tf_op jit(solution)/shard_map/ppermute | solution.py:282
  17.1 0.0 collective-permute-done.1.head.refs_3_
  17.1 0.0 copy-done.1
  17.1 1.6 %shard_map.45 = bf16[688,512]{1,0:T(8,128)(2,1)S(1)} custom-call(s32[1,8]{1,0:T(1,128)S(1)} %copy-done.1, s32[1]{0:T(128)S(6)} %copy.16.refs_1_.counts, bf16[8,512,512]{2,1,0:T(8,128)(2,1)} %refs_2_.7, bf16[512,512]{1,0:T(8,128)(2,1)S(1)} %collective-permute-done.1.head.refs_3_), custom_call_target="tpu_custom_call" | custom-call | bytes 2818048 | tf_op jit(solution)/shard_map/pallas_call | solution.py:229
  18.8 2.1 %collective-permute-start.7 = (bf16[688,512]{1,0:T(8,128)(2,1)S(1)}, bf16[688,512]{1,0:T(8,128)(2,1)S(1)}, u32[]{:S(2)}, u32[]{:S(2)}) collective-permute-start(bf16[688,512]{1,0:T(8,128)(2,1)S(1)} %shard_map.45), channel_id=1, source_target_pairs={{0,15},{1,0},{2,1},{3,2},{4,3},{5,4},{6,5},{7,6},{8,7},{9,8},{10,9... | collective-permute-start | bytes 2113544 | tf_op jit(solution)/shard_map/ppermute | solution.py:264
  20.9 1.5 %shard_map.39.band = bf16[1,10,512,512]{3,2,1,0:T(8,128)(2,1)} custom-call(bf16[8,512,512]{2,1,0:T(8,128)(2,1)S(1)} %bitcast.5, bf16[512,512]{1,0:T(8,128)(2,1)S(1)} %collective-permute-done.1.head.refs_3_), custom_call_target="tpu_custom_call" | custom-call | flops 6442450944 | bytes 6291456 | tf_op jit(solution)/shard_map/pallas_call | solution.py:245
  22.4 0.0 collective-permute-done.refs_3_.chunk
  22.4 0.6 %slice.19 = s32[1,1]{1,0:T(1,128)} slice(s32[1,9]{1,0:T(1,128)S(1)} %slice_convert_fusion), slice={[0:1], [8:9]} | slice | bytes 8 | tf_op jit(solution)/shard_map/slice | solution.py:296
  23.0 1.7 %shard_map.41 = (bf16[512,256]{1,0:T(8,128)(2,1)S(1)}, bf16[512,512]{1,0:T(8,128)(2,1)S(1)}) custom-call(s32[1,8]{1,0:T(1,128)S(1)} %copy-done.1, s32[1]{0:T(128)S(6)} %copy.16.refs_1_.counts, bf16[8,512,512]{2,1,0:T(8,128)(2,1)} %refs_2_.7, bf16[528,512]{1,0:T(8,128)(2,1)S(1)} %collective-permute-done.refs_3_.chunk), custom_call_target="tpu_custom_call" | custom-call | bytes 3145728 | tf_op jit(solution)/shard_map/pallas_call | solution.py:229
  24.7 1.3 %collective-permute-start.8 = (bf16[512,512]{1,0:T(8,128)(2,1)S(1)}, bf16[512,512]{1,0:T(8,128)(2,1)S(1)}, u32[]{:S(2)}, u32[]{:S(2)}) collective-permute-start(bf16[512,512]{1,0:T(8,128)(2,1)S(1)} %get-tuple-element.29), channel_id=1, source_target_pairs={{1,0},{3,2},{5,4},{7,6},{9,8},{11,10},{13,12},{15,14},{17,16},{19,... | collective-permute-start | bytes 1572872 | tf_op jit(solution)/shard_map/ppermute | solution.py:264
  26.0 3.5 %shard_map.40 = (bf16[1,10,512,512]{3,2,1,0:T(8,128)(2,1)}, s32[2,9]{1,0:T(2,128)S(1)}) custom-call(s32[1,8]{1,0:T(1,128)S(1)} %copy-done.1, s32[1]{0:T(128)S(6)} %copy.16.refs_1_.counts, s32[1,8]{1,0:T(1,128)S(1)} %bitcast.12, s32[1]{0:T(128)} %bitcast.1.next_counts, bf16[8,512,512]{2,1,0:T(8,128)(2,1)S(1)} %bitcast.6, ...), custom_call_target="tpu_custom_call", output_to_operand_aliasing={{0}: (5, {})} | custom-call | flops 16106127360 | bytes 15728640 | tf_op jit(solution)/shard_map/pallas_call | solution.py:245
  29.5 1.8 %shard_map.42.band = bf16[1,10,512,512]{3,2,1,0:T(8,128)(2,1)} custom-call(s32[2,9]{1,0:T(2,128)S(1)} %get-tuple-element.20.table, bf16[8,512,512]{2,1,0:T(8,128)(2,1)S(1)} %bitcast.7, bf16[528,512]{1,0:T(8,128)(2,1)S(1)} %collective-permute-done.refs_3_.chunk, bf16[1,10,512,512]{3,2,1,0:T(8,128)(2,1)} %get-tuple-element.25.band), custom_call_target="tpu_custom_call", output_to_operand_aliasing={{}: (3, {})} | custom-call | flops 536870912 | bytes 524288 | tf_op jit(solution)/shard_map/pallas_call | solution.py:245
  31.3 0.0 collective-permute-done.6.detour
  31.3 5.3 %collective-permute-start.2 = (bf16[512,256]{1,0:T(8,128)(2,1)S(1)}, bf16[512,256]{1,0:T(8,128)(2,1)S(1)}, u32[]{:S(2)}, u32[]{:S(2)}) collective-permute-start(bf16[512,256]{1,0:T(8,128)(2,1)S(1)} %get-tuple-element.21), channel_id=1, source_target_pairs={{0,15},{2,1},{4,3},{6,5},{8,7},{10,9},{12,11},{14,13},{16,31},{18,... | collective-permute-start | bytes 786440 | tf_op jit(solution)/shard_map/ppermute | solution.py:264
  36.6 0.0 collective-permute-done.4.chunk
  36.6 2.3 %shard_map.43 = (bf16[1,10,512,512]{3,2,1,0:T(8,128)(2,1)}, bf16[80,512]{1,0:T(8,128)(2,1)S(1)}) custom-call(s32[2,9]{1,0:T(2,128)S(1)} %get-tuple-element.20.table, bf16[8,512,512]{2,1,0:T(8,128)(2,1)S(1)} %bitcast.8, bf16[1024,512]{1,0:T(8,128)(2,1)S(1)} %collective-permute-done.4.chunk, ...), custom_call_target="tpu_custom_call", output_to_operand_aliasing={{0}: (5, {})} | custom-call | flops 1073741824 | bytes 1048576 | tf_op jit(solution)/shard_map/pallas_call | solution.py:245
  38.9 2.6 %collective-permute-done.3.chunk = bf16[1024,512]{1,0:T(8,128)(2,1)S(1)} collective-permute-done((bf16[1024,512]{1,0:T(8,128)(2,1)S(1)}, bf16[1024,512]{1,0:T(8,128)(2,1)S(1)}, u32[]{:S(2)}, u32[]{:S(2)}) %collective-permute-start.3) | collective-permute-done | bytes 1048608 | tf_op jit(solution)/shard_map/ppermute | solution.py:264
  41.6 2.4 %shard_map.44 = (bf16[1,10,512,512]{3,2,1,0:T(8,128)(2,1)}, f32[512,512]{1,0:T(8,128)S(1)}) custom-call(s32[2,9]{1,0:T(2,128)S(1)} %get-tuple-element.20.table, bf16[8,512,512]{2,1,0:T(8,128)(2,1)S(1)} %bitcast.9, bf16[1024,512]{1,0:T(8,128)(2,1)S(1)} %collective-permute-done.3.chunk, ...), custom_call_target="tpu_custom_call", output_to_operand_aliasing={{0}: (3, {})} | custom-call | flops 1073741824 | bytes 1048576 | tf_op jit(solution)/shard_map/pallas_call | solution.py:245
  43.9 0.0 collective-permute-done.8.near
  43.9 5.2 %collective-permute-done.7.chunk = bf16[688,512]{1,0:T(8,128)(2,1)S(1)} collective-permute-done((bf16[688,512]{1,0:T(8,128)(2,1)S(1)}, bf16[688,512]{1,0:T(8,128)(2,1)S(1)}, u32[]{:S(2)}, u32[]{:S(2)}) %collective-permute-start.7) | collective-permute-done | bytes 704544 | tf_op jit(solution)/shard_map/ppermute | solution.py:264
  49.1 1.8 %shard_map.46.band = bf16[1,10,512,512]{3,2,1,0:T(8,128)(2,1)} custom-call(s32[2,9]{1,0:T(2,128)S(1)} %get-tuple-element.20.table, bf16[8,512,512]{2,1,0:T(8,128)(2,1)S(1)} %bitcast.10, bf16[688,512]{1,0:T(8,128)(2,1)S(1)} %collective-permute-done.7.chunk, bf16[80,512]{1,0:T(8,128)(2,1)S(1)} %get-tuple-element.28.rest, ...), custom_call_target="tpu_custom_call", output_to_operand_aliasing={{}: (6, {})} | custom-call | flops 1073741824 | bytes 1048576 | tf_op jit(solution)/shard_map/pallas_call | solution.py:245
  50.9 1.0 %collective-permute-done.2.chunk = bf16[512,256]{1,0:T(8,128)(2,1)S(1)} collective-permute-done((bf16[512,256]{1,0:T(8,128)(2,1)S(1)}, bf16[512,256]{1,0:T(8,128)(2,1)S(1)}, u32[]{:S(2)}, u32[]{:S(2)}) %collective-permute-start.2) | collective-permute-done | bytes 262176 | tf_op jit(solution)/shard_map/ppermute | solution.py:264
  51.9 0.6 %shard_map.47 = bf16[1,10,512,512]{3,2,1,0:T(8,128)(2,1)} custom-call(s32[2,9]{1,0:T(2,128)S(1)} %get-tuple-element.20.table, bf16[8,512,512]{2,1,0:T(8,128)(2,1)S(1)} %bitcast.11, bf16[512,256]{1,0:T(8,128)(2,1)S(1)} %collective-permute-done.2.chunk, f32[512,512]{1,0:T(8,128)S(1)} %get-tuple-element.27.base, ...), custom_call_target="tpu_custom_call", output_to_operand_aliasing={{}: (4, {})} | custom-call | flops 536870912 | bytes 524288 | tf_op jit(solution)/shard_map/pallas_call | solution.py:245
  (1 shorter events, 0.0 us)
Async XLA Ops:
  0.0 17.1 %copy-start.1 = (s32[1,8]{1,0:T(1,128)S(1)}, s32[1,8]{1,0:T(1,128)}, u32[]{:S(2)}) copy-start(s32[1,8]{1,0:T(1,128)} %refs_0_.7) | copy-start | bytes 100
  1.1 16.0 %collective-permute-start.1 = (bf16[512,512]{1,0:T(8,128)(2,1)S(1)}, bf16[512,512]{1,0:T(8,128)(2,1)S(1)}, u32[]{:S(2)}, u32[]{:S(2)}) collective-permute-start(bf16[512,512]{1,0:T(8,128)(2,1)S(1)} %slice_bitcast_fusion.refs_3_), channel_id=1, source_target_pairs={{0,15},{1,0},{2,1},{3,2},{4,3},{5,4},{6,5},{7,6},{8,7},{9,8},{10,9... | collective-permute-start | bytes 1572872 | tf_op jit(solution)/shard_map/ppermute | solution.py:264
  7.2 0.7 %copy-start = (s32[1,8]{1,0:T(1,128)S(1)}, s32[1,8]{1,0:T(1,128)}, u32[]{:S(2)}) copy-start(s32[1,8]{1,0:T(1,128)} %refs_0_.7) | copy-start | bytes 100
  9.5 6.9 %collective-permute-start.5 = (bf16[80,512]{1,0:T(8,128)(2,1)S(1)}, bf16[80,512]{1,0:T(8,128)(2,1)S(1)}, u32[]{:S(2)}, u32[]{:S(2)}) collective-permute-start(bf16[80,512]{1,0:T(8,128)(2,1)S(1)} %get-tuple-element.24), channel_id=1, source_target_pairs={{2,1},{4,3},{6,5},{8,7},{10,9},{12,11},{14,13},{18,17},{20,19},{22... | collective-permute-start | bytes 245768 | tf_op jit(solution)/shard_map/ppermute | solution.py:282
  10.8 11.6 %collective-permute-start = (bf16[528,512]{1,0:T(8,128)(2,1)S(1)}, bf16[528,512]{1,0:T(8,128)(2,1)S(1)}, u32[]{:S(2)}, u32[]{:S(2)}) collective-permute-start(bf16[528,512]{1,0:T(8,128)(2,1)S(1)} %get-tuple-element.18.refs_3_), channel_id=1, source_target_pairs={{0,15},{1,0},{2,1},{3,2},{4,3},{5,4},{6,5},{7,6},{8,7},{9,8},{10,9... | collective-permute-start | bytes 1622024 | tf_op jit(solution)/shard_map/ppermute | solution.py:264
  14.5 22.2 %collective-permute-start.4 = (bf16[1024,512]{1,0:T(8,128)(2,1)S(1)}, bf16[1024,512]{1,0:T(8,128)(2,1)S(1)}, u32[]{:S(2)}, u32[]{:S(2)}) collective-permute-start(bf16[1024,512]{1,0:T(8,128)(2,1)S(1)} %get-tuple-element.23), channel_id=1, source_target_pairs={{0,15},{1,0},{2,1},{3,2},{4,3},{5,4},{6,5},{7,6},{8,7},{9,8},{10,9... | collective-permute-start | bytes 3145736 | tf_op jit(solution)/shard_map/ppermute | solution.py:264
  16.4 25.2 %collective-permute-start.3 = (bf16[1024,512]{1,0:T(8,128)(2,1)S(1)}, bf16[1024,512]{1,0:T(8,128)(2,1)S(1)}, u32[]{:S(2)}, u32[]{:S(2)}) collective-permute-start(bf16[1024,512]{1,0:T(8,128)(2,1)S(1)} %get-tuple-element.22), channel_id=1, source_target_pairs={{0,15},{1,0},{2,1},{3,2},{4,3},{5,4},{6,5},{7,6},{8,7},{9,8},{10,9... | collective-permute-start | bytes 3145736 | tf_op jit(solution)/shard_map/ppermute | solution.py:264
  16.4 14.9 %collective-permute-start.6 = (bf16[80,512]{1,0:T(8,128)(2,1)S(1)}, bf16[80,512]{1,0:T(8,128)(2,1)S(1)}, u32[]{:S(2)}, u32[]{:S(2)}) collective-permute-start(bf16[80,512]{1,0:T(8,128)(2,1)S(1)} %collective-permute-done.5.direct), channel_id=1, source_target_pairs={{18,15},{2,31}} | collective-permute-start | bytes 245768 | tf_op jit(solution)/shard_map/ppermute | solution.py:282
  18.8 30.3 %collective-permute-start.7 = (bf16[688,512]{1,0:T(8,128)(2,1)S(1)}, bf16[688,512]{1,0:T(8,128)(2,1)S(1)}, u32[]{:S(2)}, u32[]{:S(2)}) collective-permute-start(bf16[688,512]{1,0:T(8,128)(2,1)S(1)} %shard_map.45), channel_id=1, source_target_pairs={{0,15},{1,0},{2,1},{3,2},{4,3},{5,4},{6,5},{7,6},{8,7},{9,8},{10,9... | collective-permute-start | bytes 2113544 | tf_op jit(solution)/shard_map/ppermute | solution.py:264
  24.7 19.2 %collective-permute-start.8 = (bf16[512,512]{1,0:T(8,128)(2,1)S(1)}, bf16[512,512]{1,0:T(8,128)(2,1)S(1)}, u32[]{:S(2)}, u32[]{:S(2)}) collective-permute-start(bf16[512,512]{1,0:T(8,128)(2,1)S(1)} %get-tuple-element.29), channel_id=1, source_target_pairs={{1,0},{3,2},{5,4},{7,6},{9,8},{11,10},{13,12},{15,14},{17,16},{19,... | collective-permute-start | bytes 1572872 | tf_op jit(solution)/shard_map/ppermute | solution.py:264
  31.3 20.6 %collective-permute-start.2 = (bf16[512,256]{1,0:T(8,128)(2,1)S(1)}, bf16[512,256]{1,0:T(8,128)(2,1)S(1)}, u32[]{:S(2)}, u32[]{:S(2)}) collective-permute-start(bf16[512,256]{1,0:T(8,128)(2,1)S(1)} %get-tuple-element.21), channel_id=1, source_target_pairs={{0,15},{2,1},{4,3},{6,5},{8,7},{10,9},{12,11},{14,13},{16,31},{18,... | collective-permute-start | bytes 786440 | tf_op jit(solution)/shard_map/ppermute | solution.py:264

commit v6 on v5

--- a/solution.py
+++ b/solution.py
@@ -12,7 +12,7 @@
 META_ROWS = 16
 LAST = 7
 MIDDLE = ((1, 2), (2, 4), (4, 6))
-DETOUR = 80
+DETOUR = 96
 RELAY = 2
 ANY = pl.BlockSpec(memory_space=pl.ANY)
 HBM = pl.BlockSpec(memory_space=pltpu.HBM)
@@ -146,8 +146,6 @@
     def tile(j):
         return pltpu.make_async_copy(out_v.at[j], out.at[0, table[0, LAST - 1 + j]], sems.at[j])
 
-    left_copy = pltpu.make_async_copy(left_v, out.at[0, k_last, :, pl.ds(0, half)], sems.at[2])
-
     @pl.when(k >= 0)
     def _():
         finish(table, own, lambda: chunk[:rows], LAST - 1, out_v, 0)
@@ -159,6 +157,7 @@
         low[fold - DETOUR :] = rest[...]
         left = dot(own[1, :, :fold], low[:, :half]) + dot(own[1, :, fold:], low[:, half:])
         left_v[...] = (base[:, :half] + left).astype(left_v.dtype)
+        left_copy = pltpu.make_async_copy(left_v, out.at[0, k_last, :, pl.ds(0, half)], sems.at[2])
         left_copy.start()
         left_copy.wait()
 

time: 52.8 us -> 52.7 us (level)
  waiting for transfers between devices: 8.81 us -> 13.1 us
  starting transfers between devices: 18.2 us -> 14.8 us
  Pallas kernels: 22.3 us -> 21.2 us
    ppermute x7, waiting for transfers between devices: 8.81 us -> 13.1 us  [per_device(): send = lambda value, some=pairs: lax.ppermute(value, 'wide', some)]
    ppermute x7, starting transfers between devices: 16.3 us -> 12.9 us  [per_device(): send = lambda value, some=pairs: lax.ppermute(value, 'wide', some)]
    pallas_call x7, Pallas kernels: 13.8 us -> 12.8 us  [call(): pl.pallas_call(kernel, out_shape=[band, *extra], in_specs=spaces, out_spe...]
  transfers between devices with their start and end apart: 9 -> 9, of which waited for: 3 -> 3; matrix products, arithmetic and copies ran while one was open for 1% -> 1% of each run, Pallas kernels for 41% -> 39%
where the time goes in v6:
time: 52.7 us; the launch traced here: 52.3 us
  Pallas kernels  21.2 us (40%)
  starting transfers between devices  14.8 us (28%)
  waiting for transfers between devices  13.1 us (25%)
  local copies, waits for them, and re-layouts  2.33 us (4%)
  between operations  0.83 us (2%)
    ppermute x7, waiting for transfers between devices, per_device(): send = lambda value, some=pairs: lax.ppermute(value, 'wide', some)  13.1 us
    ppermute x7, starting transfers between devices, per_device(): send = lambda value, some=pairs: lax.ppermute(value, 'wide', some)  12.9 us
    pallas_call x7, Pallas kernels, call(): pl.pallas_call(kernel, out_shape=[band, *extra], in_specs=spaces, out_spe...  12.8 us
    pallas_call x4, Pallas kernels, pack(): pl.pallas_call(functools.partial(pack_kernel, pieces, noted), out_shape=[...  8.45 us
    ppermute x2, starting transfers between devices, per_device(): both = lambda value, some: lax.ppermute(value, ('groups', 'wide'), some)  1.95 us
    squeeze x1, local copies, waits for them, and re-layouts, per_device(): first = own[0]  1.08 us
  transfers between devices with their start and end apart: 9, of which 3 were waited for; matrix products, arithmetic and copies ran while one was open for 1% of the time, Pallas kernels for 39%

profile of v6, /device:TPU:0, one launch (start us, length us, event | category | flops | bytes accessed | tf_op | source)
XLA Modules:
  0.0 52.3 jit_solution(5684999325655603598)
XLA Ops:
  0.0 1.1 %slice_bitcast_fusion.refs_3_ = bf16[512,512]{1,0:T(8,128)(2,1)S(1)} fusion(bf16[8,512,512]{2,1,0:T(8,128)(2,1)} %refs_2_.7), kind=kLoop, calls=%fused_computation | loop fusion | bytes 1048576 | tf_op jit(solution)/shard_map/squeeze | solution.py:271
  1.1 5.5 %collective-permute-start.1 = (bf16[512,512]{1,0:T(8,128)(2,1)S(1)}, bf16[512,512]{1,0:T(8,128)(2,1)S(1)}, u32[]{:S(2)}, u32[]{:S(2)}) collective-permute-start(bf16[512,512]{1,0:T(8,128)(2,1)S(1)} %slice_bitcast_fusion.refs_3_), channel_id=1, source_target_pairs={{0,15},{1,0},{2,1},{3,2},{4,3},{5,4},{6,5},{7,6},{8,7},{9,8},{10,9... | collective-permute-start | bytes 1572872 | tf_op jit(solution)/shard_map/ppermute | solution.py:263
  7.2 0.0 copy-start
  7.2 0.6 %copy-done = s32[1,8]{1,0:T(1,128)S(1)} copy-done((s32[1,8]{1,0:T(1,128)S(1)}, s32[1,8]{1,0:T(1,128)}, u32[]{:S(2)}) %copy-start) | copy-done | bytes 56
  7.9 1.6 %shard_map.37 = (bf16[528,512]{1,0:T(8,128)(2,1)S(1)}, bf16[96,512]{1,0:T(8,128)(2,1)S(1)}) custom-call(s32[1,8]{1,0:T(1,128)S(1)} %copy-done, s32[1]{0:T(128)S(6)} %copy.16.refs_1_.counts, bf16[8,512,512]{2,1,0:T(8,128)(2,1)} %refs_2_.7, bf16[512,512]{1,0:T(8,128)(2,1)S(1)} %slice_bitcast_fusion.refs_3_), custom_call_target="tpu_custom_call" | custom-call | bytes 2555904 | tf_op jit(solution)/shard_map/pallas_call | solution.py:228
  9.5 1.3 %collective-permute-start.5 = (bf16[96,512]{1,0:T(8,128)(2,1)S(1)}, bf16[96,512]{1,0:T(8,128)(2,1)S(1)}, u32[]{:S(2)}, u32[]{:S(2)}) collective-permute-start(bf16[96,512]{1,0:T(8,128)(2,1)S(1)} %get-tuple-element.24), channel_id=1, source_target_pairs={{2,1},{4,3},{6,5},{8,7},{10,9},{12,11},{14,13},{18,17},{20,19},{22... | collective-permute-start | bytes 294920 | tf_op jit(solution)/shard_map/ppermute | solution.py:281
  10.8 0.1 collective-permute-start
  10.9 3.5 %shard_map.38 = (bf16[1024,512]{1,0:T(8,128)(2,1)S(1)}, bf16[1024,512]{1,0:T(8,128)(2,1)S(1)}, bf16[4096,512]{1,0:T(8,128)(2,1)S(1)}) custom-call(s32[1,8]{1,0:T(1,128)S(1)} %copy-done, s32[1]{0:T(128)S(6)} %copy.16.refs_1_.counts, bf16[8,512,512]{2,1,0:T(8,128)(2,1)} %refs_2_.7, bf16[528,512]{1,0:T(8,128)(2,1)S(1)} %get-tuple-element.18.refs_3_), custom_call_target="tpu_custom_call" | custom-call | bytes 25165824 | tf_op jit(solution)/shard_map/pallas_call | solution.py:228
  14.4 1.9 %collective-permute-start.4 = (bf16[1024,512]{1,0:T(8,128)(2,1)S(1)}, bf16[1024,512]{1,0:T(8,128)(2,1)S(1)}, u32[]{:S(2)}, u32[]{:S(2)}) collective-permute-start(bf16[1024,512]{1,0:T(8,128)(2,1)S(1)} %get-tuple-element.23), channel_id=1, source_target_pairs={{0,15},{1,0},{2,1},{3,2},{4,3},{5,4},{6,5},{7,6},{8,7},{9,8},{10,9... | collective-permute-start | bytes 3145736 | tf_op jit(solution)/shard_map/ppermute | solution.py:263
  16.4 0.1 collective-permute-start.3
  16.4 0.0 collective-permute-done.5.direct
  16.4 0.7 %collective-permute-start.6 = (bf16[96,512]{1,0:T(8,128)(2,1)S(1)}, bf16[96,512]{1,0:T(8,128)(2,1)S(1)}, u32[]{:S(2)}, u32[]{:S(2)}) collective-permute-start(bf16[96,512]{1,0:T(8,128)(2,1)S(1)} %collective-permute-done.5.direct), channel_id=1, source_target_pairs={{18,15},{2,31}} | collective-permute-start | bytes 294920 | tf_op jit(solution)/shard_map/ppermute | solution.py:281
  17.1 0.0 collective-permute-done.1.head.refs_3_
  17.1 1.6 %shard_map.45 = bf16[672,512]{1,0:T(8,128)(2,1)S(1)} custom-call(s32[1,8]{1,0:T(1,128)S(1)} %copy-done, s32[1]{0:T(128)S(6)} %copy.16.refs_1_.counts, bf16[8,512,512]{2,1,0:T(8,128)(2,1)} %refs_2_.7, bf16[512,512]{1,0:T(8,128)(2,1)S(1)} %collective-permute-done.1.head.refs_3_), custom_call_target="tpu_custom_call" | custom-call | bytes 2752512 | tf_op jit(solution)/shard_map/pallas_call | solution.py:228
  18.7 2.1 %collective-permute-start.7 = (bf16[672,512]{1,0:T(8,128)(2,1)S(1)}, bf16[672,512]{1,0:T(8,128)(2,1)S(1)}, u32[]{:S(2)}, u32[]{:S(2)}) collective-permute-start(bf16[672,512]{1,0:T(8,128)(2,1)S(1)} %shard_map.45), channel_id=1, source_target_pairs={{0,15},{1,0},{2,1},{3,2},{4,3},{5,4},{6,5},{7,6},{8,7},{9,8},{10,9... | collective-permute-start | bytes 2064392 | tf_op jit(solution)/shard_map/ppermute | solution.py:263
  20.9 0.0 copy-start.1
  20.9 1.5 %shard_map.39.band = bf16[1,10,512,512]{3,2,1,0:T(8,128)(2,1)} custom-call(bf16[8,512,512]{2,1,0:T(8,128)(2,1)S(1)} %bitcast.5, bf16[512,512]{1,0:T(8,128)(2,1)S(1)} %collective-permute-done.1.head.refs_3_), custom_call_target="tpu_custom_call" | custom-call | flops 6442450944 | bytes 6291456 | tf_op jit(solution)/shard_map/pallas_call | solution.py:244
  22.4 0.0 collective-permute-done.refs_3_.chunk
  22.4 0.6 %slice.19 = s32[1,1]{1,0:T(1,128)} slice(s32[1,9]{1,0:T(1,128)S(1)} %slice_convert_fusion), slice={[0:1], [8:9]} | slice | bytes 8 | tf_op jit(solution)/shard_map/slice | solution.py:295
  23.0 0.0 copy-done.1
  23.0 1.7 %shard_map.41 = (bf16[512,256]{1,0:T(8,128)(2,1)S(1)}, bf16[512,512]{1,0:T(8,128)(2,1)S(1)}) custom-call(s32[1,8]{1,0:T(1,128)S(1)} %copy-done.1, s32[1]{0:T(128)S(6)} %copy.16.refs_1_.counts, bf16[8,512,512]{2,1,0:T(8,128)(2,1)} %refs_2_.7, bf16[528,512]{1,0:T(8,128)(2,1)S(1)} %collective-permute-done.refs_3_.chunk), custom_call_target="tpu_custom_call" | custom-call | bytes 3145728 | tf_op jit(solution)/shard_map/pallas_call | solution.py:228
  24.7 1.3 %collective-permute-start.8 = (bf16[512,512]{1,0:T(8,128)(2,1)S(1)}, bf16[512,512]{1,0:T(8,128)(2,1)S(1)}, u32[]{:S(2)}, u32[]{:S(2)}) collective-permute-start(bf16[512,512]{1,0:T(8,128)(2,1)S(1)} %get-tuple-element.29), channel_id=1, source_target_pairs={{1,0},{3,2},{5,4},{7,6},{9,8},{11,10},{13,12},{15,14},{17,16},{19,... | collective-permute-start | bytes 1572872 | tf_op jit(solution)/shard_map/ppermute | solution.py:263
  26.0 4.7 %shard_map.40 = (bf16[1,10,512,512]{3,2,1,0:T(8,128)(2,1)}, s32[2,9]{1,0:T(2,128)S(1)}) custom-call(s32[1,8]{1,0:T(1,128)S(1)} %copy-done.1, s32[1]{0:T(128)S(6)} %copy.16.refs_1_.counts, s32[1,8]{1,0:T(1,128)S(1)} %bitcast.12, s32[1]{0:T(128)} %bitcast.1.next_counts, bf16[8,512,512]{2,1,0:T(8,128)(2,1)S(1)} %bitcast.6, ...), custom_call_target="tpu_custom_call", output_to_operand_aliasing={{0}: (5, {})} | custom-call | flops 16106127360 | bytes 15728640 | tf_op jit(solution)/shard_map/pallas_call | solution.py:244
  30.8 2.1 %shard_map.42.band = bf16[1,10,512,512]{3,2,1,0:T(8,128)(2,1)} custom-call(s32[2,9]{1,0:T(2,128)S(1)} %get-tuple-element.20.table, bf16[8,512,512]{2,1,0:T(8,128)(2,1)S(1)} %bitcast.7, bf16[528,512]{1,0:T(8,128)(2,1)S(1)} %collective-permute-done.refs_3_.chunk, bf16[1,10,512,512]{3,2,1,0:T(8,128)(2,1)} %get-tuple-element.25.band), custom_call_target="tpu_custom_call", output_to_operand_aliasing={{}: (3, {})} | custom-call | flops 536870912 | bytes 524288 | tf_op jit(solution)/shard_map/pallas_call | solution.py:244
  32.8 0.0 collective-permute-done.6.detour
  32.9 1.9 %collective-permute-start.2 = (bf16[512,256]{1,0:T(8,128)(2,1)S(1)}, bf16[512,256]{1,0:T(8,128)(2,1)S(1)}, u32[]{:S(2)}, u32[]{:S(2)}) collective-permute-start(bf16[512,256]{1,0:T(8,128)(2,1)S(1)} %get-tuple-element.21), channel_id=1, source_target_pairs={{0,15},{2,1},{4,3},{6,5},{8,7},{10,9},{12,11},{14,13},{16,31},{18,... | collective-permute-start | bytes 786440 | tf_op jit(solution)/shard_map/ppermute | solution.py:263
  34.7 0.0 collective-permute-done.4.chunk
  34.8 2.6 %shard_map.43 = (bf16[1,10,512,512]{3,2,1,0:T(8,128)(2,1)}, bf16[96,512]{1,0:T(8,128)(2,1)S(1)}) custom-call(s32[2,9]{1,0:T(2,128)S(1)} %get-tuple-element.20.table, bf16[8,512,512]{2,1,0:T(8,128)(2,1)S(1)} %bitcast.8, bf16[1024,512]{1,0:T(8,128)(2,1)S(1)} %collective-permute-done.4.chunk, ...), custom_call_target="tpu_custom_call", output_to_operand_aliasing={{0}: (5, {})} | custom-call | flops 1073741824 | bytes 1048576 | tf_op jit(solution)/shard_map/pallas_call | solution.py:244
  37.3 4.2 %collective-permute-done.3.chunk = bf16[1024,512]{1,0:T(8,128)(2,1)S(1)} collective-permute-done((bf16[1024,512]{1,0:T(8,128)(2,1)S(1)}, bf16[1024,512]{1,0:T(8,128)(2,1)S(1)}, u32[]{:S(2)}, u32[]{:S(2)}) %collective-permute-start.3) | collective-permute-done | bytes 1048608 | tf_op jit(solution)/shard_map/ppermute | solution.py:263
  41.5 0.7 %shard_map.44 = (bf16[1,10,512,512]{3,2,1,0:T(8,128)(2,1)}, f32[512,512]{1,0:T(8,128)S(1)}) custom-call(s32[2,9]{1,0:T(2,128)S(1)} %get-tuple-element.20.table, bf16[8,512,512]{2,1,0:T(8,128)(2,1)S(1)} %bitcast.9, bf16[1024,512]{1,0:T(8,128)(2,1)S(1)} %collective-permute-done.3.chunk, ...), custom_call_target="tpu_custom_call", output_to_operand_aliasing={{0}: (3, {})} | custom-call | flops 1073741824 | bytes 1048576 | tf_op jit(solution)/shard_map/pallas_call | solution.py:244
  42.2 0.0 collective-permute-done.8.near
  42.2 6.7 %collective-permute-done.7.chunk = bf16[672,512]{1,0:T(8,128)(2,1)S(1)} collective-permute-done((bf16[672,512]{1,0:T(8,128)(2,1)S(1)}, bf16[672,512]{1,0:T(8,128)(2,1)S(1)}, u32[]{:S(2)}, u32[]{:S(2)}) %collective-permute-start.7) | collective-permute-done | bytes 688160 | tf_op jit(solution)/shard_map/ppermute | solution.py:263
  48.9 0.6 %shard_map.46.band = bf16[1,10,512,512]{3,2,1,0:T(8,128)(2,1)} custom-call(s32[2,9]{1,0:T(2,128)S(1)} %get-tuple-element.20.table, bf16[8,512,512]{2,1,0:T(8,128)(2,1)S(1)} %bitcast.10, bf16[672,512]{1,0:T(8,128)(2,1)S(1)} %collective-permute-done.7.chunk, bf16[96,512]{1,0:T(8,128)(2,1)S(1)} %get-tuple-element.28.rest, ...), custom_call_target="tpu_custom_call", output_to_operand_aliasing={{}: (6, {})} | custom-call | flops 1073741824 | bytes 1048576 | tf_op jit(solution)/shard_map/pallas_call | solution.py:244
  49.5 2.2 %collective-permute-done.2.chunk = bf16[512,256]{1,0:T(8,128)(2,1)S(1)} collective-permute-done((bf16[512,256]{1,0:T(8,128)(2,1)S(1)}, bf16[512,256]{1,0:T(8,128)(2,1)S(1)}, u32[]{:S(2)}, u32[]{:S(2)}) %collective-permute-start.2) | collective-permute-done | bytes 262176 | tf_op jit(solution)/shard_map/ppermute | solution.py:263
  51.7 0.6 %shard_map.47 = bf16[1,10,512,512]{3,2,1,0:T(8,128)(2,1)} custom-call(s32[2,9]{1,0:T(2,128)S(1)} %get-tuple-element.20.table, bf16[8,512,512]{2,1,0:T(8,128)(2,1)S(1)} %bitcast.11, bf16[512,256]{1,0:T(8,128)(2,1)S(1)} %collective-permute-done.2.chunk, f32[512,512]{1,0:T(8,128)S(1)} %get-tuple-element.27.base, ...), custom_call_target="tpu_custom_call", output_to_operand_aliasing={{}: (4, {})} | custom-call | flops 536870912 | bytes 524288 | tf_op jit(solution)/shard_map/pallas_call | solution.py:244
  (1 shorter events, 0.0 us)
Async XLA Ops:
  1.1 16.0 %collective-permute-start.1 = (bf16[512,512]{1,0:T(8,128)(2,1)S(1)}, bf16[512,512]{1,0:T(8,128)(2,1)S(1)}, u32[]{:S(2)}, u32[]{:S(2)}) collective-permute-start(bf16[512,512]{1,0:T(8,128)(2,1)S(1)} %slice_bitcast_fusion.refs_3_), channel_id=1, source_target_pairs={{0,15},{1,0},{2,1},{3,2},{4,3},{5,4},{6,5},{7,6},{8,7},{9,8},{10,9... | collective-permute-start | bytes 1572872 | tf_op jit(solution)/shard_map/ppermute | solution.py:263
  7.2 0.7 %copy-start = (s32[1,8]{1,0:T(1,128)S(1)}, s32[1,8]{1,0:T(1,128)}, u32[]{:S(2)}) copy-start(s32[1,8]{1,0:T(1,128)} %refs_0_.7) | copy-start | bytes 100
  9.5 6.9 %collective-permute-start.5 = (bf16[96,512]{1,0:T(8,128)(2,1)S(1)}, bf16[96,512]{1,0:T(8,128)(2,1)S(1)}, u32[]{:S(2)}, u32[]{:S(2)}) collective-permute-start(bf16[96,512]{1,0:T(8,128)(2,1)S(1)} %get-tuple-element.24), channel_id=1, source_target_pairs={{2,1},{4,3},{6,5},{8,7},{10,9},{12,11},{14,13},{18,17},{20,19},{22... | collective-permute-start | bytes 294920 | tf_op jit(solution)/shard_map/ppermute | solution.py:281
  10.8 11.6 %collective-permute-start = (bf16[528,512]{1,0:T(8,128)(2,1)S(1)}, bf16[528,512]{1,0:T(8,128)(2,1)S(1)}, u32[]{:S(2)}, u32[]{:S(2)}) collective-permute-start(bf16[528,512]{1,0:T(8,128)(2,1)S(1)} %get-tuple-element.18.refs_3_), channel_id=1, source_target_pairs={{0,15},{1,0},{2,1},{3,2},{4,3},{5,4},{6,5},{7,6},{8,7},{9,8},{10,9... | collective-permute-start | bytes 1622024 | tf_op jit(solution)/shard_map/ppermute | solution.py:263
  14.4 20.3 %collective-permute-start.4 = (bf16[1024,512]{1,0:T(8,128)(2,1)S(1)}, bf16[1024,512]{1,0:T(8,128)(2,1)S(1)}, u32[]{:S(2)}, u32[]{:S(2)}) collective-permute-start(bf16[1024,512]{1,0:T(8,128)(2,1)S(1)} %get-tuple-element.23), channel_id=1, source_target_pairs={{0,15},{1,0},{2,1},{3,2},{4,3},{5,4},{6,5},{7,6},{8,7},{9,8},{10,9... | collective-permute-start | bytes 3145736 | tf_op jit(solution)/shard_map/ppermute | solution.py:263
  16.4 25.2 %collective-permute-start.3 = (bf16[1024,512]{1,0:T(8,128)(2,1)S(1)}, bf16[1024,512]{1,0:T(8,128)(2,1)S(1)}, u32[]{:S(2)}, u32[]{:S(2)}) collective-permute-start(bf16[1024,512]{1,0:T(8,128)(2,1)S(1)} %get-tuple-element.22), channel_id=1, source_target_pairs={{0,15},{1,0},{2,1},{3,2},{4,3},{5,4},{6,5},{7,6},{8,7},{9,8},{10,9... | collective-permute-start | bytes 3145736 | tf_op jit(solution)/shard_map/ppermute | solution.py:263
  16.4 16.4 %collective-permute-start.6 = (bf16[96,512]{1,0:T(8,128)(2,1)S(1)}, bf16[96,512]{1,0:T(8,128)(2,1)S(1)}, u32[]{:S(2)}, u32[]{:S(2)}) collective-permute-start(bf16[96,512]{1,0:T(8,128)(2,1)S(1)} %collective-permute-done.5.direct), channel_id=1, source_target_pairs={{18,15},{2,31}} | collective-permute-start | bytes 294920 | tf_op jit(solution)/shard_map/ppermute | solution.py:281
  18.7 30.2 %collective-permute-start.7 = (bf16[672,512]{1,0:T(8,128)(2,1)S(1)}, bf16[672,512]{1,0:T(8,128)(2,1)S(1)}, u32[]{:S(2)}, u32[]{:S(2)}) collective-permute-start(bf16[672,512]{1,0:T(8,128)(2,1)S(1)} %shard_map.45), channel_id=1, source_target_pairs={{0,15},{1,0},{2,1},{3,2},{4,3},{5,4},{6,5},{7,6},{8,7},{9,8},{10,9... | collective-permute-start | bytes 2064392 | tf_op jit(solution)/shard_map/ppermute | solution.py:263
  20.9 2.1 %copy-start.1 = (s32[1,8]{1,0:T(1,128)S(1)}, s32[1,8]{1,0:T(1,128)}, u32[]{:S(2)}) copy-start(s32[1,8]{1,0:T(1,128)} %refs_0_.7) | copy-start | bytes 100
  24.7 17.5 %collective-permute-start.8 = (bf16[512,512]{1,0:T(8,128)(2,1)S(1)}, bf16[512,512]{1,0:T(8,128)(2,1)S(1)}, u32[]{:S(2)}, u32[]{:S(2)}) collective-permute-start(bf16[512,512]{1,0:T(8,128)(2,1)S(1)} %get-tuple-element.29), channel_id=1, source_target_pairs={{1,0},{3,2},{5,4},{7,6},{9,8},{11,10},{13,12},{15,14},{17,16},{19,... | collective-permute-start | bytes 1572872 | tf_op jit(solution)/shard_map/ppermute | solution.py:263
  32.9 18.9 %collective-permute-start.2 = (bf16[512,256]{1,0:T(8,128)(2,1)S(1)}, bf16[512,256]{1,0:T(8,128)(2,1)S(1)}, u32[]{:S(2)}, u32[]{:S(2)}) collective-permute-start(bf16[512,256]{1,0:T(8,128)(2,1)S(1)} %get-tuple-element.21), channel_id=1, source_target_pairs={{0,15},{2,1},{4,3},{6,5},{8,7},{10,9},{12,11},{14,13},{16,31},{18,... | collective-permute-start | bytes 786440 | tf_op jit(solution)/shard_map/ppermute | solution.py:263

commit v7 on v6

--- a/solution.py
+++ b/solution.py
@@ -38,7 +38,7 @@
     copy.wait()
 
 
-def early_kernel(total, cols, counts, next_cols, next_counts, own, band, out, table, out_v, sems):
+def early_kernel(total, cols, counts, next_cols, next_counts, own, band, out, table, place, out_v, sems):
     here = cols[0, 0]
     for s in range(next_cols.shape[1]):
         col = next_cols[0, s]
@@ -46,6 +46,7 @@
         table[1, s] = find(cols, counts, col)
     table[0, next_cols.shape[1]] = lax.rem(here, 2)
     table[1, next_cols.shape[1]] = here
+    place[...] = jnp.full(place.shape, jnp.where(lax.rem(here, 2) == 1, table[0, LAST], -1), jnp.int32)
 
     def job(k):
         col = lax.rem(here + k - W + total, total)
@@ -172,17 +173,14 @@
         tile(0).wait()
 
 
-def last_kernel(table, own, chunk, base, band, out, places, out_v, sems):
-    fetch = pltpu.make_async_copy(table, places, sems.at[0])
-    fetch.start()
+def last_kernel(place, own, chunk, base, band, out, out_v, sem):
+    k = jnp.max(place[...])
     half = chunk.shape[1]
     out_v[...] = (base[:, half:] + dot(own[1], chunk[...])).astype(out_v.dtype)
-    fetch.wait()
-    k = places[0, LAST]
-
-    @pl.when((k >= 0) & (places[0, LAST + 1] == 1))
-    def _():
-        copy = pltpu.make_async_copy(out_v, out.at[0, k, :, pl.ds(half, half)], sems.at[1])
+
+    @pl.when(k >= 0)
+    def _():
+        copy = pltpu.make_async_copy(out_v, out.at[0, k, :, pl.ds(half, half)], sem)
         copy.start()
         copy.wait()
 
@@ -290,11 +288,11 @@
 
     (band,) = call(head_kernel, 12, (local, head), [VMEM] * 2, [tile(), sems()], own=own)
     got = chunks[0][rows, : slots + 1].astype(jnp.int32)
-    band, table = call(
+    band, table, place = call(
         functools.partial(early_kernel, total), 3 * WIDTH,
         (tile_cols, tile_counts, got[None, :slots], got[slots:], local, band),
         [SMEM] * 4 + [VMEM, ANY], [tile(WIDTH), sems(WIDTH)],
-        [jax.ShapeDtypeStruct((2, slots + 1), jnp.int32)], [SMEM], own=own,
+        [jax.ShapeDtypeStruct((2, slots + 1), jnp.int32), jax.ShapeDtypeStruct((8, 128), jnp.int32)], [SMEM, VMEM], own=own,
     )
     a, b = MIDDLE[0]
     (band,) = call(
@@ -319,8 +317,7 @@
         [pltpu.VMEM((fold, lanes), own.dtype), side, tile(2), sems(3)], own=own,
     )
     (band,) = call(
-        last_kernel, 1, (table, local, far, base, band), [VMEM] * 4 + [ANY],
-        [pltpu.SMEM(table.shape, table.dtype), side, sems(2)], own=own,
+        last_kernel, 1, (place, local, far, base, band), [VMEM] * 4 + [ANY], [side, sems()], own=own,
     )
     return band
 

time: 52.7 us -> 52.4 us (level)
  waiting for transfers between devices: 13.1 us -> 10.4 us
  starting transfers between devices: 14.8 us -> 16.7 us
  Pallas kernels: 21.2 us -> 21.8 us
    ppermute x7, waiting for transfers between devices: 13.1 us -> 10.4 us  [per_device(): send = lambda value, some=pairs: lax.ppermute(value, 'wide', some)]
    ppermute x7, starting transfers between devices: 12.9 us -> 14.8 us  [per_device(): send = lambda value, some=pairs: lax.ppermute(value, 'wide', some)]
    pallas_call x7, Pallas kernels: 12.8 us -> 13.3 us  [call(): pl.pallas_call(kernel, out_shape=[band, *extra], in_specs=spaces, out_spe...]
  transfers between devices with their start and end apart: 9 -> 9, of which waited for: 3 -> 3; matrix products, arithmetic and copies ran while one was open for 1% -> 1% of each run, Pallas kernels for 39% -> 41%
where the time goes in v7:
time: 52.4 us; the launch traced here: 52 us
  Pallas kernels  21.8 us (42%)
  starting transfers between devices  16.7 us (32%)
  waiting for transfers between devices  10.4 us (20%)
  local copies, waits for them, and re-layouts  2.33 us (4%)
  between operations  0.83 us (2%)
    ppermute x7, starting transfers between devices, per_device(): send = lambda value, some=pairs: lax.ppermute(value, 'wide', some)  14.8 us
    pallas_call x7, Pallas kernels, call(): pl.pallas_call(kernel, out_shape=[band, *extra], in_specs=spaces, out_spe...  13.3 us
    ppermute x7, waiting for transfers between devices, per_device(): send = lambda value, some=pairs: lax.ppermute(value, 'wide', some)  10.4 us
    pallas_call x4, Pallas kernels, pack(): pl.pallas_call(functools.partial(pack_kernel, pieces, noted), out_shape=[...  8.45 us
    ppermute x2, starting transfers between devices, per_device(): both = lambda value, some: lax.ppermute(value, ('groups', 'wide'), some)  1.95 us
    squeeze x1, local copies, waits for them, and re-layouts, per_device(): first = own[0]  1.08 us
  transfers between devices with their start and end apart: 9, of which 3 were waited for; matrix products, arithmetic and copies ran while one was open for 1% of the time, Pallas kernels for 41%

profile of v7, /device:TPU:0, one launch (start us, length us, event | category | flops | bytes accessed | tf_op | source)
XLA Modules:
  0.0 52.0 jit_solution(14398838765551700680)
XLA Ops:
  0.0 1.1 %slice_bitcast_fusion.refs_3_ = bf16[512,512]{1,0:T(8,128)(2,1)S(1)} fusion(bf16[8,512,512]{2,1,0:T(8,128)(2,1)} %refs_2_.7), kind=kLoop, calls=%fused_computation | loop fusion | bytes 1048576 | tf_op jit(solution)/shard_map/squeeze | solution.py:269
  1.1 5.5 %collective-permute-start.1 = (bf16[512,512]{1,0:T(8,128)(2,1)S(1)}, bf16[512,512]{1,0:T(8,128)(2,1)S(1)}, u32[]{:S(2)}, u32[]{:S(2)}) collective-permute-start(bf16[512,512]{1,0:T(8,128)(2,1)S(1)} %slice_bitcast_fusion.refs_3_), channel_id=1, source_target_pairs={{0,15},{1,0},{2,1},{3,2},{4,3},{5,4},{6,5},{7,6},{8,7},{9,8},{10,9... | collective-permute-start | bytes 1572872 | tf_op jit(solution)/shard_map/ppermute | solution.py:261
  7.2 0.0 copy-start
  7.2 0.6 %copy-done = s32[1,8]{1,0:T(1,128)S(1)} copy-done((s32[1,8]{1,0:T(1,128)S(1)}, s32[1,8]{1,0:T(1,128)}, u32[]{:S(2)}) %copy-start) | copy-done | bytes 56
  7.9 1.6 %shard_map.37 = (bf16[528,512]{1,0:T(8,128)(2,1)S(1)}, bf16[96,512]{1,0:T(8,128)(2,1)S(1)}) custom-call(s32[1,8]{1,0:T(1,128)S(1)} %copy-done, s32[1]{0:T(128)S(6)} %copy.16.refs_1_.counts, bf16[8,512,512]{2,1,0:T(8,128)(2,1)} %refs_2_.7, bf16[512,512]{1,0:T(8,128)(2,1)S(1)} %slice_bitcast_fusion.refs_3_), custom_call_target="tpu_custom_call" | custom-call | bytes 2555904 | tf_op jit(solution)/shard_map/pallas_call | solution.py:226
  9.5 1.3 %collective-permute-start.5 = (bf16[96,512]{1,0:T(8,128)(2,1)S(1)}, bf16[96,512]{1,0:T(8,128)(2,1)S(1)}, u32[]{:S(2)}, u32[]{:S(2)}) collective-permute-start(bf16[96,512]{1,0:T(8,128)(2,1)S(1)} %get-tuple-element.26), channel_id=1, source_target_pairs={{2,1},{4,3},{6,5},{8,7},{10,9},{12,11},{14,13},{18,17},{20,19},{22... | collective-permute-start | bytes 294920 | tf_op jit(solution)/shard_map/ppermute | solution.py:279
  10.8 0.1 collective-permute-start
  10.9 3.5 %shard_map.38 = (bf16[1024,512]{1,0:T(8,128)(2,1)S(1)}, bf16[1024,512]{1,0:T(8,128)(2,1)S(1)}, bf16[4096,512]{1,0:T(8,128)(2,1)S(1)}) custom-call(s32[1,8]{1,0:T(1,128)S(1)} %copy-done, s32[1]{0:T(128)S(6)} %copy.16.refs_1_.counts, bf16[8,512,512]{2,1,0:T(8,128)(2,1)} %refs_2_.7, bf16[528,512]{1,0:T(8,128)(2,1)S(1)} %get-tuple-element.19.refs_3_), custom_call_target="tpu_custom_call" | custom-call | bytes 25165824 | tf_op jit(solution)/shard_map/pallas_call | solution.py:226
  14.4 1.9 %collective-permute-start.4 = (bf16[1024,512]{1,0:T(8,128)(2,1)S(1)}, bf16[1024,512]{1,0:T(8,128)(2,1)S(1)}, u32[]{:S(2)}, u32[]{:S(2)}) collective-permute-start(bf16[1024,512]{1,0:T(8,128)(2,1)S(1)} %get-tuple-element.25), channel_id=1, source_target_pairs={{0,15},{1,0},{2,1},{3,2},{4,3},{5,4},{6,5},{7,6},{8,7},{9,8},{10,9... | collective-permute-start | bytes 3145736 | tf_op jit(solution)/shard_map/ppermute | solution.py:261
  16.4 0.1 collective-permute-start.3
  16.4 0.0 collective-permute-done.5.direct
  16.4 0.7 %collective-permute-start.6 = (bf16[96,512]{1,0:T(8,128)(2,1)S(1)}, bf16[96,512]{1,0:T(8,128)(2,1)S(1)}, u32[]{:S(2)}, u32[]{:S(2)}) collective-permute-start(bf16[96,512]{1,0:T(8,128)(2,1)S(1)} %collective-permute-done.5.direct), channel_id=1, source_target_pairs={{18,15},{2,31}} | collective-permute-start | bytes 294920 | tf_op jit(solution)/shard_map/ppermute | solution.py:279
  17.1 0.0 collective-permute-done.1.head.refs_3_
  17.1 1.6 %shard_map.45 = bf16[672,512]{1,0:T(8,128)(2,1)S(1)} custom-call(s32[1,8]{1,0:T(1,128)S(1)} %copy-done, s32[1]{0:T(128)S(6)} %copy.16.refs_1_.counts, bf16[8,512,512]{2,1,0:T(8,128)(2,1)} %refs_2_.7, bf16[512,512]{1,0:T(8,128)(2,1)S(1)} %collective-permute-done.1.head.refs_3_), custom_call_target="tpu_custom_call" | custom-call | bytes 2752512 | tf_op jit(solution)/shard_map/pallas_call | solution.py:226
  18.7 2.1 %collective-permute-start.7 = (bf16[672,512]{1,0:T(8,128)(2,1)S(1)}, bf16[672,512]{1,0:T(8,128)(2,1)S(1)}, u32[]{:S(2)}, u32[]{:S(2)}) collective-permute-start(bf16[672,512]{1,0:T(8,128)(2,1)S(1)} %shard_map.45), channel_id=1, source_target_pairs={{0,15},{1,0},{2,1},{3,2},{4,3},{5,4},{6,5},{7,6},{8,7},{9,8},{10,9... | collective-permute-start | bytes 2064392 | tf_op jit(solution)/shard_map/ppermute | solution.py:261
  20.9 0.0 copy-start.1
  20.9 1.5 %shard_map.39.band = bf16[1,10,512,512]{3,2,1,0:T(8,128)(2,1)} custom-call(bf16[8,512,512]{2,1,0:T(8,128)(2,1)S(1)} %bitcast.5, bf16[512,512]{1,0:T(8,128)(2,1)S(1)} %collective-permute-done.1.head.refs_3_), custom_call_target="tpu_custom_call" | custom-call | flops 6442450944 | bytes 6291456 | tf_op jit(solution)/shard_map/pallas_call | solution.py:242
  22.4 0.0 collective-permute-done.refs_3_.chunk
  22.4 0.6 %slice.19 = s32[1,1]{1,0:T(1,128)} slice(s32[1,9]{1,0:T(1,128)S(1)} %slice_convert_fusion), slice={[0:1], [8:9]} | slice | bytes 8 | tf_op jit(solution)/shard_map/slice | solution.py:293
  23.0 0.0 copy-done.1
  23.0 1.7 %shard_map.41 = (bf16[512,256]{1,0:T(8,128)(2,1)S(1)}, bf16[512,512]{1,0:T(8,128)(2,1)S(1)}) custom-call(s32[1,8]{1,0:T(1,128)S(1)} %copy-done.1, s32[1]{0:T(128)S(6)} %copy.16.refs_1_.counts, bf16[8,512,512]{2,1,0:T(8,128)(2,1)} %refs_2_.7, bf16[528,512]{1,0:T(8,128)(2,1)S(1)} %collective-permute-done.refs_3_.chunk), custom_call_target="tpu_custom_call" | custom-call | bytes 3145728 | tf_op jit(solution)/shard_map/pallas_call | solution.py:226
  24.7 1.3 %collective-permute-start.8 = (bf16[512,512]{1,0:T(8,128)(2,1)S(1)}, bf16[512,512]{1,0:T(8,128)(2,1)S(1)}, u32[]{:S(2)}, u32[]{:S(2)}) collective-permute-start(bf16[512,512]{1,0:T(8,128)(2,1)S(1)} %get-tuple-element.31), channel_id=1, source_target_pairs={{1,0},{3,2},{5,4},{7,6},{9,8},{11,10},{13,12},{15,14},{17,16},{19,... | collective-permute-start | bytes 1572872 | tf_op jit(solution)/shard_map/ppermute | solution.py:261
  26.0 3.7 %shard_map.40 = (bf16[1,10,512,512]{3,2,1,0:T(8,128)(2,1)}, s32[2,9]{1,0:T(2,128)S(1)}, s32[8,128]{1,0:T(8,128)S(1)}) custom-call(s32[1,8]{1,0:T(1,128)S(1)} %copy-done.1, s32[1]{0:T(128)S(6)} %copy.16.refs_1_.counts, s32[1,8]{1,0:T(1,128)S(1)} %bitcast.12, s32[1]{0:T(128)} %bitcast.1.next_counts, ...), custom_call_target="tpu_custom_call", output_to_operand_aliasing={{0}: (5, {})} | custom-call | flops 16106127360 | bytes 15728640 | tf_op jit(solution)/shard_map/pallas_call | solution.py:242
  29.7 2.1 %shard_map.42.band = bf16[1,10,512,512]{3,2,1,0:T(8,128)(2,1)} custom-call(s32[2,9]{1,0:T(2,128)S(1)} %get-tuple-element.23.table, bf16[8,512,512]{2,1,0:T(8,128)(2,1)S(1)} %bitcast.7, bf16[528,512]{1,0:T(8,128)(2,1)S(1)} %collective-permute-done.refs_3_.chunk, bf16[1,10,512,512]{3,2,1,0:T(8,128)(2,1)} %get-tuple-element.27.band), custom_call_target="tpu_custom_call", output_to_operand_aliasing={{}: (3, {})} | custom-call | flops 536870912 | bytes 524288 | tf_op jit(solution)/shard_map/pallas_call | solution.py:242
  31.8 0.0 collective-permute-done.6.detour
  31.8 3.8 %collective-permute-start.2 = (bf16[512,256]{1,0:T(8,128)(2,1)S(1)}, bf16[512,256]{1,0:T(8,128)(2,1)S(1)}, u32[]{:S(2)}, u32[]{:S(2)}) collective-permute-start(bf16[512,256]{1,0:T(8,128)(2,1)S(1)} %get-tuple-element.22), channel_id=1, source_target_pairs={{0,15},{2,1},{4,3},{6,5},{8,7},{10,9},{12,11},{14,13},{16,31},{18,... | collective-permute-start | bytes 786440 | tf_op jit(solution)/shard_map/ppermute | solution.py:261
  35.6 0.0 collective-permute-done.4.chunk
  35.6 2.6 %shard_map.43 = (bf16[1,10,512,512]{3,2,1,0:T(8,128)(2,1)}, bf16[96,512]{1,0:T(8,128)(2,1)S(1)}) custom-call(s32[2,9]{1,0:T(2,128)S(1)} %get-tuple-element.23.table, bf16[8,512,512]{2,1,0:T(8,128)(2,1)S(1)} %bitcast.8, bf16[1024,512]{1,0:T(8,128)(2,1)S(1)} %collective-permute-done.4.chunk, ...), custom_call_target="tpu_custom_call", output_to_operand_aliasing={{0}: (5, {})} | custom-call | flops 1073741824 | bytes 1048576 | tf_op jit(solution)/shard_map/pallas_call | solution.py:242
  38.1 3.4 %collective-permute-done.3.chunk = bf16[1024,512]{1,0:T(8,128)(2,1)S(1)} collective-permute-done((bf16[1024,512]{1,0:T(8,128)(2,1)S(1)}, bf16[1024,512]{1,0:T(8,128)(2,1)S(1)}, u32[]{:S(2)}, u32[]{:S(2)}) %collective-permute-start.3) | collective-permute-done | bytes 1048608 | tf_op jit(solution)/shard_map/ppermute | solution.py:261
  41.5 2.6 %shard_map.44 = (bf16[1,10,512,512]{3,2,1,0:T(8,128)(2,1)}, f32[512,512]{1,0:T(8,128)S(1)}) custom-call(s32[2,9]{1,0:T(2,128)S(1)} %get-tuple-element.23.table, bf16[8,512,512]{2,1,0:T(8,128)(2,1)S(1)} %bitcast.9, bf16[1024,512]{1,0:T(8,128)(2,1)S(1)} %collective-permute-done.3.chunk, ...), custom_call_target="tpu_custom_call", output_to_operand_aliasing={{0}: (3, {})} | custom-call | flops 1073741824 | bytes 1048576 | tf_op jit(solution)/shard_map/pallas_call | solution.py:242
  44.2 0.0 collective-permute-done.8.near
  44.2 4.7 %collective-permute-done.7.chunk = bf16[672,512]{1,0:T(8,128)(2,1)S(1)} collective-permute-done((bf16[672,512]{1,0:T(8,128)(2,1)S(1)}, bf16[672,512]{1,0:T(8,128)(2,1)S(1)}, u32[]{:S(2)}, u32[]{:S(2)}) %collective-permute-start.7) | collective-permute-done | bytes 688160 | tf_op jit(solution)/shard_map/ppermute | solution.py:261
  48.9 0.6 %shard_map.46.band = bf16[1,10,512,512]{3,2,1,0:T(8,128)(2,1)} custom-call(s32[2,9]{1,0:T(2,128)S(1)} %get-tuple-element.23.table, bf16[8,512,512]{2,1,0:T(8,128)(2,1)S(1)} %bitcast.10, bf16[672,512]{1,0:T(8,128)(2,1)S(1)} %collective-permute-done.7.chunk, bf16[96,512]{1,0:T(8,128)(2,1)S(1)} %get-tuple-element.30.rest, ...), custom_call_target="tpu_custom_call", output_to_operand_aliasing={{}: (6, {})} | custom-call | flops 1073741824 | bytes 1048576 | tf_op jit(solution)/shard_map/pallas_call | solution.py:242
  49.5 2.2 %collective-permute-done.2.chunk = bf16[512,256]{1,0:T(8,128)(2,1)S(1)} collective-permute-done((bf16[512,256]{1,0:T(8,128)(2,1)S(1)}, bf16[512,256]{1,0:T(8,128)(2,1)S(1)}, u32[]{:S(2)}, u32[]{:S(2)}) %collective-permute-start.2) | collective-permute-done | bytes 262176 | tf_op jit(solution)/shard_map/ppermute | solution.py:261
  51.7 0.3 shard_map.47
  (1 shorter events, 0.0 us)
Async XLA Ops:
  1.1 16.0 %collective-permute-start.1 = (bf16[512,512]{1,0:T(8,128)(2,1)S(1)}, bf16[512,512]{1,0:T(8,128)(2,1)S(1)}, u32[]{:S(2)}, u32[]{:S(2)}) collective-permute-start(bf16[512,512]{1,0:T(8,128)(2,1)S(1)} %slice_bitcast_fusion.refs_3_), channel_id=1, source_target_pairs={{0,15},{1,0},{2,1},{3,2},{4,3},{5,4},{6,5},{7,6},{8,7},{9,8},{10,9... | collective-permute-start | bytes 1572872 | tf_op jit(solution)/shard_map/ppermute | solution.py:261
  7.2 0.7 %copy-start = (s32[1,8]{1,0:T(1,128)S(1)}, s32[1,8]{1,0:T(1,128)}, u32[]{:S(2)}) copy-start(s32[1,8]{1,0:T(1,128)} %refs_0_.7) | copy-start | bytes 100
  9.5 6.9 %collective-permute-start.5 = (bf16[96,512]{1,0:T(8,128)(2,1)S(1)}, bf16[96,512]{1,0:T(8,128)(2,1)S(1)}, u32[]{:S(2)}, u32[]{:S(2)}) collective-permute-start(bf16[96,512]{1,0:T(8,128)(2,1)S(1)} %get-tuple-element.26), channel_id=1, source_target_pairs={{2,1},{4,3},{6,5},{8,7},{10,9},{12,11},{14,13},{18,17},{20,19},{22... | collective-permute-start | bytes 294920 | tf_op jit(solution)/shard_map/ppermute | solution.py:279
  10.8 11.6 %collective-permute-start = (bf16[528,512]{1,0:T(8,128)(2,1)S(1)}, bf16[528,512]{1,0:T(8,128)(2,1)S(1)}, u32[]{:S(2)}, u32[]{:S(2)}) collective-permute-start(bf16[528,512]{1,0:T(8,128)(2,1)S(1)} %get-tuple-element.19.refs_3_), channel_id=1, source_target_pairs={{0,15},{1,0},{2,1},{3,2},{4,3},{5,4},{6,5},{7,6},{8,7},{9,8},{10,9... | collective-permute-start | bytes 1622024 | tf_op jit(solution)/shard_map/ppermute | solution.py:261
  14.4 21.1 %collective-permute-start.4 = (bf16[1024,512]{1,0:T(8,128)(2,1)S(1)}, bf16[1024,512]{1,0:T(8,128)(2,1)S(1)}, u32[]{:S(2)}, u32[]{:S(2)}) collective-permute-start(bf16[1024,512]{1,0:T(8,128)(2,1)S(1)} %get-tuple-element.25), channel_id=1, source_target_pairs={{0,15},{1,0},{2,1},{3,2},{4,3},{5,4},{6,5},{7,6},{8,7},{9,8},{10,9... | collective-permute-start | bytes 3145736 | tf_op jit(solution)/shard_map/ppermute | solution.py:261
  16.4 25.2 %collective-permute-start.3 = (bf16[1024,512]{1,0:T(8,128)(2,1)S(1)}, bf16[1024,512]{1,0:T(8,128)(2,1)S(1)}, u32[]{:S(2)}, u32[]{:S(2)}) collective-permute-start(bf16[1024,512]{1,0:T(8,128)(2,1)S(1)} %get-tuple-element.24), channel_id=1, source_target_pairs={{0,15},{1,0},{2,1},{3,2},{4,3},{5,4},{6,5},{7,6},{8,7},{9,8},{10,9... | collective-permute-start | bytes 3145736 | tf_op jit(solution)/shard_map/ppermute | solution.py:261
  16.4 15.3 %collective-permute-start.6 = (bf16[96,512]{1,0:T(8,128)(2,1)S(1)}, bf16[96,512]{1,0:T(8,128)(2,1)S(1)}, u32[]{:S(2)}, u32[]{:S(2)}) collective-permute-start(bf16[96,512]{1,0:T(8,128)(2,1)S(1)} %collective-permute-done.5.direct), channel_id=1, source_target_pairs={{18,15},{2,31}} | collective-permute-start | bytes 294920 | tf_op jit(solution)/shard_map/ppermute | solution.py:279
  18.7 30.2 %collective-permute-start.7 = (bf16[672,512]{1,0:T(8,128)(2,1)S(1)}, bf16[672,512]{1,0:T(8,128)(2,1)S(1)}, u32[]{:S(2)}, u32[]{:S(2)}) collective-permute-start(bf16[672,512]{1,0:T(8,128)(2,1)S(1)} %shard_map.45), channel_id=1, source_target_pairs={{0,15},{1,0},{2,1},{3,2},{4,3},{5,4},{6,5},{7,6},{8,7},{9,8},{10,9... | collective-permute-start | bytes 2064392 | tf_op jit(solution)/shard_map/ppermute | solution.py:261
  20.9 2.1 %copy-start.1 = (s32[1,8]{1,0:T(1,128)S(1)}, s32[1,8]{1,0:T(1,128)}, u32[]{:S(2)}) copy-start(s32[1,8]{1,0:T(1,128)} %refs_0_.7) | copy-start | bytes 100
  24.7 19.5 %collective-permute-start.8 = (bf16[512,512]{1,0:T(8,128)(2,1)S(1)}, bf16[512,512]{1,0:T(8,128)(2,1)S(1)}, u32[]{:S(2)}, u32[]{:S(2)}) collective-permute-start(bf16[512,512]{1,0:T(8,128)(2,1)S(1)} %get-tuple-element.31), channel_id=1, source_target_pairs={{1,0},{3,2},{5,4},{7,6},{9,8},{11,10},{13,12},{15,14},{17,16},{19,... | collective-permute-start | bytes 1572872 | tf_op jit(solution)/shard_map/ppermute | solution.py:261
  31.8 20.0 %collective-permute-start.2 = (bf16[512,256]{1,0:T(8,128)(2,1)S(1)}, bf16[512,256]{1,0:T(8,128)(2,1)S(1)}, u32[]{:S(2)}, u32[]{:S(2)}) collective-permute-start(bf16[512,256]{1,0:T(8,128)(2,1)S(1)} %get-tuple-element.22), channel_id=1, source_target_pairs={{0,15},{2,1},{4,3},{6,5},{8,7},{10,9},{12,11},{14,13},{16,31},{18,... | collective-permute-start | bytes 786440 | tf_op jit(solution)/shard_map/ppermute | solution.py:261

commit v8 on v7

--- a/solution.py
+++ b/solution.py
@@ -12,8 +12,8 @@
 META_ROWS = 16
 LAST = 7
 MIDDLE = ((1, 2), (2, 4), (4, 6))
-DETOUR = 96
-RELAY = 2
+BLOCKS = (48, 64)
+DETOUR = sum(BLOCKS)
 ANY = pl.BlockSpec(memory_space=pl.ANY)
 HBM = pl.BlockSpec(memory_space=pltpu.HBM)
 SMEM = pl.BlockSpec(memory_space=pltpu.SMEM)
@@ -113,11 +113,13 @@
 
 
 def rest_kernel(last_device, first_slot, jobs, table, own, chunk, direct, detour, band, out, rest, out_v, sems):
-    @pl.when(table[1, LAST + 1] == last_device)
+    here = table[1, LAST + 1]
+
+    @pl.when(here == last_device)
     def _():
         rest[...] = detour[...]
 
-    @pl.when(table[1, LAST + 1] != last_device)
+    @pl.when(here != last_device)
     def _():
         rest[...] = direct[...]
 
@@ -138,7 +140,7 @@
     chunk_kernel(first_slot, jobs, table, own, chunk, band, out, out_v, sems)
 
 
-def late_kernel(table, own, chunk, rest, near, base, band, out, low, left_v, out_v, sems):
+def late_kernel(last_device, table, own, chunk, rest, direct, detour, near, base, band, out, low, left_v, out_v, sems):
     rows, half = left_v.shape
     fold = low.shape[0]
     k, k_last = table[0, LAST - 1], table[0, LAST]
@@ -155,7 +157,18 @@
     @pl.when((k_last >= 0) & jnp.logical_not(even))
     def _():
         low[: fold - DETOUR] = chunk[rows:]
-        low[fold - DETOUR :] = rest[...]
+        low[fold - DETOUR : fold - BLOCKS[1]] = rest[...]
+        here = table[1, LAST + 1]
+        around = (here == last_device) | (here == 3)
+
+        @pl.when(around)
+        def _():
+            low[fold - BLOCKS[1] :] = detour[...]
+
+        @pl.when(jnp.logical_not(around))
+        def _():
+            low[fold - BLOCKS[1] :] = direct[...]
+
         left = dot(own[1, :, :fold], low[:, :half]) + dot(own[1, :, fold:], low[:, half:])
         left_v[...] = (base[:, :half] + left).astype(left_v.dtype)
         left_copy = pltpu.make_async_copy(left_v, out.at[0, k_last, :, pl.ds(0, half)], sems.at[2])
@@ -268,20 +281,25 @@
 
     first = own[0]
     head = send(first)
-    one, end = pack([whole(1, 2), folded(fold - DETOUR, fold, 0)], True, tile_cols, tile_counts, own, first)
-    two, three, local = pack([whole(*MIDDLE[1]), whole(*MIDDLE[2]), whole(0, slots)], False, tile_cols, tile_counts, own, one)
-    (four,) = pack([whole(LAST - 1, LAST) + folded(0, fold - DETOUR, rows)], False, tile_cols, tile_counts, own, head)
+    cut = fold - BLOCKS[1]
+    one, end_a = pack([whole(1, 2), folded(fold - DETOUR, cut, 0)], True, tile_cols, tile_counts, own, first)
+    two, local = pack([whole(*MIDDLE[1]), whole(0, slots)], False, tile_cols, tile_counts, own, one)
+    three, end_b = pack([whole(*MIDDLE[2]), folded(cut, fold, 0)], False, tile_cols, tile_counts, own, head)
     chunks = [send(part) for part in (one, two, three)]
-    five, seven = pack([((LAST, 0, rows, half, half, 0, 0),), whole(LAST, LAST + 1)], False, tile_cols, tile_counts, own, chunks[0])
+    four, five, seven = pack(
+        [whole(LAST - 1, LAST) + folded(0, fold - DETOUR, rows), ((LAST, 0, rows, half, half, 0, 0),), whole(LAST, LAST + 1)],
+        False, tile_cols, tile_counts, own, chunks[0],
+    )
     late = send(four)
     groups = lax.axis_size("groups")
     across = [(g * total, (g ^ 1 if groups % 2 == 0 else g) * total) for g in range(groups)]
     both = lambda value, some: lax.ppermute(value, ("groups", "wide"), some)
-    direct = both(
-        end,
-        [(g + a, g + b) for g, _ in across for a, b in pairs[2::2]] + [(g, h + RELAY) for g, h in across],
-    )
-    detour = both(direct, [(h + RELAY, g + total - 1) for g, h in across])
+    straight = [(g * total + i, g * total + j) for g in range(groups) for i, j in pairs[2::2]]
+    shift = lambda some: [(g + i, h + j) for g, h in across for i, j in some]
+    direct_a = both(end_a, straight + shift([(0, 2)]))
+    direct_b = both(end_b, [p for p in straight if p[0] % total != 4] + shift([(0, 2), (4, 6)]))
+    detour_a = both(direct_a, shift([(2, total - 1)]))
+    detour_b = both(direct_b, shift([(2, total - 1), (6, 3)]))
     near = send(seven, pairs[1::2])
     far = send(five, pairs[0::2])
     local = local.reshape(own.shape)
@@ -295,25 +313,26 @@
         [jax.ShapeDtypeStruct((2, slots + 1), jnp.int32), jax.ShapeDtypeStruct((8, 128), jnp.int32)], [SMEM, VMEM], own=own,
     )
     a, b = MIDDLE[0]
-    (band,) = call(
-        functools.partial(chunk_kernel, a, b - a), b - a,
-        (table, local, chunks[0], band), [SMEM] + [VMEM] * 2 + [ANY], [tile(b - a), sems(b - a)], own=own,
+    band, base = call(
+        functools.partial(base_kernel, a, b - a), b - a,
+        (table, local, chunks[0], band), [SMEM] + [VMEM] * 2 + [ANY], [tile(b - a), sems(b - a)],
+        [jax.ShapeDtypeStruct((rows, lanes), jnp.float32)], [VMEM], own=own,
     )
     a, b = MIDDLE[1]
     band, rest = call(
         functools.partial(rest_kernel, total - 1, a, b - a), b - a,
-        (table, local, chunks[1], direct, detour, band), [SMEM] + [VMEM] * 4 + [ANY], [tile(b - a), sems(b - a)],
-        [jax.ShapeDtypeStruct(end.shape, own.dtype)], [VMEM], own=own,
+        (table, local, chunks[1], direct_a, detour_a, band), [SMEM] + [VMEM] * 4 + [ANY], [tile(b - a), sems(b - a)],
+        [jax.ShapeDtypeStruct((BLOCKS[0], lanes), own.dtype)], [VMEM], own=own,
     )
     a, b = MIDDLE[2]
-    band, base = call(
-        functools.partial(base_kernel, a, b - a), b - a,
-        (table, local, chunks[2], band), [SMEM] + [VMEM] * 2 + [ANY], [tile(b - a), sems(b - a)],
-        [jax.ShapeDtypeStruct((rows, lanes), jnp.float32)], [VMEM], own=own,
+    (band,) = call(
+        functools.partial(chunk_kernel, a, b - a), b - a,
+        (table, local, chunks[2], band), [SMEM] + [VMEM] * 2 + [ANY], [tile(b - a), sems(b - a)], own=own,
     )
     side = pltpu.VMEM((rows, half), own.dtype)
     (band,) = call(
-        late_kernel, 2, (table, local, late, rest, near, base, band), [SMEM] + [VMEM] * 5 + [ANY],
+        functools.partial(late_kernel, total - 1), 2,
+        (table, local, late, rest, direct_b, detour_b, near, base, band), [SMEM] + [VMEM] * 7 + [ANY],
         [pltpu.VMEM((fold, lanes), own.dtype), side, tile(2), sems(3)], own=own,
     )
     (band,) = call(

time: 52.4 us -> 52.3 us (level)
  waiting for transfers between devices: 10.4 us -> 8.19 us
  Pallas kernels: 21.8 us -> 22.9 us
  starting transfers between devices: 16.7 us -> 17.5 us
    ppermute x2 -> x4, starting transfers between devices: 1.95 us -> 6.02 us  [per_device(): both = lambda value, some: lax.ppermute(value, ('groups', 'wide'), some)]
    ppermute x7, starting transfers between devices: 14.8 us -> 11.5 us  [per_device(): send = lambda value, some=pairs: lax.ppermute(value, 'wide', some)]
    ppermute x7, waiting for transfers between devices: 10.4 us -> 8.18 us  [per_device(): send = lambda value, some=pairs: lax.ppermute(value, 'wide', some)]
    pallas_call x7, Pallas kernels: 13.3 us -> 14.5 us  [call(): pl.pallas_call(kernel, out_shape=[band, *extra], in_specs=spaces, out_spe...]
  transfers between devices with their start and end apart: 9 -> 11, of which waited for: 3 -> 3; matrix products, arithmetic and copies ran while one was open for 1% -> 1% of each run, Pallas kernels for 41% -> 44%
where the time goes in v8:
time: 52.3 us; the launch traced here: 51.9 us
  Pallas kernels  22.9 us (44%)
  starting transfers between devices  17.5 us (33%)
  waiting for transfers between devices  8.19 us (16%)
  local copies, waits for them, and re-layouts  2.38 us (5%)
  between operations  0.86 us (2%)
    pallas_call x7, Pallas kernels, call(): pl.pallas_call(kernel, out_shape=[band, *extra], in_specs=spaces, out_spe...  14.5 us
    ppermute x7, starting transfers between devices, per_device(): send = lambda value, some=pairs: lax.ppermute(value, 'wide', some)  11.5 us
    pallas_call x4, Pallas kernels, pack(): pl.pallas_call(functools.partial(pack_kernel, pieces, noted), out_shape=[...  8.42 us
    ppermute x7, waiting for transfers between devices, per_device(): send = lambda value, some=pairs: lax.ppermute(value, 'wide', some)  8.18 us
    ppermute x4, starting transfers between devices, per_device(): both = lambda value, some: lax.ppermute(value, ('groups', 'wide'), some)  6.02 us
    squeeze x1, local copies, waits for them, and re-layouts, per_device(): first = own[0]  1.08 us
  transfers between devices with their start and end apart: 11, of which 3 were waited for; matrix products, arithmetic and copies ran while one was open for 1% of the time, Pallas kernels for 44%

profile of v8, /device:TPU:0, one launch (start us, length us, event | category | flops | bytes accessed | tf_op | source)
XLA Modules:
  0.0 51.9 jit_solution(1321187648138941747)
XLA Ops:
  0.0 1.1 %slice_bitcast_fusion.refs_3_ = bf16[512,512]{1,0:T(8,128)(2,1)S(1)} fusion(bf16[8,512,512]{2,1,0:T(8,128)(2,1)} %refs_2_.7), kind=kLoop, calls=%fused_computation | loop fusion | bytes 1048576 | tf_op jit(solution)/shard_map/squeeze | solution.py:282
  1.1 5.5 %collective-permute-start.1 = (bf16[512,512]{1,0:T(8,128)(2,1)S(1)}, bf16[512,512]{1,0:T(8,128)(2,1)S(1)}, u32[]{:S(2)}, u32[]{:S(2)}) collective-permute-start(bf16[512,512]{1,0:T(8,128)(2,1)S(1)} %slice_bitcast_fusion.refs_3_), channel_id=1, source_target_pairs={{0,15},{1,0},{2,1},{3,2},{4,3},{5,4},{6,5},{7,6},{8,7},{9,8},{10,9... | collective-permute-start | bytes 1572872 | tf_op jit(solution)/shard_map/ppermute | solution.py:274
  7.2 0.0 copy-start
  7.2 0.6 %copy-done = s32[1,8]{1,0:T(1,128)S(1)} copy-done((s32[1,8]{1,0:T(1,128)S(1)}, s32[1,8]{1,0:T(1,128)}, u32[]{:S(2)}) %copy-start) | copy-done | bytes 56
  7.9 1.6 %shard_map.37 = (bf16[528,512]{1,0:T(8,128)(2,1)S(1)}, bf16[48,512]{1,0:T(8,128)(2,1)S(1)}) custom-call(s32[1,8]{1,0:T(1,128)S(1)} %copy-done, s32[1]{0:T(128)S(6)} %copy.16.refs_1_.counts, bf16[8,512,512]{2,1,0:T(8,128)(2,1)} %refs_2_.7, bf16[512,512]{1,0:T(8,128)(2,1)S(1)} %slice_bitcast_fusion.refs_3_), custom_call_target="tpu_custom_call" | custom-call | bytes 2359296 | tf_op jit(solution)/shard_map/pallas_call | solution.py:239
  9.5 1.3 %collective-permute-start.5 = (bf16[48,512]{1,0:T(8,128)(2,1)S(1)}, bf16[48,512]{1,0:T(8,128)(2,1)S(1)}, u32[]{:S(2)}, u32[]{:S(2)}) collective-permute-start(bf16[48,512]{1,0:T(8,128)(2,1)S(1)} %get-tuple-element.30), channel_id=1, source_target_pairs={{2,1},{4,3},{6,5},{8,7},{10,9},{12,11},{14,13},{18,17},{20,19},{22... | collective-permute-start | bytes 147464 | tf_op jit(solution)/shard_map/ppermute | solution.py:296
  10.8 0.1 collective-permute-start
  10.9 3.1 %shard_map.38 = (bf16[1024,512]{1,0:T(8,128)(2,1)S(1)}, bf16[4096,512]{1,0:T(8,128)(2,1)S(1)}) custom-call(s32[1,8]{1,0:T(1,128)S(1)} %copy-done, s32[1]{0:T(128)S(6)} %copy.16.refs_1_.counts, bf16[8,512,512]{2,1,0:T(8,128)(2,1)} %refs_2_.7, bf16[528,512]{1,0:T(8,128)(2,1)S(1)} %get-tuple-element.21.refs_3_), custom_call_target="tpu_custom_call" | custom-call | bytes 20971520 | tf_op jit(solution)/shard_map/pallas_call | solution.py:239
  14.0 1.9 %collective-permute-start.4 = (bf16[1024,512]{1,0:T(8,128)(2,1)S(1)}, bf16[1024,512]{1,0:T(8,128)(2,1)S(1)}, u32[]{:S(2)}, u32[]{:S(2)}) collective-permute-start(bf16[1024,512]{1,0:T(8,128)(2,1)S(1)} %get-tuple-element.29), channel_id=1, source_target_pairs={{0,15},{1,0},{2,1},{3,2},{4,3},{5,4},{6,5},{7,6},{8,7},{9,8},{10,9... | collective-permute-start | bytes 3145736 | tf_op jit(solution)/shard_map/ppermute | solution.py:274
  16.0 0.0 collective-permute-done.5.direct
  16.0 0.7 %collective-permute-start.6 = (bf16[48,512]{1,0:T(8,128)(2,1)S(1)}, bf16[48,512]{1,0:T(8,128)(2,1)S(1)}, u32[]{:S(2)}, u32[]{:S(2)}) collective-permute-start(bf16[48,512]{1,0:T(8,128)(2,1)S(1)} %collective-permute-done.5.direct), channel_id=1, source_target_pairs={{2,31},{18,15}} | collective-permute-start | bytes 147464 | tf_op jit(solution)/shard_map/ppermute | solution.py:296
  16.6 0.0 collective-permute-done.1.head.refs_3_
  16.6 1.8 %shard_map.44 = (bf16[1024,512]{1,0:T(8,128)(2,1)S(1)}, bf16[64,512]{1,0:T(8,128)(2,1)S(1)}) custom-call(s32[1,8]{1,0:T(1,128)S(1)} %copy-done, s32[1]{0:T(128)S(6)} %copy.16.refs_1_.counts, bf16[8,512,512]{2,1,0:T(8,128)(2,1)} %refs_2_.7, bf16[512,512]{1,0:T(8,128)(2,1)S(1)} %collective-permute-done.1.head.refs_3_), custom_call_target="tpu_custom_call" | custom-call | bytes 4456448 | tf_op jit(solution)/shard_map/pallas_call | solution.py:239
  18.4 1.3 %collective-permute-start.10 = (bf16[1024,512]{1,0:T(8,128)(2,1)S(1)}, bf16[1024,512]{1,0:T(8,128)(2,1)S(1)}, u32[]{:S(2)}, u32[]{:S(2)}) collective-permute-start(bf16[1024,512]{1,0:T(8,128)(2,1)S(1)} %get-tuple-element.35), channel_id=1, source_target_pairs={{0,15},{1,0},{2,1},{3,2},{4,3},{5,4},{6,5},{7,6},{8,7},{9,8},{10,9... | collective-permute-start | bytes 3145736 | tf_op jit(solution)/shard_map/ppermute | solution.py:274
  19.7 3.4 %collective-permute-start.7 = (bf16[64,512]{1,0:T(8,128)(2,1)S(1)}, bf16[64,512]{1,0:T(8,128)(2,1)S(1)}, u32[]{:S(2)}, u32[]{:S(2)}) collective-permute-start(bf16[64,512]{1,0:T(8,128)(2,1)S(1)} %get-tuple-element.33), channel_id=1, source_target_pairs={{2,1},{6,5},{8,7},{10,9},{12,11},{14,13},{18,17},{22,21},{24,23},{... | collective-permute-start | bytes 196616 | tf_op jit(solution)/shard_map/ppermute | solution.py:296
  23.1 1.5 %shard_map.39.band = bf16[1,10,512,512]{3,2,1,0:T(8,128)(2,1)} custom-call(bf16[8,512,512]{2,1,0:T(8,128)(2,1)S(1)} %bitcast.5, bf16[512,512]{1,0:T(8,128)(2,1)S(1)} %collective-permute-done.1.head.refs_3_), custom_call_target="tpu_custom_call" | custom-call | flops 6442450944 | bytes 6291456 | tf_op jit(solution)/shard_map/pallas_call | solution.py:255
  24.7 0.0 collective-permute-done.refs_3_.chunk
  24.7 0.7 %slice.19 = s32[1,1]{1,0:T(1,128)} slice(s32[1,9]{1,0:T(1,128)S(1)} %slice_convert_fusion), slice={[0:1], [8:9]} | slice | bytes 8 | tf_op jit(solution)/shard_map/slice | solution.py:311
  25.3 1.9 %shard_map.41 = (bf16[656,512]{1,0:T(8,128)(2,1)S(1)}, bf16[512,256]{1,0:T(8,128)(2,1)S(1)}, bf16[512,512]{1,0:T(8,128)(2,1)S(1)}) custom-call(s32[1,8]{1,0:T(1,128)S(1)} %copy-done, s32[1]{0:T(128)S(6)} %copy.16.refs_1_.counts, bf16[8,512,512]{2,1,0:T(8,128)(2,1)} %refs_2_.7, bf16[528,512]{1,0:T(8,128)(2,1)S(1)} %collective-permute-done.refs_3_.chunk), custom_call_target="tpu_custom_call" | custom-call | bytes 5832704 | tf_op jit(solution)/shard_map/pallas_call | solution.py:239
  27.3 0.1 collective-permute-start.3
  27.3 0.0 collective-permute-done.6.detour
  27.3 1.3 %collective-permute-start.9 = (bf16[512,512]{1,0:T(8,128)(2,1)S(1)}, bf16[512,512]{1,0:T(8,128)(2,1)S(1)}, u32[]{:S(2)}, u32[]{:S(2)}) collective-permute-start(bf16[512,512]{1,0:T(8,128)(2,1)S(1)} %get-tuple-element.34), channel_id=1, source_target_pairs={{1,0},{3,2},{5,4},{7,6},{9,8},{11,10},{13,12},{15,14},{17,16},{19,... | collective-permute-start | bytes 1572872 | tf_op jit(solution)/shard_map/ppermute | solution.py:274
  28.6 4.9 %shard_map.40 = (bf16[1,10,512,512]{3,2,1,0:T(8,128)(2,1)}, s32[2,9]{1,0:T(2,128)S(1)}, s32[8,128]{1,0:T(8,128)S(1)}) custom-call(s32[1,8]{1,0:T(1,128)S(1)} %copy-done, s32[1]{0:T(128)S(6)} %copy.16.refs_1_.counts, s32[1,8]{1,0:T(1,128)S(1)} %bitcast.12, s32[1]{0:T(128)} %bitcast.1.next_counts, ...), custom_call_target="tpu_custom_call", output_to_operand_aliasing={{0}: (5, {})} | custom-call | flops 16106127360 | bytes 15728640 | tf_op jit(solution)/shard_map/pallas_call | solution.py:255
  33.6 2.5 %shard_map.42 = (bf16[1,10,512,512]{3,2,1,0:T(8,128)(2,1)}, f32[512,512]{1,0:T(8,128)S(1)}) custom-call(s32[2,9]{1,0:T(2,128)S(1)} %get-tuple-element.25.table, bf16[8,512,512]{2,1,0:T(8,128)(2,1)S(1)} %bitcast.7, bf16[528,512]{1,0:T(8,128)(2,1)S(1)} %collective-permute-done.refs_3_.chunk, ...), custom_call_target="tpu_custom_call", output_to_operand_aliasing={{0}: (3, {})} | custom-call | flops 536870912 | bytes 524288 | tf_op jit(solution)/shard_map/pallas_call | solution.py:255
  36.1 0.0 collective-permute-done.7.direct
  36.1 1.3 %collective-permute-start.2 = (bf16[512,256]{1,0:T(8,128)(2,1)S(1)}, bf16[512,256]{1,0:T(8,128)(2,1)S(1)}, u32[]{:S(2)}, u32[]{:S(2)}) collective-permute-start(bf16[512,256]{1,0:T(8,128)(2,1)S(1)} %get-tuple-element.24), channel_id=1, source_target_pairs={{0,15},{2,1},{4,3},{6,5},{8,7},{10,9},{12,11},{14,13},{16,31},{18,... | collective-permute-start | bytes 786440 | tf_op jit(solution)/shard_map/ppermute | solution.py:274
  37.4 0.0 collective-permute-done.4.chunk
  37.4 0.7 %collective-permute-start.8 = (bf16[64,512]{1,0:T(8,128)(2,1)S(1)}, bf16[64,512]{1,0:T(8,128)(2,1)S(1)}, u32[]{:S(2)}, u32[]{:S(2)}) collective-permute-start(bf16[64,512]{1,0:T(8,128)(2,1)S(1)} %collective-permute-done.7.direct), channel_id=1, source_target_pairs={{2,31},{6,19},{18,15},{22,3}} | collective-permute-start | bytes 196616 | tf_op jit(solution)/shard_map/ppermute | solution.py:296
  38.1 2.8 %shard_map.43 = (bf16[1,10,512,512]{3,2,1,0:T(8,128)(2,1)}, bf16[48,512]{1,0:T(8,128)(2,1)S(1)}) custom-call(s32[2,9]{1,0:T(2,128)S(1)} %get-tuple-element.25.table, bf16[8,512,512]{2,1,0:T(8,128)(2,1)S(1)} %bitcast.8, bf16[1024,512]{1,0:T(8,128)(2,1)S(1)} %collective-permute-done.4.chunk, ...), custom_call_target="tpu_custom_call", output_to_operand_aliasing={{0}: (5, {})} | custom-call | flops 1073741824 | bytes 1048576 | tf_op jit(solution)/shard_map/pallas_call | solution.py:255
  40.9 0.6 %collective-permute-done.10.chunk = bf16[1024,512]{1,0:T(8,128)(2,1)S(1)} collective-permute-done((bf16[1024,512]{1,0:T(8,128)(2,1)S(1)}, bf16[1024,512]{1,0:T(8,128)(2,1)S(1)}, u32[]{:S(2)}, u32[]{:S(2)}) %collective-permute-start.10) | collective-permute-done | bytes 1048608 | tf_op jit(solution)/shard_map/ppermute | solution.py:274
  41.5 1.8 %shard_map.45.band = bf16[1,10,512,512]{3,2,1,0:T(8,128)(2,1)} custom-call(s32[2,9]{1,0:T(2,128)S(1)} %get-tuple-element.25.table, bf16[8,512,512]{2,1,0:T(8,128)(2,1)S(1)} %bitcast.9, bf16[1024,512]{1,0:T(8,128)(2,1)S(1)} %collective-permute-done.10.chunk, bf16[1,10,512,512]{3,2,1,0:T(8,128)(2,1)} %get-tuple-element.36.band), custom_call_target="tpu_custom_call", output_to_operand_aliasing={{}: (3, {})} | custom-call | flops 1073741824 | bytes 1048576 | tf_op jit(solution)/shard_map/pallas_call | solution.py:255
  43.4 0.0 collective-permute-done.8.detour
  43.4 0.0 collective-permute-done.9.near
  43.4 5.4 %collective-permute-done.3.chunk = bf16[656,512]{1,0:T(8,128)(2,1)S(1)} collective-permute-done((bf16[656,512]{1,0:T(8,128)(2,1)S(1)}, bf16[656,512]{1,0:T(8,128)(2,1)S(1)}, u32[]{:S(2)}, u32[]{:S(2)}) %collective-permute-start.3) | collective-permute-done | bytes 671776 | tf_op jit(solution)/shard_map/ppermute | solution.py:274
  48.7 0.6 %shard_map.46.band = bf16[1,10,512,512]{3,2,1,0:T(8,128)(2,1)} custom-call(s32[2,9]{1,0:T(2,128)S(1)} %get-tuple-element.25.table, bf16[8,512,512]{2,1,0:T(8,128)(2,1)S(1)} %bitcast.10, bf16[656,512]{1,0:T(8,128)(2,1)S(1)} %collective-permute-done.3.chunk, bf16[48,512]{1,0:T(8,128)(2,1)S(1)} %get-tuple-element.32.rest, ...), custom_call_target="tpu_custom_call", output_to_operand_aliasing={{}: (8, {})} | custom-call | flops 1073741824 | bytes 1048576 | tf_op jit(solution)/shard_map/pallas_call | solution.py:255
  49.3 2.2 %collective-permute-done.2.chunk = bf16[512,256]{1,0:T(8,128)(2,1)S(1)} collective-permute-done((bf16[512,256]{1,0:T(8,128)(2,1)S(1)}, bf16[512,256]{1,0:T(8,128)(2,1)S(1)}, u32[]{:S(2)}, u32[]{:S(2)}) %collective-permute-start.2) | collective-permute-done | bytes 262176 | tf_op jit(solution)/shard_map/ppermute | solution.py:274
  51.5 0.3 shard_map.47
  (1 shorter events, 0.0 us)
Async XLA Ops:
  1.1 15.5 %collective-permute-start.1 = (bf16[512,512]{1,0:T(8,128)(2,1)S(1)}, bf16[512,512]{1,0:T(8,128)(2,1)S(1)}, u32[]{:S(2)}, u32[]{:S(2)}) collective-permute-start(bf16[512,512]{1,0:T(8,128)(2,1)S(1)} %slice_bitcast_fusion.refs_3_), channel_id=1, source_target_pairs={{0,15},{1,0},{2,1},{3,2},{4,3},{5,4},{6,5},{7,6},{8,7},{9,8},{10,9... | collective-permute-start | bytes 1572872 | tf_op jit(solution)/shard_map/ppermute | solution.py:274
  7.2 0.7 %copy-start = (s32[1,8]{1,0:T(1,128)S(1)}, s32[1,8]{1,0:T(1,128)}, u32[]{:S(2)}) copy-start(s32[1,8]{1,0:T(1,128)} %refs_0_.7) | copy-start | bytes 100
  9.5 6.5 %collective-permute-start.5 = (bf16[48,512]{1,0:T(8,128)(2,1)S(1)}, bf16[48,512]{1,0:T(8,128)(2,1)S(1)}, u32[]{:S(2)}, u32[]{:S(2)}) collective-permute-start(bf16[48,512]{1,0:T(8,128)(2,1)S(1)} %get-tuple-element.30), channel_id=1, source_target_pairs={{2,1},{4,3},{6,5},{8,7},{10,9},{12,11},{14,13},{18,17},{20,19},{22... | collective-permute-start | bytes 147464 | tf_op jit(solution)/shard_map/ppermute | solution.py:296
  10.8 13.9 %collective-permute-start = (bf16[528,512]{1,0:T(8,128)(2,1)S(1)}, bf16[528,512]{1,0:T(8,128)(2,1)S(1)}, u32[]{:S(2)}, u32[]{:S(2)}) collective-permute-start(bf16[528,512]{1,0:T(8,128)(2,1)S(1)} %get-tuple-element.21.refs_3_), channel_id=1, source_target_pairs={{0,15},{1,0},{2,1},{3,2},{4,3},{5,4},{6,5},{7,6},{8,7},{9,8},{10,9... | collective-permute-start | bytes 1622024 | tf_op jit(solution)/shard_map/ppermute | solution.py:274
  14.0 23.4 %collective-permute-start.4 = (bf16[1024,512]{1,0:T(8,128)(2,1)S(1)}, bf16[1024,512]{1,0:T(8,128)(2,1)S(1)}, u32[]{:S(2)}, u32[]{:S(2)}) collective-permute-start(bf16[1024,512]{1,0:T(8,128)(2,1)S(1)} %get-tuple-element.29), channel_id=1, source_target_pairs={{0,15},{1,0},{2,1},{3,2},{4,3},{5,4},{6,5},{7,6},{8,7},{9,8},{10,9... | collective-permute-start | bytes 3145736 | tf_op jit(solution)/shard_map/ppermute | solution.py:274
  16.0 11.4 %collective-permute-start.6 = (bf16[48,512]{1,0:T(8,128)(2,1)S(1)}, bf16[48,512]{1,0:T(8,128)(2,1)S(1)}, u32[]{:S(2)}, u32[]{:S(2)}) collective-permute-start(bf16[48,512]{1,0:T(8,128)(2,1)S(1)} %collective-permute-done.5.direct), channel_id=1, source_target_pairs={{2,31},{18,15}} | collective-permute-start | bytes 147464 | tf_op jit(solution)/shard_map/ppermute | solution.py:296
  18.4 23.1 %collective-permute-start.10 = (bf16[1024,512]{1,0:T(8,128)(2,1)S(1)}, bf16[1024,512]{1,0:T(8,128)(2,1)S(1)}, u32[]{:S(2)}, u32[]{:S(2)}) collective-permute-start(bf16[1024,512]{1,0:T(8,128)(2,1)S(1)} %get-tuple-element.35), channel_id=1, source_target_pairs={{0,15},{1,0},{2,1},{3,2},{4,3},{5,4},{6,5},{7,6},{8,7},{9,8},{10,9... | collective-permute-start | bytes 3145736 | tf_op jit(solution)/shard_map/ppermute | solution.py:274
  19.7 16.4 %collective-permute-start.7 = (bf16[64,512]{1,0:T(8,128)(2,1)S(1)}, bf16[64,512]{1,0:T(8,128)(2,1)S(1)}, u32[]{:S(2)}, u32[]{:S(2)}) collective-permute-start(bf16[64,512]{1,0:T(8,128)(2,1)S(1)} %get-tuple-element.33), channel_id=1, source_target_pairs={{2,1},{6,5},{8,7},{10,9},{12,11},{14,13},{18,17},{22,21},{24,23},{... | collective-permute-start | bytes 196616 | tf_op jit(solution)/shard_map/ppermute | solution.py:296
  27.3 21.5 %collective-permute-start.3 = (bf16[656,512]{1,0:T(8,128)(2,1)S(1)}, bf16[656,512]{1,0:T(8,128)(2,1)S(1)}, u32[]{:S(2)}, u32[]{:S(2)}) collective-permute-start(bf16[656,512]{1,0:T(8,128)(2,1)S(1)} %get-tuple-element.28), channel_id=1, source_target_pairs={{0,15},{1,0},{2,1},{3,2},{4,3},{5,4},{6,5},{7,6},{8,7},{9,8},{10,9... | collective-permute-start | bytes 2015240 | tf_op jit(solution)/shard_map/ppermute | solution.py:274
  27.3 16.0 %collective-permute-start.9 = (bf16[512,512]{1,0:T(8,128)(2,1)S(1)}, bf16[512,512]{1,0:T(8,128)(2,1)S(1)}, u32[]{:S(2)}, u32[]{:S(2)}) collective-permute-start(bf16[512,512]{1,0:T(8,128)(2,1)S(1)} %get-tuple-element.34), channel_id=1, source_target_pairs={{1,0},{3,2},{5,4},{7,6},{9,8},{11,10},{13,12},{15,14},{17,16},{19,... | collective-permute-start | bytes 1572872 | tf_op jit(solution)/shard_map/ppermute | solution.py:274
  36.1 15.4 %collective-permute-start.2 = (bf16[512,256]{1,0:T(8,128)(2,1)S(1)}, bf16[512,256]{1,0:T(8,128)(2,1)S(1)}, u32[]{:S(2)}, u32[]{:S(2)}) collective-permute-start(bf16[512,256]{1,0:T(8,128)(2,1)S(1)} %get-tuple-element.24), channel_id=1, source_target_pairs={{0,15},{2,1},{4,3},{6,5},{8,7},{10,9},{12,11},{14,13},{16,31},{18,... | collective-permute-start | bytes 786440 | tf_op jit(solution)/shard_map/ppermute | solution.py:274
  37.4 5.9 %collective-permute-start.8 = (bf16[64,512]{1,0:T(8,128)(2,1)S(1)}, bf16[64,512]{1,0:T(8,128)(2,1)S(1)}, u32[]{:S(2)}, u32[]{:S(2)}) collective-permute-start(bf16[64,512]{1,0:T(8,128)(2,1)S(1)} %collective-permute-done.7.direct), channel_id=1, source_target_pairs={{2,31},{6,19},{18,15},{22,3}} | collective-permute-start | bytes 196616 | tf_op jit(solution)/shard_map/ppermute | solution.py:296

commit v9 on v8

--- a/solution.py
+++ b/solution.py
@@ -186,16 +186,27 @@
         tile(0).wait()
 
 
-def last_kernel(place, own, chunk, base, band, out, out_v, sem):
+def last_kernel(place, own, chunk, base, band, out, out_v, sems):
     k = jnp.max(place[...])
-    half = chunk.shape[1]
-    out_v[...] = (base[:, half:] + dot(own[1], chunk[...])).astype(out_v.dtype)
+    rows, half = chunk.shape
+    blocks = sems.shape[0]
+
+    def copy(j):
+        block = pl.ds(j * (rows // blocks), rows // blocks)
+        return pltpu.make_async_copy(out_v.at[block], out.at[0, k, block, pl.ds(half, half)], sems.at[j])
+
+    for j in range(blocks):
+        block = pl.ds(j * (rows // blocks), rows // blocks)
+        out_v[block] = (base[block, half:] + dot(own[1, block], chunk[...])).astype(out_v.dtype)
+
+        @pl.when(k >= 0)
+        def _():
+            copy(j).start()
 
     @pl.when(k >= 0)
     def _():
-        copy = pltpu.make_async_copy(out_v, out.at[0, k, :, pl.ds(half, half)], sem)
-        copy.start()
-        copy.wait()
+        for j in range(blocks):
+            copy(j).wait()
 
 
 def pack_kernel(pieces, noted, *refs):
@@ -336,7 +347,7 @@
         [pltpu.VMEM((fold, lanes), own.dtype), side, tile(2), sems(3)], own=own,
     )
     (band,) = call(
-        last_kernel, 1, (place, local, far, base, band), [VMEM] * 4 + [ANY], [side, sems()], own=own,
+        last_kernel, 1, (place, local, far, base, band), [VMEM] * 4 + [ANY], [side, sems(4)], own=own,
     )
     return band
 

time: 52.3 us -> 52.3 us (level)
  waiting for transfers between devices: 8.19 us -> 9.22 us
  Pallas kernels: 22.9 us -> 21.9 us
    ppermute x7, waiting for transfers between devices: 8.18 us -> 9.21 us  [per_device(): send = lambda value, some=pairs: lax.ppermute(value, 'wide', some)]
    pallas_call x7, Pallas kernels: 14.5 us -> 13.5 us  [call(): pl.pallas_call(kernel, out_shape=[band, *extra], in_specs=spaces, out_spe...]
  transfers between devices with their start and end apart: 11 -> 11, of which waited for: 3 -> 3; matrix products, arithmetic and copies ran while one was open for 1% -> 1% of each run, Pallas kernels for 44% -> 42%
where the time goes in v9:
time: 52.3 us; the launch traced here: 51.9 us
  Pallas kernels  21.9 us (42%)
  starting transfers between devices  17.5 us (33%)
  waiting for transfers between devices  9.22 us (18%)
  local copies, waits for them, and re-layouts  2.38 us (5%)
  between operations  0.86 us (2%)
    pallas_call x7, Pallas kernels, call(): pl.pallas_call(kernel, out_shape=[band, *extra], in_specs=spaces, out_spe...  13.5 us
    ppermute x7, starting transfers between devices, per_device(): send = lambda value, some=pairs: lax.ppermute(value, 'wide', some)  11.5 us
    ppermute x7, waiting for transfers between devices, per_device(): send = lambda value, some=pairs: lax.ppermute(value, 'wide', some)  9.21 us
    pallas_call x4, Pallas kernels, pack(): pl.pallas_call(functools.partial(pack_kernel, pieces, noted), out_shape=[...  8.42 us
    ppermute x4, starting transfers between devices, per_device(): both = lambda value, some: lax.ppermute(value, ('groups', 'wide'), some)  6.02 us
    squeeze x1, local copies, waits for them, and re-layouts, per_device(): first = own[0]  1.08 us
  transfers between devices with their start and end apart: 11, of which 3 were waited for; matrix products, arithmetic and copies ran while one was open for 1% of the time, Pallas kernels for 42%

profile of v9, /device:TPU:0, one launch (start us, length us, event | category | flops | bytes accessed | tf_op | source)
XLA Modules:
  0.0 51.9 jit_solution(6987383677603014356)
XLA Ops:
  0.0 1.1 %slice_bitcast_fusion.refs_3_ = bf16[512,512]{1,0:T(8,128)(2,1)S(1)} fusion(bf16[8,512,512]{2,1,0:T(8,128)(2,1)} %refs_2_.7), kind=kLoop, calls=%fused_computation | loop fusion | bytes 1048576 | tf_op jit(solution)/shard_map/squeeze | solution.py:293
  1.1 5.5 %collective-permute-start.1 = (bf16[512,512]{1,0:T(8,128)(2,1)S(1)}, bf16[512,512]{1,0:T(8,128)(2,1)S(1)}, u32[]{:S(2)}, u32[]{:S(2)}) collective-permute-start(bf16[512,512]{1,0:T(8,128)(2,1)S(1)} %slice_bitcast_fusion.refs_3_), channel_id=1, source_target_pairs={{0,15},{1,0},{2,1},{3,2},{4,3},{5,4},{6,5},{7,6},{8,7},{9,8},{10,9... | collective-permute-start | bytes 1572872 | tf_op jit(solution)/shard_map/ppermute | solution.py:285
  7.2 0.0 copy-start
  7.2 0.6 %copy-done = s32[1,8]{1,0:T(1,128)S(1)} copy-done((s32[1,8]{1,0:T(1,128)S(1)}, s32[1,8]{1,0:T(1,128)}, u32[]{:S(2)}) %copy-start) | copy-done | bytes 56
  7.9 1.6 %shard_map.37 = (bf16[528,512]{1,0:T(8,128)(2,1)S(1)}, bf16[48,512]{1,0:T(8,128)(2,1)S(1)}) custom-call(s32[1,8]{1,0:T(1,128)S(1)} %copy-done, s32[1]{0:T(128)S(6)} %copy.16.refs_1_.counts, bf16[8,512,512]{2,1,0:T(8,128)(2,1)} %refs_2_.7, bf16[512,512]{1,0:T(8,128)(2,1)S(1)} %slice_bitcast_fusion.refs_3_), custom_call_target="tpu_custom_call" | custom-call | bytes 2359296 | tf_op jit(solution)/shard_map/pallas_call | solution.py:250
  9.5 1.3 %collective-permute-start.5 = (bf16[48,512]{1,0:T(8,128)(2,1)S(1)}, bf16[48,512]{1,0:T(8,128)(2,1)S(1)}, u32[]{:S(2)}, u32[]{:S(2)}) collective-permute-start(bf16[48,512]{1,0:T(8,128)(2,1)S(1)} %get-tuple-element.30), channel_id=1, source_target_pairs={{2,1},{4,3},{6,5},{8,7},{10,9},{12,11},{14,13},{18,17},{20,19},{22... | collective-permute-start | bytes 147464 | tf_op jit(solution)/shard_map/ppermute | solution.py:307
  10.8 0.1 collective-permute-start
  10.9 3.1 %shard_map.38 = (bf16[1024,512]{1,0:T(8,128)(2,1)S(1)}, bf16[4096,512]{1,0:T(8,128)(2,1)S(1)}) custom-call(s32[1,8]{1,0:T(1,128)S(1)} %copy-done, s32[1]{0:T(128)S(6)} %copy.16.refs_1_.counts, bf16[8,512,512]{2,1,0:T(8,128)(2,1)} %refs_2_.7, bf16[528,512]{1,0:T(8,128)(2,1)S(1)} %get-tuple-element.21.refs_3_), custom_call_target="tpu_custom_call" | custom-call | bytes 20971520 | tf_op jit(solution)/shard_map/pallas_call | solution.py:250
  14.0 1.9 %collective-permute-start.4 = (bf16[1024,512]{1,0:T(8,128)(2,1)S(1)}, bf16[1024,512]{1,0:T(8,128)(2,1)S(1)}, u32[]{:S(2)}, u32[]{:S(2)}) collective-permute-start(bf16[1024,512]{1,0:T(8,128)(2,1)S(1)} %get-tuple-element.29), channel_id=1, source_target_pairs={{0,15},{1,0},{2,1},{3,2},{4,3},{5,4},{6,5},{7,6},{8,7},{9,8},{10,9... | collective-permute-start | bytes 3145736 | tf_op jit(solution)/shard_map/ppermute | solution.py:285
  16.0 0.0 collective-permute-done.5.direct
  16.0 0.7 %collective-permute-start.6 = (bf16[48,512]{1,0:T(8,128)(2,1)S(1)}, bf16[48,512]{1,0:T(8,128)(2,1)S(1)}, u32[]{:S(2)}, u32[]{:S(2)}) collective-permute-start(bf16[48,512]{1,0:T(8,128)(2,1)S(1)} %collective-permute-done.5.direct), channel_id=1, source_target_pairs={{2,31},{18,15}} | collective-permute-start | bytes 147464 | tf_op jit(solution)/shard_map/ppermute | solution.py:307
  16.6 0.0 collective-permute-done.1.head.refs_3_
  16.6 1.8 %shard_map.44 = (bf16[1024,512]{1,0:T(8,128)(2,1)S(1)}, bf16[64,512]{1,0:T(8,128)(2,1)S(1)}) custom-call(s32[1,8]{1,0:T(1,128)S(1)} %copy-done, s32[1]{0:T(128)S(6)} %copy.16.refs_1_.counts, bf16[8,512,512]{2,1,0:T(8,128)(2,1)} %refs_2_.7, bf16[512,512]{1,0:T(8,128)(2,1)S(1)} %collective-permute-done.1.head.refs_3_), custom_call_target="tpu_custom_call" | custom-call | bytes 4456448 | tf_op jit(solution)/shard_map/pallas_call | solution.py:250
  18.4 1.3 %collective-permute-start.10 = (bf16[1024,512]{1,0:T(8,128)(2,1)S(1)}, bf16[1024,512]{1,0:T(8,128)(2,1)S(1)}, u32[]{:S(2)}, u32[]{:S(2)}) collective-permute-start(bf16[1024,512]{1,0:T(8,128)(2,1)S(1)} %get-tuple-element.35), channel_id=1, source_target_pairs={{0,15},{1,0},{2,1},{3,2},{4,3},{5,4},{6,5},{7,6},{8,7},{9,8},{10,9... | collective-permute-start | bytes 3145736 | tf_op jit(solution)/shard_map/ppermute | solution.py:285
  19.7 3.4 %collective-permute-start.7 = (bf16[64,512]{1,0:T(8,128)(2,1)S(1)}, bf16[64,512]{1,0:T(8,128)(2,1)S(1)}, u32[]{:S(2)}, u32[]{:S(2)}) collective-permute-start(bf16[64,512]{1,0:T(8,128)(2,1)S(1)} %get-tuple-element.33), channel_id=1, source_target_pairs={{2,1},{6,5},{8,7},{10,9},{12,11},{14,13},{18,17},{22,21},{24,23},{... | collective-permute-start | bytes 196616 | tf_op jit(solution)/shard_map/ppermute | solution.py:307
  23.1 1.5 %shard_map.39.band = bf16[1,10,512,512]{3,2,1,0:T(8,128)(2,1)} custom-call(bf16[8,512,512]{2,1,0:T(8,128)(2,1)S(1)} %bitcast.5, bf16[512,512]{1,0:T(8,128)(2,1)S(1)} %collective-permute-done.1.head.refs_3_), custom_call_target="tpu_custom_call" | custom-call | flops 6442450944 | bytes 6291456 | tf_op jit(solution)/shard_map/pallas_call | solution.py:266
  24.7 0.0 collective-permute-done.refs_3_.chunk
  24.7 0.7 %slice.19 = s32[1,1]{1,0:T(1,128)} slice(s32[1,9]{1,0:T(1,128)S(1)} %slice_convert_fusion), slice={[0:1], [8:9]} | slice | bytes 8 | tf_op jit(solution)/shard_map/slice | solution.py:322
  25.3 1.9 %shard_map.41 = (bf16[656,512]{1,0:T(8,128)(2,1)S(1)}, bf16[512,256]{1,0:T(8,128)(2,1)S(1)}, bf16[512,512]{1,0:T(8,128)(2,1)S(1)}) custom-call(s32[1,8]{1,0:T(1,128)S(1)} %copy-done, s32[1]{0:T(128)S(6)} %copy.16.refs_1_.counts, bf16[8,512,512]{2,1,0:T(8,128)(2,1)} %refs_2_.7, bf16[528,512]{1,0:T(8,128)(2,1)S(1)} %collective-permute-done.refs_3_.chunk), custom_call_target="tpu_custom_call" | custom-call | bytes 5832704 | tf_op jit(solution)/shard_map/pallas_call | solution.py:250
  27.3 0.1 collective-permute-start.3
  27.3 0.0 collective-permute-done.6.detour
  27.3 1.3 %collective-permute-start.9 = (bf16[512,512]{1,0:T(8,128)(2,1)S(1)}, bf16[512,512]{1,0:T(8,128)(2,1)S(1)}, u32[]{:S(2)}, u32[]{:S(2)}) collective-permute-start(bf16[512,512]{1,0:T(8,128)(2,1)S(1)} %get-tuple-element.34), channel_id=1, source_target_pairs={{1,0},{3,2},{5,4},{7,6},{9,8},{11,10},{13,12},{15,14},{17,16},{19,... | collective-permute-start | bytes 1572872 | tf_op jit(solution)/shard_map/ppermute | solution.py:285
  28.6 5.1 %shard_map.40 = (bf16[1,10,512,512]{3,2,1,0:T(8,128)(2,1)}, s32[2,9]{1,0:T(2,128)S(1)}, s32[8,128]{1,0:T(8,128)S(1)}) custom-call(s32[1,8]{1,0:T(1,128)S(1)} %copy-done, s32[1]{0:T(128)S(6)} %copy.16.refs_1_.counts, s32[1,8]{1,0:T(1,128)S(1)} %bitcast.12, s32[1]{0:T(128)} %bitcast.1.next_counts, ...), custom_call_target="tpu_custom_call", output_to_operand_aliasing={{0}: (5, {})} | custom-call | flops 16106127360 | bytes 15728640 | tf_op jit(solution)/shard_map/pallas_call | solution.py:266
  33.7 2.5 %shard_map.42 = (bf16[1,10,512,512]{3,2,1,0:T(8,128)(2,1)}, f32[512,512]{1,0:T(8,128)S(1)}) custom-call(s32[2,9]{1,0:T(2,128)S(1)} %get-tuple-element.25.table, bf16[8,512,512]{2,1,0:T(8,128)(2,1)S(1)} %bitcast.7, bf16[528,512]{1,0:T(8,128)(2,1)S(1)} %collective-permute-done.refs_3_.chunk, ...), custom_call_target="tpu_custom_call", output_to_operand_aliasing={{0}: (3, {})} | custom-call | flops 536870912 | bytes 524288 | tf_op jit(solution)/shard_map/pallas_call | solution.py:266
  36.3 0.0 collective-permute-done.7.direct
  36.3 1.3 %collective-permute-start.2 = (bf16[512,256]{1,0:T(8,128)(2,1)S(1)}, bf16[512,256]{1,0:T(8,128)(2,1)S(1)}, u32[]{:S(2)}, u32[]{:S(2)}) collective-permute-start(bf16[512,256]{1,0:T(8,128)(2,1)S(1)} %get-tuple-element.24), channel_id=1, source_target_pairs={{0,15},{2,1},{4,3},{6,5},{8,7},{10,9},{12,11},{14,13},{16,31},{18,... | collective-permute-start | bytes 786440 | tf_op jit(solution)/shard_map/ppermute | solution.py:285
  37.6 0.0 collective-permute-done.4.chunk
  37.6 0.7 %collective-permute-start.8 = (bf16[64,512]{1,0:T(8,128)(2,1)S(1)}, bf16[64,512]{1,0:T(8,128)(2,1)S(1)}, u32[]{:S(2)}, u32[]{:S(2)}) collective-permute-start(bf16[64,512]{1,0:T(8,128)(2,1)S(1)} %collective-permute-done.7.direct), channel_id=1, source_target_pairs={{2,31},{6,19},{18,15},{22,3}} | collective-permute-start | bytes 196616 | tf_op jit(solution)/shard_map/ppermute | solution.py:307
  38.3 2.8 %shard_map.43 = (bf16[1,10,512,512]{3,2,1,0:T(8,128)(2,1)}, bf16[48,512]{1,0:T(8,128)(2,1)S(1)}) custom-call(s32[2,9]{1,0:T(2,128)S(1)} %get-tuple-element.25.table, bf16[8,512,512]{2,1,0:T(8,128)(2,1)S(1)} %bitcast.8, bf16[1024,512]{1,0:T(8,128)(2,1)S(1)} %collective-permute-done.4.chunk, ...), custom_call_target="tpu_custom_call", output_to_operand_aliasing={{0}: (5, {})} | custom-call | flops 1073741824 | bytes 1048576 | tf_op jit(solution)/shard_map/pallas_call | solution.py:266
  41.1 0.4 collective-permute-done.10.chunk
  41.5 0.6 %shard_map.45.band = bf16[1,10,512,512]{3,2,1,0:T(8,128)(2,1)} custom-call(s32[2,9]{1,0:T(2,128)S(1)} %get-tuple-element.25.table, bf16[8,512,512]{2,1,0:T(8,128)(2,1)S(1)} %bitcast.9, bf16[1024,512]{1,0:T(8,128)(2,1)S(1)} %collective-permute-done.10.chunk, bf16[1,10,512,512]{3,2,1,0:T(8,128)(2,1)} %get-tuple-element.36.band), custom_call_target="tpu_custom_call", output_to_operand_aliasing={{}: (3, {})} | custom-call | flops 1073741824 | bytes 1048576 | tf_op jit(solution)/shard_map/pallas_call | solution.py:266
  42.2 0.0 collective-permute-done.8.detour
  42.2 0.0 collective-permute-done.9.near
  42.2 6.6 %collective-permute-done.3.chunk = bf16[656,512]{1,0:T(8,128)(2,1)S(1)} collective-permute-done((bf16[656,512]{1,0:T(8,128)(2,1)S(1)}, bf16[656,512]{1,0:T(8,128)(2,1)S(1)}, u32[]{:S(2)}, u32[]{:S(2)}) %collective-permute-start.3) | collective-permute-done | bytes 671776 | tf_op jit(solution)/shard_map/ppermute | solution.py:285
  48.7 0.6 %shard_map.46.band = bf16[1,10,512,512]{3,2,1,0:T(8,128)(2,1)} custom-call(s32[2,9]{1,0:T(2,128)S(1)} %get-tuple-element.25.table, bf16[8,512,512]{2,1,0:T(8,128)(2,1)S(1)} %bitcast.10, bf16[656,512]{1,0:T(8,128)(2,1)S(1)} %collective-permute-done.3.chunk, bf16[48,512]{1,0:T(8,128)(2,1)S(1)} %get-tuple-element.32.rest, ...), custom_call_target="tpu_custom_call", output_to_operand_aliasing={{}: (8, {})} | custom-call | flops 1073741824 | bytes 1048576 | tf_op jit(solution)/shard_map/pallas_call | solution.py:266
  49.3 2.2 %collective-permute-done.2.chunk = bf16[512,256]{1,0:T(8,128)(2,1)S(1)} collective-permute-done((bf16[512,256]{1,0:T(8,128)(2,1)S(1)}, bf16[512,256]{1,0:T(8,128)(2,1)S(1)}, u32[]{:S(2)}, u32[]{:S(2)}) %collective-permute-start.2) | collective-permute-done | bytes 262176 | tf_op jit(solution)/shard_map/ppermute | solution.py:285
  51.5 0.4 shard_map.47
  (1 shorter events, 0.0 us)
Async XLA Ops:
  1.1 15.5 %collective-permute-start.1 = (bf16[512,512]{1,0:T(8,128)(2,1)S(1)}, bf16[512,512]{1,0:T(8,128)(2,1)S(1)}, u32[]{:S(2)}, u32[]{:S(2)}) collective-permute-start(bf16[512,512]{1,0:T(8,128)(2,1)S(1)} %slice_bitcast_fusion.refs_3_), channel_id=1, source_target_pairs={{0,15},{1,0},{2,1},{3,2},{4,3},{5,4},{6,5},{7,6},{8,7},{9,8},{10,9... | collective-permute-start | bytes 1572872 | tf_op jit(solution)/shard_map/ppermute | solution.py:285
  7.2 0.7 %copy-start = (s32[1,8]{1,0:T(1,128)S(1)}, s32[1,8]{1,0:T(1,128)}, u32[]{:S(2)}) copy-start(s32[1,8]{1,0:T(1,128)} %refs_0_.7) | copy-start | bytes 100
  9.5 6.5 %collective-permute-start.5 = (bf16[48,512]{1,0:T(8,128)(2,1)S(1)}, bf16[48,512]{1,0:T(8,128)(2,1)S(1)}, u32[]{:S(2)}, u32[]{:S(2)}) collective-permute-start(bf16[48,512]{1,0:T(8,128)(2,1)S(1)} %get-tuple-element.30), channel_id=1, source_target_pairs={{2,1},{4,3},{6,5},{8,7},{10,9},{12,11},{14,13},{18,17},{20,19},{22... | collective-permute-start | bytes 147464 | tf_op jit(solution)/shard_map/ppermute | solution.py:307
  10.8 13.9 %collective-permute-start = (bf16[528,512]{1,0:T(8,128)(2,1)S(1)}, bf16[528,512]{1,0:T(8,128)(2,1)S(1)}, u32[]{:S(2)}, u32[]{:S(2)}) collective-permute-start(bf16[528,512]{1,0:T(8,128)(2,1)S(1)} %get-tuple-element.21.refs_3_), channel_id=1, source_target_pairs={{0,15},{1,0},{2,1},{3,2},{4,3},{5,4},{6,5},{7,6},{8,7},{9,8},{10,9... | collective-permute-start | bytes 1622024 | tf_op jit(solution)/shard_map/ppermute | solution.py:285
  14.0 23.5 %collective-permute-start.4 = (bf16[1024,512]{1,0:T(8,128)(2,1)S(1)}, bf16[1024,512]{1,0:T(8,128)(2,1)S(1)}, u32[]{:S(2)}, u32[]{:S(2)}) collective-permute-start(bf16[1024,512]{1,0:T(8,128)(2,1)S(1)} %get-tuple-element.29), channel_id=1, source_target_pairs={{0,15},{1,0},{2,1},{3,2},{4,3},{5,4},{6,5},{7,6},{8,7},{9,8},{10,9... | collective-permute-start | bytes 3145736 | tf_op jit(solution)/shard_map/ppermute | solution.py:285
  16.0 11.4 %collective-permute-start.6 = (bf16[48,512]{1,0:T(8,128)(2,1)S(1)}, bf16[48,512]{1,0:T(8,128)(2,1)S(1)}, u32[]{:S(2)}, u32[]{:S(2)}) collective-permute-start(bf16[48,512]{1,0:T(8,128)(2,1)S(1)} %collective-permute-done.5.direct), channel_id=1, source_target_pairs={{2,31},{18,15}} | collective-permute-start | bytes 147464 | tf_op jit(solution)/shard_map/ppermute | solution.py:307
  18.4 23.1 %collective-permute-start.10 = (bf16[1024,512]{1,0:T(8,128)(2,1)S(1)}, bf16[1024,512]{1,0:T(8,128)(2,1)S(1)}, u32[]{:S(2)}, u32[]{:S(2)}) collective-permute-start(bf16[1024,512]{1,0:T(8,128)(2,1)S(1)} %get-tuple-element.35), channel_id=1, source_target_pairs={{0,15},{1,0},{2,1},{3,2},{4,3},{5,4},{6,5},{7,6},{8,7},{9,8},{10,9... | collective-permute-start | bytes 3145736 | tf_op jit(solution)/shard_map/ppermute | solution.py:285
  19.7 16.5 %collective-permute-start.7 = (bf16[64,512]{1,0:T(8,128)(2,1)S(1)}, bf16[64,512]{1,0:T(8,128)(2,1)S(1)}, u32[]{:S(2)}, u32[]{:S(2)}) collective-permute-start(bf16[64,512]{1,0:T(8,128)(2,1)S(1)} %get-tuple-element.33), channel_id=1, source_target_pairs={{2,1},{6,5},{8,7},{10,9},{12,11},{14,13},{18,17},{22,21},{24,23},{... | collective-permute-start | bytes 196616 | tf_op jit(solution)/shard_map/ppermute | solution.py:307
  27.3 21.5 %collective-permute-start.3 = (bf16[656,512]{1,0:T(8,128)(2,1)S(1)}, bf16[656,512]{1,0:T(8,128)(2,1)S(1)}, u32[]{:S(2)}, u32[]{:S(2)}) collective-permute-start(bf16[656,512]{1,0:T(8,128)(2,1)S(1)} %get-tuple-element.28), channel_id=1, source_target_pairs={{0,15},{1,0},{2,1},{3,2},{4,3},{5,4},{6,5},{7,6},{8,7},{9,8},{10,9... | collective-permute-start | bytes 2015240 | tf_op jit(solution)/shard_map/ppermute | solution.py:285
  27.3 14.8 %collective-permute-start.9 = (bf16[512,512]{1,0:T(8,128)(2,1)S(1)}, bf16[512,512]{1,0:T(8,128)(2,1)S(1)}, u32[]{:S(2)}, u32[]{:S(2)}) collective-permute-start(bf16[512,512]{1,0:T(8,128)(2,1)S(1)} %get-tuple-element.34), channel_id=1, source_target_pairs={{1,0},{3,2},{5,4},{7,6},{9,8},{11,10},{13,12},{15,14},{17,16},{19,... | collective-permute-start | bytes 1572872 | tf_op jit(solution)/shard_map/ppermute | solution.py:285
  36.3 15.3 %collective-permute-start.2 = (bf16[512,256]{1,0:T(8,128)(2,1)S(1)}, bf16[512,256]{1,0:T(8,128)(2,1)S(1)}, u32[]{:S(2)}, u32[]{:S(2)}) collective-permute-start(bf16[512,256]{1,0:T(8,128)(2,1)S(1)} %get-tuple-element.24), channel_id=1, source_target_pairs={{0,15},{2,1},{4,3},{6,5},{8,7},{10,9},{12,11},{14,13},{16,31},{18,... | collective-permute-start | bytes 786440 | tf_op jit(solution)/shard_map/ppermute | solution.py:285
  37.6 4.6 %collective-permute-start.8 = (bf16[64,512]{1,0:T(8,128)(2,1)S(1)}, bf16[64,512]{1,0:T(8,128)(2,1)S(1)}, u32[]{:S(2)}, u32[]{:S(2)}) collective-permute-start(bf16[64,512]{1,0:T(8,128)(2,1)S(1)} %collective-permute-done.7.direct), channel_id=1, source_target_pairs={{2,31},{6,19},{18,15},{22,3}} | collective-permute-start | bytes 196616 | tf_op jit(solution)/shard_map/ppermute | solution.py:307
